TPU v7x, 32 devices: a whole 2x2x4 slice. The times are simulated.
32 devices in a mesh: grp: 2 (over y), ia: 8 (over z, x), ja: 2 (over core).
Axes of the slice: x: 2, y: 2, z: 4, core: 2. Of those that a mesh axis runs over, the one named last changes fastest.
Arguments:
- adjoint_temp: float32 [50, 32, 1024], P('grp', 'ja', 'ia'), parts along dimension 0
- adjoint_surface: float32 [64, 1024], P(('grp', 'ja'), 'ia'), parts along dimension 0, may hold values from -6 to 6
- trajectory_u: float32 [2, 25, 32, 1024], P(None, None, 'ja', 'ia'), may hold values from -6 to 6
- trajectory_v: float32 [2, 25, 32, 1024], P(None, None, 'ja', 'ia'), may hold values from -6 to 6
- levels: int32 [32, 1024], P('ja', 'ia'), may hold values from 0 to 25, as said below
- partner: int32 [1024], P('ia'), may hold values from 0 to 1023, as said below
- thickness: float32 [25], replicated, may hold values from 0.2 to 1
- coupling: float32 [25], replicated, may hold values from 0.2 to 1
Outputs:
- temp_gradient: float32 [50, 32, 1024], P('grp', 'ja', 'ia'), parts along dimension 0
- surface_gradient: float32 [64, 1024], P(('grp', 'ja'), 'ia'), parts along dimension 0
There are 2 independent parts, one for each index of `grp`. A program takes and returns all parts, laid end to end along the dimension named above; an argument that names none is the same for every part. Nothing has to cross between parts.
Inputs may be any that keep to these rules, and one draw needn't show every extreme that they name: `levels`: 0 marks a land column. partner[partner[i]] = i and partner[i] != i for every column i.
All inputs are finite; a program needn't handle non-finite values.
Results may differ from a plain program's by a relative error of at most 0.0001.
Values sent between devices are 32-bit elements; how exact they have to be, the bound alone decides.
No kernel may reach another device: no remote copies, remote signals or barrier semaphores. Data moves between devices by JAX's collectives and lax.ppermute only.
A program may use at most 64 MiB of HBM per device.

v0:
```python
import jax
import jax.numpy as jnp
from jax import lax
from jax.sharding import PartitionSpec as P

SOLVER_ITERS = 2


time_step = 0.5
surface_coef = 2.0


def with_halo(x, sides, width):
    for axis, dim in sides:
        count, length = (lax.axis_size(axis), x.shape[dim])
        up = [(i, (i + 1) % count) for i in range(count)]
        down = [(j, i) for i, j in up]
        last = lax.slice_in_dim(x, length - width, length, axis=dim)
        leading = lax.slice_in_dim(x, 0, width, axis=dim)
        before = lax.ppermute(last, axis, up)
        after = lax.ppermute(leading, axis, down)
        x = jnp.concatenate([before, x, after], axis=dim)
    return x


def surface_apply(field, partner, last_row, first_row):
    padded = with_halo(field, (("ia", 1), ("ja", 0)), 1)
    top_whole = lax.all_gather(field[-1], "ia", axis=0, tiled=True)
    across = jnp.take(top_whole, partner)
    east_cells = padded[1:-1, 2:]
    west_cells = padded[1:-1, :-2]
    north_cells = jnp.where(last_row, across[None, :], padded[2:, 1:-1])
    south_cells = jnp.where(first_row, 0.0, padded[:-2, 1:-1])
    return (1.0 + 4.0 * surface_coef) * field - surface_coef * (
        east_cells + west_cells + north_cells + south_cells
    )


def squares(residual):
    return lax.psum(jnp.sum(residual * residual), ("ia", "ja"))


def surface_solve(forcing, partner, last_row, first_row):
    iterate = jnp.zeros_like(forcing)
    residual = forcing
    direction = forcing
    norm_now = squares(residual)
    for sweep in range(SOLVER_ITERS):
        applied = surface_apply(direction, partner, last_row, first_row)
        step_size = norm_now / lax.psum(jnp.sum(direction * applied), ("ia", "ja"))
        iterate = iterate + step_size * direction
        if sweep + 1 < SOLVER_ITERS:
            residual = residual - step_size * applied
            norm_next = squares(residual)
            direction = residual + norm_next / norm_now * direction
            norm_now = norm_next
    return iterate


def on_device(
    adjoint_temp, adjoint_surface, trajectory_u, trajectory_v, levels, partner, thickness, coupling
):
    step_count, level_count, row_count, col_count = trajectory_u.shape
    is_top = lax.axis_index("ja") == lax.axis_size("ja") - 1
    is_bottom = lax.axis_index("ja") == 0
    ocean = (jnp.arange(level_count, dtype=jnp.int32)[:, None, None] < levels[None]).astype(
        jnp.float32
    )
    layer_count = step_count * level_count
    stacked = jnp.concatenate(
        [
            trajectory_u.reshape(layer_count, row_count, col_count),
            trajectory_v.reshape(layer_count, row_count, col_count),
            ocean,
        ],
        axis=0,
    )
    padded = with_halo(stacked, (("ia", 2), ("ja", 1)), 1)
    speed_u = padded[:layer_count].reshape(step_count, level_count, row_count + 2, col_count + 2)
    speed_v = padded[layer_count : 2 * layer_count].reshape(
        step_count, level_count, row_count + 2, col_count + 2
    )
    ocean_pad = padded[2 * layer_count :]
    ocean_rows = ocean_pad[:, 1:-1, :]
    eastward = (
        0.5 * speed_u[:, :, 1:-1, :-1] * ocean_rows[None, :, :, :-1] * ocean_rows[None, :, :, 1:]
    )
    ocean_cols = ocean_pad[:, :, 1:-1]
    upper_top = jnp.concatenate([ocean_cols[:, 1:-1], ocean_cols[:, -2:-1]], axis=1)
    upper = jnp.where(is_top, upper_top, ocean_cols[:, 1:])
    northward = 0.5 * speed_v[:, :, :-1, 1:-1] * ocean_cols[None, :, :-1] * upper[None]
    first_face = (jnp.arange(row_count + 1)[:, None] == 0) & is_bottom
    northward = jnp.where(first_face, 0.0, northward)
    last_row = (jnp.arange(row_count)[:, None] == row_count - 1) & is_top
    first_row = (jnp.arange(row_count)[:, None] == 0) & is_bottom
    temp_gradient = adjoint_temp
    surface_gradient = adjoint_surface
    for step_index in range(step_count - 1, -1, -1):
        forcing = surface_gradient + jnp.sum(
            coupling[:, None, None] * ocean * temp_gradient, axis=0
        )
        solved = surface_solve(forcing, partner, last_row, first_row)
        adjoint_mid = temp_gradient + thickness[:, None, None] * ocean * solved[None]
        scaled = time_step * ocean * adjoint_mid
        face_north = northward[step_index]
        fold_values = face_north[:, -1, :] * scaled[:, -1, :]
        row_whole = lax.all_gather(fold_values, "ia", axis=1, tiled=True)
        fold_terms = jnp.take(row_whole, partner, axis=1)
        extended = with_halo(scaled, (("ia", 2), ("ja", 1)), 1)
        east_cells = extended[:, 1:-1, 2:]
        west_cells = extended[:, 1:-1, :-2]
        north_cells = jnp.where(last_row, 0.0, extended[:, 2:, 1:-1])
        south_cells = extended[:, :-2, 1:-1]
        face_east = eastward[step_index]
        result = (
            adjoint_mid
            + face_east[:, :, 1:] * (east_cells - scaled)
            + face_east[:, :, :-1] * (scaled - west_cells)
        )
        result = (
            result
            + face_north[:, 1:] * (north_cells - scaled)
            + face_north[:, :-1] * (scaled - south_cells)
        )
        temp_gradient = result - jnp.where(last_row, fold_terms[:, None, :], 0.0)
        surface_gradient = solved
    return (temp_gradient, surface_gradient)


def solution(mesh):
    return jax.shard_map(
        on_device,
        mesh=mesh,
        in_specs=(
            P("grp", "ja", "ia"),
            P(("grp", "ja"), "ia"),
            P(None, None, "ja", "ia"),
            P(None, None, "ja", "ia"),
            P("ja", "ia"),
            P("ia"),
            P(),
            P(),
        ),
        out_specs=(P("grp", "ja", "ia"), P(("grp", "ja"), "ia")),
        check_vma=False,
    )
```

profile of v0, /device:TPU:0, one launch (start us, length us, event | category | flops | bytes accessed | tf_op | source)
XLA Modules:
  0.0 428.5 jit_solution(16102219851847045073)
XLA Ops:
  2.7 6.0 %collective-permute-start = (f32[16,1]{1,0:T(8,128)S(1)}, f32[16,1]{1,0:T(8,128)S(1)}, u32[]{:S(2)}, u32[]{:S(2)}) collective-permute-start(f32[16,1]{1,0:T(8,128)S(1)} %get-tuple-element.67), channel_id=1, source_target_pairs={{2,0},{4,2},{6,4},{8,6},{10,8},{12,10},{14,12},{0,14},{3,1},{5,3},... | collective-permute-start | bytes 200 | tf_op jit(solution)/shard_map/ppermute | solution.py:21
  10.9 20.9 %all-gather = f32[1,1024]{1,0:T(1,128)S(1)} all-gather(f32[1,128]{1,0:T(1,128)S(1)} %slice.385), channel_id=2, replica_groups=mesh['grp'=2,'ia'=8,'ja'=2] {'ia'}, dimensions={1}, use_global_device_ids=true | all-gather | bytes 4608 | tf_op jit(solution)/shard_map/all_gather | solution.py:28
  35.0 30.4 %all-reduce.1 = (f32[]{:T(128)}, f32[]{:T(128)}) all-reduce(f32[]{:T(128)} %get-tuple-element.19, f32[]{:T(128)} %get-tuple-element.18), channel_id=1, replica_groups=mesh['grp'=2,'ia'=8,'ja'=2] {'ia','ja'}, use_global_device_ids=true, to_apply=%region_2.3 | all-reduce | flops 2 | bytes 16 | tf_op jit(solution)/shard_map/psum | solution.py:40
  67.4 33.7 %psum.58 = f32[]{:T(128)} all-reduce(f32[]{:T(128)} %multiply_reduce_fusion.3), channel_id=1, replica_groups=mesh['grp'=2,'ia'=8,'ja'=2] {'ia','ja'}, use_global_device_ids=true, to_apply=%region_6.8 | all-reduce | flops 1 | bytes 8 | tf_op jit(solution)/shard_map/psum | solution.py:40
  102.5 16.1 %all-gather.1 = f32[1,1024]{1,0:T(1,128)S(1)} all-gather(f32[1,128]{1,0:T(1,128)S(1)} %slice.388), channel_id=3, replica_groups=mesh['grp'=2,'ia'=8,'ja'=2] {'ia'}, dimensions={1}, use_global_device_ids=true | all-gather | bytes 4608 | tf_op jit(solution)/shard_map/all_gather | solution.py:28
  119.7 2.1 collective-permute-start.4
  123.4 4.7 %collective-permute-done.5 = f32[16,1]{1,0:T(8,128)S(1)} collective-permute-done((f32[16,1]{1,0:T(8,128)S(1)}, f32[16,1]{1,0:T(8,128)S(1)}, u32[]{:S(2)}, u32[]{:S(2)}) %collective-permute-start.5) | collective-permute-done | bytes 96 | tf_op jit(solution)/shard_map/ppermute | solution.py:20
  130.2 30.4 %psum.59 = f32[]{:T(128)} all-reduce(f32[]{:T(128)} %fusion.61), channel_id=1, replica_groups=mesh['grp'=2,'ia'=8,'ja'=2] {'ia','ja'}, use_global_device_ids=true, to_apply=%region_8.10 | all-reduce | flops 1 | bytes 8 | tf_op jit(solution)/shard_map/psum | solution.py:50
  167.5 2.9 collective-permute-done.13
  171.7 2.6 fusion.6
  176.9 3.6 reshape.140
  184.5 3.6 reshape.141
  193.3 33.3 %all-gather.2 = f32[25,1,1024]{0,2,1:T(8,128)} all-gather(f32[25,1,128]{0,2,1:T(8,128)S(1)} %slice_multiply_fusion.1), channel_id=4, replica_groups=mesh['grp'=2,'ia'=8,'ja'=2] {'ia'}, dimensions={2}, use_global_device_ids=true | all-gather | bytes 115200 | tf_op jit(solution)/shard_map/all_gather | solution.py:107
  228.4 4.4 %fusion.10 = (f32[16,128]{1,0:T(8,128)S(1)}, f32[25,16,128]{0,2,1:T(8,128)}) fusion(f32[25]{0:T(128)S(1)} %copy-done.16, s32[16,128]{1,0:T(8,128)S(1)} %copy-done.12, f32[25,128]{0,1:T(8,128)S(1)} %select_bitcast_fusion.1, f32[25,16,128]{0,2,1:T(8,128)S(1)} %copy-done.5, f32[25,16,1]{0,2,1:T(1,128)S(1)} %collective-permute-done.12, ...), kind=kLoop, calls=%fused_computation.44 | loop fusion | flops 1533952 | bytes 1500392 | tf_op jit(solution)/shard_map/reduce_sum | solution.py:99
  232.9 16.3 %all-gather.3 = f32[1,1024]{1,0:T(1,128)S(1)} all-gather(f32[1,128]{1,0:T(1,128)S(1)} %slice.406), channel_id=5, replica_groups=mesh['grp'=2,'ia'=8,'ja'=2] {'ia'}, dimensions={1}, use_global_device_ids=true | all-gather | bytes 4608 | tf_op jit(solution)/shard_map/all_gather | solution.py:28
  253.9 4.7 %collective-permute-done.17 = f32[16,1]{1,0:T(8,128)S(1)} collective-permute-done((f32[16,1]{1,0:T(8,128)S(1)}, f32[16,1]{1,0:T(8,128)S(1)}, u32[]{:S(2)}, u32[]{:S(2)}) %collective-permute-start.17) | collective-permute-done | bytes 96 | tf_op jit(solution)/shard_map/ppermute | solution.py:20
  260.7 30.4 %all-reduce = (f32[]{:T(128)}, f32[]{:T(128)}) all-reduce(f32[]{:T(128)} %get-tuple-element.17, f32[]{:T(128)} %get-tuple-element.16), channel_id=1, replica_groups=mesh['grp'=2,'ia'=8,'ja'=2] {'ia','ja'}, use_global_device_ids=true, to_apply=%region_11.14 | all-reduce | flops 2 | bytes 16 | tf_op jit(solution)/shard_map/psum | solution.py:40
  293.1 30.1 %psum.62 = f32[]{:T(128)} all-reduce(f32[]{:T(128)} %multiply_reduce_fusion), channel_id=1, replica_groups=mesh['grp'=2,'ia'=8,'ja'=2] {'ia','ja'}, use_global_device_ids=true, to_apply=%region_15.18 | all-reduce | flops 1 | bytes 8 | tf_op jit(solution)/shard_map/psum | solution.py:40
  324.6 16.2 %all-gather.4 = f32[1,1024]{1,0:T(1,128)S(1)} all-gather(f32[1,128]{1,0:T(1,128)S(1)} %slice.409), channel_id=6, replica_groups=mesh['grp'=2,'ia'=8,'ja'=2] {'ia'}, dimensions={1}, use_global_device_ids=true | all-gather | bytes 4608 | tf_op jit(solution)/shard_map/all_gather | solution.py:28
  345.4 4.7 %collective-permute-done.21 = f32[16,1]{1,0:T(8,128)S(1)} collective-permute-done((f32[16,1]{1,0:T(8,128)S(1)}, f32[16,1]{1,0:T(8,128)S(1)}, u32[]{:S(2)}, u32[]{:S(2)}) %collective-permute-start.21) | collective-permute-done | bytes 96 | tf_op jit(solution)/shard_map/ppermute | solution.py:20
  352.2 30.4 %psum.63 = f32[]{:T(128)} all-reduce(f32[]{:T(128)} %fusion.45), channel_id=1, replica_groups=mesh['grp'=2,'ia'=8,'ja'=2] {'ia','ja'}, use_global_device_ids=true, to_apply=%region_17.20 | all-reduce | flops 1 | bytes 8 | tf_op jit(solution)/shard_map/psum | solution.py:50
  386.9 33.4 %all-gather.5 = f32[25,1,1024]{0,2,1:T(8,128)} all-gather(f32[25,1,128]{0,2,1:T(8,128)S(1)} %slice_multiply_fusion), channel_id=7, replica_groups=mesh['grp'=2,'ia'=8,'ja'=2] {'ia'}, dimensions={2}, use_global_device_ids=true | all-gather | bytes 115200 | tf_op jit(solution)/shard_map/all_gather | solution.py:107
  423.5 2.8 fusion.14
  426.3 2.2 copy.166
  (152 shorter events, 53.2 us)
Async XLA Ops:
  2.7 30.2 %collective-permute-start = (f32[16,1]{1,0:T(8,128)S(1)}, f32[16,1]{1,0:T(8,128)S(1)}, u32[]{:S(2)}, u32[]{:S(2)}) collective-permute-start(f32[16,1]{1,0:T(8,128)S(1)} %get-tuple-element.67), channel_id=1, source_target_pairs={{2,0},{4,2},{6,4},{8,6},{10,8},{12,10},{14,12},{0,14},{3,1},{5,3},... | collective-permute-start | bytes 200 | tf_op jit(solution)/shard_map/ppermute | solution.py:21
  8.7 24.2 %collective-permute-start.1 = (f32[16,1]{1,0:T(8,128)S(1)}, f32[16,1]{1,0:T(8,128)S(1)}, u32[]{:S(2)}, u32[]{:S(2)}) collective-permute-start(f32[16,1]{1,0:T(8,128)S(1)} %get-tuple-element.66), channel_id=1, source_target_pairs={{0,2},{2,4},{4,6},{6,8},{8,10},{10,12},{12,14},{14,0},{1,3},{3,5},... | collective-permute-start | bytes 200 | tf_op jit(solution)/shard_map/ppermute | solution.py:20
  33.0 1.3 collective-permute-start.3
  67.4 103.6 %collective-permute-start.8 = (f32[125,16,1]{0,1,2:T(8,128)S(1)}, f32[125,16,1]{0,1,2:T(8,128)S(1)}, u32[]{:S(2)}, u32[]{:S(2)}) collective-permute-start(f32[125,16,1]{0,1,2:T(8,128)S(1)} %bitcast.45), channel_id=1, source_target_pairs={{0,2},{2,4},{4,6},{6,8},{8,10},{10,12},{12,14},{14,0},{1,3},{3,5},... | collective-permute-start | bytes 24008 | tf_op jit(solution)/shard_map/ppermute | solution.py:20
  119.7 3.7 collective-permute-start.4
  121.7 6.3 %collective-permute-start.5 = (f32[16,1]{1,0:T(8,128)S(1)}, f32[16,1]{1,0:T(8,128)S(1)}, u32[]{:S(2)}, u32[]{:S(2)}) collective-permute-start(f32[16,1]{1,0:T(8,128)S(1)} %get-tuple-element.64), channel_id=1, source_target_pairs={{0,2},{2,4},{4,6},{6,8},{8,10},{10,12},{12,14},{14,0},{1,3},{3,5},... | collective-permute-start | bytes 200 | tf_op jit(solution)/shard_map/ppermute | solution.py:20
  128.2 1.3 collective-permute-start.7
  130.2 40.8 %collective-permute-start.9 = (f32[125,16,1]{0,1,2:T(8,128)S(1)}, f32[125,16,1]{0,1,2:T(8,128)S(1)}, u32[]{:S(2)}, u32[]{:S(2)}) collective-permute-start(f32[125,16,1]{0,1,2:T(8,128)S(1)} %bitcast.44), channel_id=1, source_target_pairs={{2,0},{4,2},{6,4},{8,6},{10,8},{12,10},{14,12},{0,14},{3,1},{5,3},... | collective-permute-start | bytes 24008 | tf_op jit(solution)/shard_map/ppermute | solution.py:21
  163.8 3.7 collective-permute-start.12
  163.8 6.6 %collective-permute-start.13 = (f32[25,16,1]{0,2,1:T(1,128)S(1)}, f32[25,16,1]{0,2,1:T(1,128)S(1)}, u32[]{:S(2)}, u32[]{:S(2)}) collective-permute-start(f32[25,16,1]{0,2,1:T(1,128)S(1)} %get-tuple-element.50), channel_id=1, source_target_pairs={{0,2},{2,4},{4,6},{6,8},{8,10},{10,12},{12,14},{14,0},{1,3},{3,5},... | collective-permute-start | bytes 4808 | tf_op jit(solution)/shard_map/ppermute | solution.py:20
  170.4 57.9 %collective-permute-start.14 = (f32[25,1,130]{0,2,1:T(8,128)S(1)}, f32[25,1,130]{0,2,1:T(8,128)}, u32[]{:S(2)}, u32[]{:S(2)}) collective-permute-start(f32[25,1,130]{0,2,1:T(8,128)S(1)} %get-tuple-element.46), channel_id=1, source_target_pairs={{1,0},{0,1},{3,2},{2,3},{5,4},{4,5},{7,6},{6,7},{9,8},{8,9},{11,10... | collective-permute-start | bytes 39008 | tf_op jit(solution)/shard_map/ppermute | solution.py:21
  170.5 57.9 %collective-permute-start.15 = (f32[25,1,130]{0,2,1:T(8,128)S(1)}, f32[25,1,130]{0,2,1:T(8,128)}, u32[]{:S(2)}, u32[]{:S(2)}) collective-permute-start(f32[25,1,130]{0,2,1:T(8,128)S(1)} %get-tuple-element.47), channel_id=1, source_target_pairs={{0,1},{1,0},{2,3},{3,2},{4,5},{5,4},{6,7},{7,6},{8,9},{9,8},{10,11... | collective-permute-start | bytes 39008 | tf_op jit(solution)/shard_map/ppermute | solution.py:20
  171.2 3.2 collective-permute-start.10
  171.3 3.1 collective-permute-start.11
  250.2 3.7 collective-permute-start.16
  252.2 6.3 %collective-permute-start.17 = (f32[16,1]{1,0:T(8,128)S(1)}, f32[16,1]{1,0:T(8,128)S(1)}, u32[]{:S(2)}, u32[]{:S(2)}) collective-permute-start(f32[16,1]{1,0:T(8,128)S(1)} %get-tuple-element.62), channel_id=1, source_target_pairs={{0,2},{2,4},{4,6},{6,8},{8,10},{10,12},{12,14},{14,0},{1,3},{3,5},... | collective-permute-start | bytes 200 | tf_op jit(solution)/shard_map/ppermute | solution.py:20
  258.7 1.3 collective-permute-start.19
  341.7 3.7 collective-permute-start.20
  343.8 6.3 %collective-permute-start.21 = (f32[16,1]{1,0:T(8,128)S(1)}, f32[16,1]{1,0:T(8,128)S(1)}, u32[]{:S(2)}, u32[]{:S(2)}) collective-permute-start(f32[16,1]{1,0:T(8,128)S(1)} %get-tuple-element.60), channel_id=1, source_target_pairs={{0,2},{2,4},{4,6},{6,8},{8,10},{10,12},{12,14},{14,0},{1,3},{3,5},... | collective-permute-start | bytes 200 | tf_op jit(solution)/shard_map/ppermute | solution.py:20
  350.2 1.3 collective-permute-start.23
  384.8 37.2 %collective-permute-start.24 = (f32[25,16,1]{0,2,1:T(1,128)S(1)}, f32[25,16,1]{0,2,1:T(1,128)S(1)}, u32[]{:S(2)}, u32[]{:S(2)}) collective-permute-start(f32[25,16,1]{0,2,1:T(1,128)S(1)} %get-tuple-element.49), channel_id=1, source_target_pairs={{2,0},{4,2},{6,4},{8,6},{10,8},{12,10},{14,12},{0,14},{3,1},{5,3},... | collective-permute-start | bytes 4808 | tf_op jit(solution)/shard_map/ppermute | solution.py:21
  384.9 37.1 %collective-permute-start.25 = (f32[25,16,1]{0,2,1:T(1,128)S(1)}, f32[25,16,1]{0,2,1:T(1,128)S(1)}, u32[]{:S(2)}, u32[]{:S(2)}) collective-permute-start(f32[25,16,1]{0,2,1:T(1,128)S(1)} %get-tuple-element.48), channel_id=1, source_target_pairs={{0,2},{2,4},{4,6},{6,8},{8,10},{10,12},{12,14},{14,0},{1,3},{3,5},... | collective-permute-start | bytes 4808 | tf_op jit(solution)/shard_map/ppermute | solution.py:20
  422.0 1.3 collective-permute-start.26
  422.1 1.4 collective-permute-start.27
  (23 other events, 586.9 us)
where the time goes:
time: 429 us
  blocking collectives  322 us (75%)
  local copies, waits for them, and re-layouts  29.2 us (7%)
  waiting for transfers between devices  27.5 us (6%)
  other arithmetic  20.7 us (5%)
  starting transfers between devices  20.2 us (5%)
  between operations  9.29 us (2%)
    psum x4, blocking collectives, squares(): return lax.psum(jnp.sum(residual * residual), ('ia', 'ja'))  125 us
    all_gather x4, blocking collectives, surface_apply(): top_whole = lax.all_gather(field[-1], 'ia', axis=0, tiled=True)  69.5 us
    all_gather x2, blocking collectives, on_device(): row_whole = lax.all_gather(fold_values, 'ia', axis=1, tiled=True)  66.7 us
    psum x2, blocking collectives, surface_solve(): step_size = norm_now / lax.psum(jnp.sum(direction * applied), ('ia', 'ja'))  60.8 us
    ppermute x14, waiting for transfers between devices, with_halo(): before = lax.ppermute(last, axis, up)  18 us
    ppermute x14, starting transfers between devices, with_halo(): after = lax.ppermute(leading, axis, down)  12.9 us
    ppermute x14, waiting for transfers between devices, with_halo(): after = lax.ppermute(leading, axis, down)  9.54 us
  transfers between devices with their start and end apart: 28, of which 18 were waited for; matrix products, arithmetic and copies ran while one was open for 7% of the time, Pallas kernels for 0%

commit v1 on v0

v1 whole, which is shorter than its diff:
```python
import jax
import jax.numpy as jnp
from jax import lax
from jax.experimental import pallas as pl
from jax.experimental.pallas import tpu as pltpu
from jax.sharding import PartitionSpec as P

SOLVER_ITERS = 2
SURFACE_COEF = 2.0
F32 = jnp.float32

PART1, LEV1, V1ROW, EDGE1, ROWS1 = 16, 17, 18, 48, 64
HROW2, G2ROW, T2ROW, EDGE2, ROWS2 = 16, 17, 42, 72, 88
SHARED = 24
PEER1, PEER2 = 80, 32


def iota(shape, dim):
    return lax.broadcasted_iota(jnp.int32, shape, dim)


def full_sum(x):
    return jnp.sum(jnp.sum(x, axis=0), axis=(0, 1), keepdims=True)


def fold_take(values, block, lane):
    out = jnp.zeros(block.shape, F32)
    for b in range(values.shape[0]):
        source = jnp.broadcast_to(values[b : b + 1], block.shape)
        out = jnp.where(block == b, jnp.take_along_axis(source, lane, axis=1), out)
    return out


def shift_blocks(x, step):
    return jnp.concatenate([x[step:], x[:step]], axis=0)


def surface_apply(field, block, lane):
    n, rows, cols = field.shape
    col = iota(field.shape, 2)
    row = iota(field.shape, 1)
    left = pltpu.roll(field, 1, 2)
    right = pltpu.roll(field, cols - 1, 2)
    west = jnp.where(col == 0, shift_blocks(left, n - 1), left)
    east = jnp.where(col == cols - 1, shift_blocks(right, 1), right)
    across = fold_take(field[:, rows - 1, :], block, lane)
    north = jnp.where(row == rows - 1, across[:, None, :], pltpu.roll(field, rows - 1, 1))
    south = jnp.where(row == 0, 0.0, pltpu.roll(field, 1, 1))
    return (1.0 + 4.0 * SURFACE_COEF) * field - SURFACE_COEF * (east + west + north + south)


def surface_solve(forcing, block, lane):
    residual = forcing
    direction = forcing
    iterate = None
    norm_now = full_sum(residual * residual)
    for sweep in range(SOLVER_ITERS):
        applied = surface_apply(direction, block, lane)
        step_size = norm_now / full_sum(direction * applied)
        part = step_size * direction
        iterate = part if iterate is None else iterate + part
        if sweep + 1 < SOLVER_ITERS:
            residual = residual - step_size * applied
            norm_next = full_sum(residual * residual)
            direction = residual + norm_next / norm_now * direction
            norm_now = norm_next
    return iterate


def level_rows(ref, base, count, rows):
    return ref[pl.ds(base, count, stride=rows), :]


def pack_kernel(cp, adj, surf, u, v, lev, par, out, peer):
    rows, cols = surf.shape
    count = adj.shape[0] // rows
    top = lax.axis_index("ja") == lax.axis_size("ja") - 1
    lane = iota((rows, cols), 1)
    depth = lev[...].astype(F32)
    forcing = surf[...]
    last, first = cols - 1, 0
    edge = jnp.where(lane == 4 * count, depth[:, last:], 0.0)
    edge = jnp.where(lane == 4 * count + 1, depth[:, :1], edge)
    for k in range(count):
        here = adj[k * rows : (k + 1) * rows, :]
        u0 = u[0, k * rows : (k + 1) * rows, :]
        u1 = u[1, k * rows : (k + 1) * rows, :]
        forcing = forcing + cp[k] * jnp.where(depth > k, here, 0.0)
        edge = jnp.where(lane == k, here[:, last:], edge)
        edge = jnp.where(lane == count + k, u1[:, last:], edge)
        edge = jnp.where(lane == 2 * count + k, u0[:, last:], edge)
        edge = jnp.where(lane == 3 * count + k, here[:, :1], edge)
    out[...] = jnp.zeros(out.shape, F32)
    out[0:rows, :] = forcing
    out[PART1 : PART1 + 1, :] = par[...].astype(F32)
    out[LEV1 : LEV1 + 1, :] = depth[rows - 1 :]
    out[EDGE1 : EDGE1 + rows, :] = edge
    peer[...] = jnp.zeros(peer.shape, F32)
    v0row = v[0, pl.ds(rows - 1, count, stride=rows), :]
    out[V1ROW : V1ROW + count, :] = v0row
    is_top = jnp.full((count, cols), top.astype(jnp.int32)) == 1
    peer[0:count, :] = jnp.where(
        is_top, level_rows(adj, 0, count, rows), level_rows(adj, rows - 1, count, rows)
    )
    peer[count : 2 * count, :] = v[1, pl.ds(rows - 1, count, stride=rows), :]
    peer[2 * count : 3 * count, :] = v0row
    peer[3 * count : 3 * count + 1, :] = jnp.where(is_top[:1], depth[:1], depth[rows - 1 :])


def whole_field(mine, other, rows, top):
    n, _, cols = mine.shape
    here = mine[:, 0:rows, :]
    there = other[0 : n * SHARED, :].reshape(n, SHARED, cols)[:, :rows, :]
    is_top = jnp.full(here.shape, top.astype(jnp.int32)) == 1
    low = jnp.where(is_top, there, here)
    high = jnp.where(is_top, here, there)
    return jnp.concatenate([low, high], axis=1)


def top_row(mine, other, index, top):
    n, _, cols = mine.shape
    is_top = jnp.full((n, cols), top.astype(jnp.int32)) == 1
    there = other[pl.ds(index, n, stride=SHARED), :]
    return jnp.where(is_top, mine[:, index, :], there)


def position(n):
    me = lax.axis_index("ia")
    return me, lax.rem(me + n - 1, n), lax.rem(me + 1, n)


def sweep_levels(count, rows, th, fetch, west_of, east_of, u, v, pieces, top, depth, masks, emit):
    own, left, right, beside, beside_temp, beside_v = pieces
    east_depth, west_depth, north_depth, south_depth = masks
    cols = own.shape[1]
    lane = iota((rows, cols), 1)
    row = iota((rows, cols), 0)
    is_top = jnp.full((1, cols), top.astype(jnp.int32)) == 1
    for k in range(count):
        here = fetch(k)
        add = th[k] * own
        mid = here + jnp.where(depth > k, add, 0.0)
        bare = here + add
        u_west, t_west = west_of(k)
        west_value = t_west + th[k] * left
        east_value = jnp.where(
            lane == cols - 1, east_of(k) + th[k] * right, pltpu.roll(bare, cols - 1, 1)
        )
        u_here = u[k * rows : (k + 1) * rows, :]
        v_here = v[k * rows : (k + 1) * rows, :]
        flux_east = jnp.where(east_depth > k, 0.25 * u_here * (east_value - bare), 0.0)
        flux_first = jnp.where(west_depth > k, 0.25 * u_west * (bare - west_value), 0.0)
        flux_west = jnp.where(lane == 0, flux_first, pltpu.roll(flux_east, 1, 1))
        beside_value = beside_temp(k) + th[k] * beside
        above = jnp.where(is_top, 0.0, beside_value)
        north_value = jnp.where(row == rows - 1, above, pltpu.roll(bare, rows - 1, 0))
        flux_north = jnp.where(north_depth > k, 0.25 * v_here * (north_value - bare), 0.0)
        flux_below = jnp.where(south_depth > k, 0.25 * beside_v(k) * (bare[:1] - beside_value), 0.0)
        flux_south = jnp.where(row == 0, flux_below, pltpu.roll(flux_north, 1, 0))
        emit(k, mid + flux_east + flux_west + flux_north + flux_south, flux_north)


def face_depths(depth, edge_left, edge_right, beside_depth, count, top):
    rows, cols = depth.shape
    lane = iota(depth.shape, 1)
    row = iota(depth.shape, 0)
    is_top = jnp.full(depth.shape, top.astype(jnp.int32)) == 1
    right = edge_right[:, 4 * count + 1 : 4 * count + 2]
    east = jnp.minimum(depth, jnp.where(lane == cols - 1, right, pltpu.roll(depth, cols - 1, 1)))
    west = jnp.minimum(depth, edge_left[:, 4 * count : 4 * count + 1])
    above = jnp.where(is_top, depth, beside_depth)
    north = jnp.minimum(depth, jnp.where(row == rows - 1, above, pltpu.roll(depth, rows - 1, 0)))
    south = jnp.where(is_top[:1], jnp.minimum(depth[:1], beside_depth), 0.0)
    return east, west, north, south


def load_pieces(solved, me, west, east, rows, top):
    cols = solved.shape[-1]
    here = pl.ds(pl.multiple_of(jnp.where(top, rows, 0), 8), rows)
    own = solved[me, here, :]
    left = pltpu.roll(solved[west, here, :], 1, 1)
    right = pltpu.roll(solved[east, here, :], cols - 1, 1)
    is_top = jnp.full((1, cols), top.astype(jnp.int32)) == 1
    block = solved[me]
    beside = jnp.where(is_top, block[rows - 1 : rows], block[rows : rows + 1])
    return own, left, right, beside


def first_kernel(cp, th, mine, other, adj, u, v, lev, t_out, out, peer, solved, rowbuf):
    n, _, cols = mine.shape
    rows = lev.shape[0]
    count = adj.shape[0] // rows
    top = lax.axis_index("ja") == lax.axis_size("ja") - 1
    me, west, east = position(n)
    partner = mine[:, PART1, :].astype(jnp.int32)
    block, lane = partner >> 7, partner & 127
    forcing = whole_field(mine, other, rows, top)
    solved[...] = surface_solve(forcing, block, lane)
    rowbuf[...] = fold_take(top_row(mine, other, LEV1, top), block, lane)
    across_depth = rowbuf[pl.ds(me, 1), :]
    depth = lev[...].astype(F32)
    edge_left = mine[west, EDGE1 : EDGE1 + rows, :]
    edge_right = mine[east, EDGE1 : EDGE1 + rows, :]
    base = n * SHARED
    beside_depth = other[base + 3 * count : base + 3 * count + 1, :]
    masks = face_depths(depth, edge_left, edge_right, beside_depth, count, top)
    own, left, right, beside = load_pieces(solved, me, west, east, rows, top)
    pieces = (
        own,
        left,
        right,
        beside,
        lambda k: other[base + k : base + k + 1, :],
        lambda k: other[base + count + k : base + count + k + 1, :],
    )
    out[...] = jnp.zeros(out.shape, F32)
    peer[...] = jnp.zeros(peer.shape, F32)
    spot = iota((rows, cols), 1)
    is_top = jnp.full((1, cols), top.astype(jnp.int32)) == 1
    carry = {
        "forcing": own,
        "edge": jnp.zeros((rows, cols), F32),
        "fold": jnp.zeros((1, cols), F32),
    }

    def emit(k, value, flux_north):
        t_out[k * rows : (k + 1) * rows, :] = value
        carry["forcing"] = carry["forcing"] + cp[k] * jnp.where(depth > k, value, 0.0)
        edge = jnp.where(spot == k, value[:, cols - 1 :], carry["edge"])
        carry["edge"] = jnp.where(spot == count + k, value[:, :1], edge)
        fold = -flux_north[rows - 1 :]
        carry["fold"] = carry["fold"] + cp[k] * jnp.where(across_depth > k, fold, 0.0)
        out[G2ROW + k : G2ROW + k + 1, :] = fold
        out[T2ROW + k : T2ROW + k + 1, :] = value[rows - 1 :]
        peer[k : k + 1, :] = jnp.where(is_top, value[:1], value[rows - 1 :])

    sweep_levels(
        count,
        rows,
        th,
        lambda k: adj[k * rows : (k + 1) * rows, :],
        lambda k: (edge_left[:, count + k : count + k + 1], edge_left[:, k : k + 1]),
        lambda k: edge_right[:, 3 * count + k : 3 * count + k + 1],
        u.at[1],
        v.at[1],
        pieces,
        top,
        depth,
        masks,
        emit,
    )
    out[0:rows, :] = carry["forcing"]
    out[HROW2 : HROW2 + 1, :] = carry["fold"]
    out[EDGE2 : EDGE2 + rows, :] = carry["edge"]


def second_kernel(
    th, mine, other, mine1, other1, temp, u, v, lev, t_out, s_out, solved, rowbuf, rowbuf2
):
    n, _, cols = mine.shape
    rows = lev.shape[0]
    count = temp.shape[0] // rows
    top = lax.axis_index("ja") == lax.axis_size("ja") - 1
    me, west, east = position(n)
    partner = mine1[:, PART1, :].astype(jnp.int32)
    block, lane = partner >> 7, partner & 127
    forcing = whole_field(mine, other, rows, top)
    fold = fold_take(top_row(mine, other, HROW2, top), block, lane)
    row3 = iota(forcing.shape, 1)
    forcing = forcing - jnp.where(row3 == 2 * rows - 1, fold[:, None, :], 0.0)
    iterate = surface_solve(forcing, block, lane)
    solved[...] = iterate
    rowbuf[...] = fold_take(top_row(mine1, other1, LEV1, top), block, lane)
    rowbuf2[...] = fold_take(iterate[:, 2 * rows - 1, :], block, lane)
    across_depth = rowbuf[pl.ds(me, 1), :]
    across_solved = rowbuf2[pl.ds(me, 1), :]

    tall = 32
    spot = iota((1, cols), 1)
    own_partner = mine1[me, PART1 : PART1 + 1, :].astype(jnp.int32)
    beside_left = pltpu.roll(mine1[west, PART1 : PART1 + 8, :], 1, 1)[:1].astype(jnp.int32)
    beside_right = pltpu.roll(mine1[east, PART1 : PART1 + 8, :], cols - 1, 1)[:1].astype(jnp.int32)
    end_partner = jnp.where(spot == 0, beside_left, beside_right)
    end_partner = jnp.where((spot == 0) | (spot == cols - 1), end_partner, 0)
    own_partner = jnp.broadcast_to(own_partner, (tall, cols))
    end_partner = jnp.broadcast_to(end_partner, (tall, cols))
    own_block, own_lane = own_partner >> 7, own_partner & 127
    end_block, end_lane = end_partner >> 7, end_partner & 127
    zero = jnp.zeros((tall, cols), F32)
    fold_own, fold_end, temp_across, v_across = zero, zero, zero, zero
    for b in range(n):
        flux = mine[b, G2ROW : G2ROW + tall, :]
        here = own_block == b
        fold_own = jnp.where(here, jnp.take_along_axis(flux, own_lane, axis=1), fold_own)
        fold_end = jnp.where(
            end_block == b, jnp.take_along_axis(flux, end_lane, axis=1), fold_end
        )
        line = mine[b, T2ROW : T2ROW + tall, :]
        temp_across = jnp.where(here, jnp.take_along_axis(line, own_lane, axis=1), temp_across)
        speed = mine1[b, V1ROW : V1ROW + tall, :]
        v_across = jnp.where(here, jnp.take_along_axis(speed, own_lane, axis=1), v_across)
    level = iota((tall, cols), 0)
    weight = zero
    for k in range(count):
        weight = jnp.where(level == k, th[k], weight)
    sent = mine[me, G2ROW : G2ROW + tall, :]
    fold_last = jnp.where(
        across_depth > level.astype(F32),
        0.25 * v_across * (temp_across - sent + weight * across_solved),
        0.0,
    )

    depth = lev[...].astype(F32)
    edge1_left = mine1[west, EDGE1 : EDGE1 + rows, :]
    edge1_right = mine1[east, EDGE1 : EDGE1 + rows, :]
    edge_left = mine[west, EDGE2 : EDGE2 + rows, :]
    edge_right = mine[east, EDGE2 : EDGE2 + rows, :]
    base, base1 = n * SHARED, n * SHARED
    beside_depth = other1[base1 + 3 * count : base1 + 3 * count + 1, :]
    masks = face_depths(depth, edge1_left, edge1_right, beside_depth, count, top)
    own, left, right, beside = load_pieces(solved, me, west, east, rows, top)
    s_out[...] = own
    pieces = (
        own,
        left,
        right,
        beside,
        lambda k: other[base + k : base + k + 1, :],
        lambda k: other1[base1 + 2 * count + k : base1 + 2 * count + k + 1, :],
    )
    row = iota((rows, cols), 0)
    on_fold = (row == rows - 1) & (jnp.full((rows, cols), top.astype(jnp.int32)) == 1)

    def less(value, lines, k):
        return value - jnp.where(on_fold, lines[k : k + 1], 0.0)

    def emit(k, value, flux_north):
        t_out[k * rows : (k + 1) * rows, :] = less(value, fold_last, k)

    sweep_levels(
        count,
        rows,
        th,
        lambda k: less(temp[k * rows : (k + 1) * rows, :], fold_own, k),
        lambda k: (
            edge1_left[:, 2 * count + k : 2 * count + k + 1],
            less(jnp.broadcast_to(edge_left[:, k : k + 1], (rows, cols)), fold_end, k),
        ),
        lambda k: less(
            jnp.broadcast_to(edge_right[:, count + k : count + k + 1], (rows, cols)), fold_end, k
        ),
        u.at[0],
        v.at[0],
        pieces,
        top,
        depth,
        masks,
        emit,
    )


def gather_columns(block):
    n = lax.axis_size("ia")
    me = lax.axis_index("ia")
    y = block
    dim = 0
    step = n // 2
    while step:
        z = lax.ppermute(y, "ia", [(i, i ^ step) for i in range(n)])
        odd = (me // step) % 2 == 1
        y = jnp.where(odd, jnp.stack([z, y], axis=dim), jnp.stack([y, z], axis=dim))
        dim += 1
        step //= 2
    return y.reshape((n,) + block.shape)


def swap_cores(gathered, peer):
    n, _, cols = gathered.shape
    shared = gathered[:, :SHARED, :].reshape(n * SHARED, cols)
    return lax.ppermute(jnp.concatenate([shared, peer]), "ja", [(0, 1), (1, 0)])


def on_device(
    adjoint_temp, adjoint_surface, trajectory_u, trajectory_v, levels, partner, thickness, coupling
):
    steps, count, rows, cols = trajectory_u.shape
    n = lax.axis_size("ia")
    flat = count * rows
    adj = adjoint_temp.reshape(flat, cols)
    u = trajectory_u.reshape(steps, flat, cols)
    v = trajectory_v.reshape(steps, flat, cols)
    par = partner.reshape(1, cols)
    smem = pl.BlockSpec(memory_space=pltpu.SMEM)
    vmem = pl.BlockSpec(memory_space=pltpu.VMEM)

    def shape(*dims):
        return jax.ShapeDtypeStruct(dims, F32)

    out, peer = pl.pallas_call(
        pack_kernel,
        out_shape=(shape(ROWS1, cols), shape(PEER1, cols)),
        in_specs=[smem] + [vmem] * 6,
        out_specs=(vmem, vmem),
    )(coupling, adj, adjoint_surface, u, v, levels, par)
    mine1 = gather_columns(out)
    other1 = swap_cores(mine1, peer)
    temp, out, peer = pl.pallas_call(
        first_kernel,
        out_shape=(shape(flat, cols), shape(ROWS2, cols), shape(PEER2, cols)),
        in_specs=[smem, smem] + [vmem] * 6,
        out_specs=(vmem, vmem, vmem),
        scratch_shapes=[pltpu.VMEM((n, 2 * rows, cols), F32), pltpu.VMEM((n, cols), F32)],
    )(coupling, thickness, mine1, other1, adj, u, v, levels)
    mine = gather_columns(out)
    other = swap_cores(mine, peer)
    temp_gradient, surface_gradient = pl.pallas_call(
        second_kernel,
        out_shape=(shape(flat, cols), shape(rows, cols)),
        in_specs=[smem] + [vmem] * 8,
        out_specs=(vmem, vmem),
        scratch_shapes=[
            pltpu.VMEM((n, 2 * rows, cols), F32),
            pltpu.VMEM((n, cols), F32),
            pltpu.VMEM((n, cols), F32),
        ],
    )(thickness, mine, other, mine1, other1, temp, u, v, levels)
    return temp_gradient.reshape(count, rows, cols), surface_gradient


def solution(mesh):
    return jax.shard_map(
        on_device,
        mesh=mesh,
        in_specs=(
            P("grp", "ja", "ia"),
            P(("grp", "ja"), "ia"),
            P(None, None, "ja", "ia"),
            P(None, None, "ja", "ia"),
            P("ja", "ia"),
            P("ia"),
            P(),
            P(),
        ),
        out_specs=(P("grp", "ja", "ia"), P(("grp", "ja"), "ia")),
        check_vma=False,
    )
```

time: 429 us -> 48.7 us (0.11)
  blocking collectives: 322 us -> 0 us
  local copies, waits for them, and re-layouts: 29.2 us -> 2.9 us
  other arithmetic: 20.7 us -> 1.07 us
  Pallas kernels: 0 us -> 9.02 us
  between operations: 9.29 us -> 0.76 us
  starting transfers between devices: 20.2 us -> 13.5 us
  waiting for transfers between devices: 27.5 us -> 21 us
    psum x6 -> x0, blocking collectives: 185 us -> none  [the longest x4 125 us: squares(): return lax.psum(jnp.sum(residual * residual), ('ia', 'ja'))]
    all_gather x6 -> x0, blocking collectives: 136 us -> none  [the longest x4 69.5 us: surface_apply(): top_whole = lax.all_gather(field[-1], 'ia', axis=0, tiled=True)]
    reduce_sum x8 -> x0, other arithmetic: 9.04 us -> none  [the longest x2 5.08 us: on_device(): jnp.sum(coupling[:, None, None] * ocean * temp_gradient, axis=0)]
    pallas_call x0 -> x3, Pallas kernels: none -> 9.02 us  [the longest x1 3.45 us: on_device(): pl.pallas_call(second_kernel, out_shape=(shape(flat, cols), shape(rows, c...]
    reshape x4 -> x0, local copies, waits for them, and re-layouts: 9.02 us -> none  [the longest x1 3.64 us: on_device(): padded[:layer_count]]
    gather x6 -> x0, local copies, waits for them, and re-layouts: 7.25 us -> none  [the longest x4 3.88 us: surface_apply(): across = jnp.take(top_whole, partner)]
    ppermute x28 -> x8, starting transfers between devices: 20.2 us -> 13.5 us  [the longest x6 13.4 us: gather_columns(): z = lax.ppermute(y, 'ia', [(i, i ^ step) for i in range(n)])]
    mul x7 -> x0, other arithmetic: 6.55 us -> none  [the longest x2 2.85 us: on_device(): 0.5 * speed_u[:, :, 1:-1, :-1] * ocean_rows[None, :, :, :-1]]
  transfers between devices with their start and end apart: 28 -> 8, of which waited for: 18 -> 8; matrix products, arithmetic and copies ran while one was open for 7% -> 0% of each run, Pallas kernels for 0% -> 0%
where the time goes in v1:
time: 48.7 us; the launch traced here: 48.3 us
  waiting for transfers between devices  21 us (43%)
  starting transfers between devices  13.5 us (28%)
  Pallas kernels  9.02 us (19%)
  local copies, waits for them, and re-layouts  2.9 us (6%)
  other arithmetic  1.07 us (2%)
  between operations  0.76 us (2%)
    ppermute x6, waiting for transfers between devices, gather_columns(): z = lax.ppermute(y, 'ia', [(i, i ^ step) for i in range(n)])  18.3 us
    ppermute x6, starting transfers between devices, gather_columns(): z = lax.ppermute(y, 'ia', [(i, i ^ step) for i in range(n)])  13.4 us
    pallas_call x1, Pallas kernels, on_device(): pl.pallas_call(second_kernel, out_shape=(shape(flat, cols), shape(rows, c...  3.45 us
    pallas_call x1, Pallas kernels, on_device(): pl.pallas_call(first_kernel, out_shape=(shape(flat, cols), shape(ROWS2, c...  3.34 us
    unnamed x16, local copies, waits for them, and re-layouts  2.84 us
    ppermute x2, waiting for transfers between devices, swap_cores(): return lax.ppermute(jnp.concatenate([shared, peer]), 'ja', [(0, 1), (1, 0)])  2.66 us
    pallas_call x1, Pallas kernels, on_device(): pl.pallas_call(pack_kernel, out_shape=(shape(ROWS1, cols), shape(PEER1, c...  2.23 us
    select_n x10, other arithmetic, gather_columns(): y = jnp.where(odd, jnp.stack([z, y], axis=dim), jnp.stack([y, z], axis=dim))  1.05 us
  transfers between devices with their start and end apart: 8, of which 8 were waited for; matrix products, arithmetic and copies ran while one was open for 0% of the time, Pallas kernels for 0%

profile of v1, /device:TPU:0, one launch (start us, length us, event | category | flops | bytes accessed | tf_op | source)
XLA Modules:
  0.0 48.3 jit_solution(16859148171255356573)
XLA Ops:
  0.6 2.2 %shard_map.95 = (f32[64,128]{1,0:T(8,128)}, f32[80,128]{1,0:T(8,128)}) custom-call(f32[25]{0:T(128)} %cp.3, f32[400,128]{1,0:T(8,128)} %bitcast.42, f32[16,128]{1,0:T(8,128)} %surf.1, f32[2,400,128]{2,1,0:T(8,128)} %bitcast.31, f32[2,400,128]{2,1,0:T(8,128)} %bitcast.34, s32[16,128]{1,0:T(8,128)} %lev.5, s32[1,128]{1,0:T(1,128)} %bitcast.60), custom_call_target="tpu_custom_call" | custom-call | tf_op jit(solution)/shard_map/pallas_call | solution.py:399
  2.9 4.0 %collective-permute-start = (f32[64,128]{1,0:T(8,128)}, f32[64,128]{1,0:T(8,128)S(1)}, u32[]{:S(2)}, u32[]{:S(2)}) collective-permute-start(f32[64,128]{1,0:T(8,128)} %get-tuple-element.9), channel_id=1, source_target_pairs={{0,8},{2,10},{4,12},{6,14},{8,0},{10,2},{12,4},{14,6},{1,9},{3,11}... | collective-permute-start | bytes 98312 | tf_op jit(solution)/shard_map/ppermute | solution.py:369
  6.9 2.5 %collective-permute-done = f32[64,128]{1,0:T(8,128)S(1)} collective-permute-done((f32[64,128]{1,0:T(8,128)}, f32[64,128]{1,0:T(8,128)S(1)}, u32[]{:S(2)}, u32[]{:S(2)}) %collective-permute-start) | collective-permute-done | bytes 32800 | tf_op jit(solution)/shard_map/ppermute | solution.py:369
  9.4 1.6 %collective-permute-start.1 = (f32[2,64,128]{2,1,0:T(8,128)S(1)}, f32[2,64,128]{2,1,0:T(8,128)S(1)}, u32[]{:S(2)}, u32[]{:S(2)}) collective-permute-start(f32[2,64,128]{2,1,0:T(8,128)S(1)} %maximum_select_fusion.8), channel_id=1, source_target_pairs={{0,4},{2,6},{4,0},{6,2},{8,12},{10,14},{12,8},{14,10},{1,5},{3,7},... | collective-permute-start | bytes 196616 | tf_op jit(solution)/shard_map/ppermute | solution.py:369
  11.0 2.7 %collective-permute-done.1 = f32[2,64,128]{2,1,0:T(8,128)S(1)} collective-permute-done((f32[2,64,128]{2,1,0:T(8,128)S(1)}, f32[2,64,128]{2,1,0:T(8,128)S(1)}, u32[]{:S(2)}, u32[]{:S(2)}) %collective-permute-start.1) | collective-permute-done | bytes 65568 | tf_op jit(solution)/shard_map/ppermute | solution.py:369
  13.7 1.8 %collective-permute-start.2 = (f32[2,2,64,128]{3,2,0,1:T(8,128)S(1)}, f32[2,2,64,128]{3,2,0,1:T(8,128)S(1)}, u32[]{:S(2)}, u32[]{:S(2)}) collective-permute-start(f32[2,2,64,128]{3,2,0,1:T(8,128)S(1)} %maximum_select_fusion.4), channel_id=1, source_target_pairs={{0,2},{2,0},{4,6},{6,4},{8,10},{10,8},{12,14},{14,12},{1,3},{3,1},... | collective-permute-start | bytes 393224 | tf_op jit(solution)/shard_map/ppermute | solution.py:369
  15.5 3.3 %collective-permute-done.2 = f32[2,2,64,128]{3,2,0,1:T(8,128)S(1)} collective-permute-done((f32[2,2,64,128]{3,2,0,1:T(8,128)S(1)}, f32[2,2,64,128]{3,2,0,1:T(8,128)S(1)}, u32[]{:S(2)}, u32[]{:S(2)}) %collective-permute-start.2) | collective-permute-done | bytes 131104 | tf_op jit(solution)/shard_map/ppermute | solution.py:369
  18.8 0.8 %copy-done.6 = f32[80,128]{1,0:T(8,128)S(1)} copy-done((f32[80,128]{1,0:T(8,128)S(1)}, f32[80,128]{1,0:T(8,128)}, u32[]{:S(2)}) %copy-start.6) | copy-done | bytes 40984
  19.6 0.1 collective-permute-start.3
  19.7 1.3 %collective-permute-done.3.other.other1 = f32[272,128]{1,0:T(8,128)S(1)} collective-permute-done((f32[272,128]{1,0:T(8,128)S(1)}, f32[272,128]{1,0:T(8,128)S(1)}, u32[]{:S(2)}, u32[]{:S(2)}) %collective-permute-start.3) | collective-permute-done | bytes 139296 | tf_op jit(solution)/shard_map/ppermute | solution.py:380
  21.1 0.7 %copy-done.2 = f32[272,128]{1,0:T(8,128)} copy-done((f32[272,128]{1,0:T(8,128)}, f32[272,128]{1,0:T(8,128)S(1)}, u32[]{:S(2)}) %copy-start.2) | copy-done | bytes 139288
  21.7 3.3 %shard_map.96 = (f32[400,128]{1,0:T(8,128)}, f32[88,128]{1,0:T(8,128)}, f32[32,128]{1,0:T(8,128)}) custom-call(f32[25]{0:T(128)} %cp.3, f32[25]{0:T(128)} %th.3, f32[8,64,128]{2,1,0:T(8,128)} %bitcast.38, f32[272,128]{1,0:T(8,128)} %copy-done.2, f32[400,128]{1,0:T(8,128)} %bitcast.43, f32[2,400,128]{2,1,0:T(8,128)} %bitcast.32, f32[2,400,128]{2,1,0:T(8,128)} %bitcast.35, ...), custom_call_target="tpu_custom_call" | custom-call | tf_op jit(solution)/shard_map/pallas_call | solution.py:407
  25.1 2.6 %collective-permute-start.4 = (f32[88,128]{1,0:T(8,128)}, f32[88,128]{1,0:T(8,128)S(1)}, u32[]{:S(2)}, u32[]{:S(2)}) collective-permute-start(f32[88,128]{1,0:T(8,128)} %get-tuple-element.11), channel_id=1, source_target_pairs={{0,8},{2,10},{4,12},{6,14},{8,0},{10,2},{12,4},{14,6},{1,9},{3,11}... | collective-permute-start | bytes 135176 | tf_op jit(solution)/shard_map/ppermute | solution.py:369
  27.7 3.0 %collective-permute-done.4 = f32[88,128]{1,0:T(8,128)S(1)} collective-permute-done((f32[88,128]{1,0:T(8,128)}, f32[88,128]{1,0:T(8,128)S(1)}, u32[]{:S(2)}, u32[]{:S(2)}) %collective-permute-start.4) | collective-permute-done | bytes 45088 | tf_op jit(solution)/shard_map/ppermute | solution.py:369
  30.7 0.9 %maximum_select_fusion.6 = f32[2,88,128]{2,1,0:T(8,128)S(1)} fusion(f32[1,88,128]{2,1,0:T(8,128)} %bitcast.51, f32[1,88,128]{2,1,0:T(8,128)S(1)} %bitcast.53, pred[]{:T(512)S(6)} %eq.21), kind=kLoop, calls=%fused_computation.8 | loop fusion | flops 67584 | bytes 180225 | tf_op jit(solution)/shard_map/jit(_where)/select_n | solution.py:371
  31.6 1.1 %collective-permute-start.5 = (f32[2,88,128]{2,1,0:T(8,128)S(1)}, f32[2,88,128]{2,1,0:T(8,128)S(1)}, u32[]{:S(2)}, u32[]{:S(2)}) collective-permute-start(f32[2,88,128]{2,1,0:T(8,128)S(1)} %maximum_select_fusion.6), channel_id=1, source_target_pairs={{0,4},{2,6},{4,0},{6,2},{8,12},{10,14},{12,8},{14,10},{1,5},{3,7},... | collective-permute-start | bytes 270344 | tf_op jit(solution)/shard_map/ppermute | solution.py:369
  32.8 3.4 %collective-permute-done.5 = f32[2,88,128]{2,1,0:T(8,128)S(1)} collective-permute-done((f32[2,88,128]{2,1,0:T(8,128)S(1)}, f32[2,88,128]{2,1,0:T(8,128)S(1)}, u32[]{:S(2)}, u32[]{:S(2)}) %collective-permute-start.5) | collective-permute-done | bytes 90144 | tf_op jit(solution)/shard_map/ppermute | solution.py:369
  36.2 2.2 %collective-permute-start.6 = (f32[2,2,88,128]{3,2,0,1:T(8,128)S(1)}, f32[2,2,88,128]{3,2,0,1:T(8,128)S(1)}, u32[]{:S(2)}, u32[]{:S(2)}) collective-permute-start(f32[2,2,88,128]{3,2,0,1:T(8,128)S(1)} %maximum_select_fusion.2), channel_id=1, source_target_pairs={{0,2},{2,0},{4,6},{6,4},{8,10},{10,8},{12,14},{14,12},{1,3},{3,1},... | collective-permute-start | bytes 540680 | tf_op jit(solution)/shard_map/ppermute | solution.py:369
  38.5 3.5 %collective-permute-done.6 = f32[2,2,88,128]{3,2,0,1:T(8,128)S(1)} collective-permute-done((f32[2,2,88,128]{3,2,0,1:T(8,128)S(1)}, f32[2,2,88,128]{3,2,0,1:T(8,128)S(1)}, u32[]{:S(2)}, u32[]{:S(2)}) %collective-permute-start.6) | collective-permute-done | bytes 180256 | tf_op jit(solution)/shard_map/ppermute | solution.py:369
  42.1 0.7 %copy-done.7 = f32[32,128]{1,0:T(8,128)S(1)} copy-done((f32[32,128]{1,0:T(8,128)S(1)}, f32[32,128]{1,0:T(8,128)}, u32[]{:S(2)}) %copy-start.7) | copy-done | bytes 16408
  42.8 0.1 collective-permute-start.7
  42.9 1.3 %collective-permute-done.7.other = f32[224,128]{1,0:T(8,128)S(1)} collective-permute-done((f32[224,128]{1,0:T(8,128)S(1)}, f32[224,128]{1,0:T(8,128)S(1)}, u32[]{:S(2)}, u32[]{:S(2)}) %collective-permute-start.7) | collective-permute-done | bytes 114720 | tf_op jit(solution)/shard_map/ppermute | solution.py:380
  44.2 0.6 %copy-done.5 = f32[224,128]{1,0:T(8,128)} copy-done((f32[224,128]{1,0:T(8,128)}, f32[224,128]{1,0:T(8,128)S(1)}, u32[]{:S(2)}) %copy-start.5) | copy-done | bytes 114712
  44.8 3.5 %shard_map.97 = (f32[400,128]{1,0:T(8,128)}, f32[16,128]{1,0:T(8,128)}) custom-call(f32[25]{0:T(128)} %th.3, f32[8,88,128]{2,1,0:T(8,128)} %bitcast.41, f32[224,128]{1,0:T(8,128)} %copy-done.5, f32[8,64,128]{2,1,0:T(8,128)} %bitcast.39, f32[272,128]{1,0:T(8,128)} %copy-done.2, f32[400,128]{1,0:T(8,128)} %get-tuple-element.13.temp, f32[2,400,128]{2,1,0:T(8,128)} %bitcast.33, ...), custom_call_target="tpu_custom_call" | custom-call | tf_op jit(solution)/shard_map/pallas_call | solution.py:416
  (27 shorter events, 0.3 us)
Async XLA Ops:
  2.9 6.5 %collective-permute-start = (f32[64,128]{1,0:T(8,128)}, f32[64,128]{1,0:T(8,128)S(1)}, u32[]{:S(2)}, u32[]{:S(2)}) collective-permute-start(f32[64,128]{1,0:T(8,128)} %get-tuple-element.9), channel_id=1, source_target_pairs={{0,8},{2,10},{4,12},{6,14},{8,0},{10,2},{12,4},{14,6},{1,9},{3,11}... | collective-permute-start | bytes 98312 | tf_op jit(solution)/shard_map/ppermute | solution.py:369
  6.9 2.5 %copy-start.4 = (f32[64,128]{1,0:T(8,128)S(1)}, f32[64,128]{1,0:T(8,128)}, u32[]{:S(2)}) copy-start(f32[64,128]{1,0:T(8,128)} %get-tuple-element.9) | copy-start | bytes 98308
  9.4 4.3 %collective-permute-start.1 = (f32[2,64,128]{2,1,0:T(8,128)S(1)}, f32[2,64,128]{2,1,0:T(8,128)S(1)}, u32[]{:S(2)}, u32[]{:S(2)}) collective-permute-start(f32[2,64,128]{2,1,0:T(8,128)S(1)} %maximum_select_fusion.8), channel_id=1, source_target_pairs={{0,4},{2,6},{4,0},{6,2},{8,12},{10,14},{12,8},{14,10},{1,5},{3,7},... | collective-permute-start | bytes 196616 | tf_op jit(solution)/shard_map/ppermute | solution.py:369
  13.7 5.0 %collective-permute-start.2 = (f32[2,2,64,128]{3,2,0,1:T(8,128)S(1)}, f32[2,2,64,128]{3,2,0,1:T(8,128)S(1)}, u32[]{:S(2)}, u32[]{:S(2)}) collective-permute-start(f32[2,2,64,128]{3,2,0,1:T(8,128)S(1)} %maximum_select_fusion.4), channel_id=1, source_target_pairs={{0,2},{2,0},{4,6},{6,4},{8,10},{10,8},{12,14},{14,12},{1,3},{3,1},... | collective-permute-start | bytes 393224 | tf_op jit(solution)/shard_map/ppermute | solution.py:369
  18.8 2.3 %copy-start = (f32[2,2,2,64,128]{4,3,2,1,0:T(8,128)}, f32[2,2,2,64,128]{4,3,2,1,0:T(8,128)S(1)}, u32[]{:S(2)}) copy-start(f32[2,2,2,64,128]{4,3,2,1,0:T(8,128)S(1)} %copy.12) | copy-start | bytes 786436
  18.8 0.8 %copy-start.6 = (f32[80,128]{1,0:T(8,128)S(1)}, f32[80,128]{1,0:T(8,128)}, u32[]{:S(2)}) copy-start(f32[80,128]{1,0:T(8,128)} %get-tuple-element.10) | copy-start | bytes 122884
  19.6 1.4 %collective-permute-start.3 = (f32[272,128]{1,0:T(8,128)S(1)}, f32[272,128]{1,0:T(8,128)S(1)}, u32[]{:S(2)}, u32[]{:S(2)}) collective-permute-start(f32[272,128]{1,0:T(8,128)S(1)} %pad_maximum_fusion), channel_id=1, source_target_pairs={{0,1},{1,0},{2,3},{3,2},{4,5},{5,4},{6,7},{7,6},{8,9},{9,8},{10,11... | collective-permute-start | bytes 417800 | tf_op jit(solution)/shard_map/ppermute | solution.py:380
  21.1 0.7 %copy-start.2 = (f32[272,128]{1,0:T(8,128)}, f32[272,128]{1,0:T(8,128)S(1)}, u32[]{:S(2)}) copy-start(f32[272,128]{1,0:T(8,128)S(1)} %collective-permute-done.3.other.other1) | copy-start | bytes 417796
  25.1 5.6 %collective-permute-start.4 = (f32[88,128]{1,0:T(8,128)}, f32[88,128]{1,0:T(8,128)S(1)}, u32[]{:S(2)}, u32[]{:S(2)}) collective-permute-start(f32[88,128]{1,0:T(8,128)} %get-tuple-element.11), channel_id=1, source_target_pairs={{0,8},{2,10},{4,12},{6,14},{8,0},{10,2},{12,4},{14,6},{1,9},{3,11}... | collective-permute-start | bytes 135176 | tf_op jit(solution)/shard_map/ppermute | solution.py:369
  30.7 2.1 %copy-start.3 = (f32[88,128]{1,0:T(8,128)S(1)}, f32[88,128]{1,0:T(8,128)}, u32[]{:S(2)}) copy-start(f32[88,128]{1,0:T(8,128)} %get-tuple-element.11) | copy-start | bytes 135172
  31.6 4.6 %collective-permute-start.5 = (f32[2,88,128]{2,1,0:T(8,128)S(1)}, f32[2,88,128]{2,1,0:T(8,128)S(1)}, u32[]{:S(2)}, u32[]{:S(2)}) collective-permute-start(f32[2,88,128]{2,1,0:T(8,128)S(1)} %maximum_select_fusion.6), channel_id=1, source_target_pairs={{0,4},{2,6},{4,0},{6,2},{8,12},{10,14},{12,8},{14,10},{1,5},{3,7},... | collective-permute-start | bytes 270344 | tf_op jit(solution)/shard_map/ppermute | solution.py:369
  36.2 5.7 %collective-permute-start.6 = (f32[2,2,88,128]{3,2,0,1:T(8,128)S(1)}, f32[2,2,88,128]{3,2,0,1:T(8,128)S(1)}, u32[]{:S(2)}, u32[]{:S(2)}) collective-permute-start(f32[2,2,88,128]{3,2,0,1:T(8,128)S(1)} %maximum_select_fusion.2), channel_id=1, source_target_pairs={{0,2},{2,0},{4,6},{6,4},{8,10},{10,8},{12,14},{14,12},{1,3},{3,1},... | collective-permute-start | bytes 540680 | tf_op jit(solution)/shard_map/ppermute | solution.py:369
  42.0 2.2 %copy-start.1 = (f32[2,2,2,88,128]{4,3,2,1,0:T(8,128)}, f32[2,2,2,88,128]{4,3,2,1,0:T(8,128)S(1)}, u32[]{:S(2)}) copy-start(f32[2,2,2,88,128]{4,3,2,1,0:T(8,128)S(1)} %copy.15) | copy-start | bytes 1081348
  42.0 0.7 %copy-start.7 = (f32[32,128]{1,0:T(8,128)S(1)}, f32[32,128]{1,0:T(8,128)}, u32[]{:S(2)}) copy-start(f32[32,128]{1,0:T(8,128)} %get-tuple-element.12) | copy-start | bytes 49156
  42.8 1.4 %collective-permute-start.7 = (f32[224,128]{1,0:T(8,128)S(1)}, f32[224,128]{1,0:T(8,128)S(1)}, u32[]{:S(2)}, u32[]{:S(2)}) collective-permute-start(f32[224,128]{1,0:T(8,128)S(1)} %pad_maximum_fusion.1), channel_id=1, source_target_pairs={{0,1},{1,0},{2,3},{3,2},{4,5},{5,4},{6,7},{7,6},{8,9},{9,8},{10,11... | collective-permute-start | bytes 344072 | tf_op jit(solution)/shard_map/ppermute | solution.py:380
  44.2 0.6 %copy-start.5 = (f32[224,128]{1,0:T(8,128)}, f32[224,128]{1,0:T(8,128)S(1)}, u32[]{:S(2)}) copy-start(f32[224,128]{1,0:T(8,128)S(1)} %collective-permute-done.7.other) | copy-start | bytes 344068

commit v2 on v1

v2 whole, which is shorter than its diff:
```python
import jax
import jax.numpy as jnp
from jax import lax
from jax.experimental import pallas as pl
from jax.experimental.pallas import tpu as pltpu
from jax.sharding import PartitionSpec as P

SOLVER_ITERS = 2
SURFACE_COEF = 2.0
F32 = jnp.float32

EDGE1, PART1, LEV1, ROWS1 = 16, 32, 33, 40
EDGE2, HROW2, LINE2, FLUX2, ROWS2 = 16, 24, 25, 50, 64
PEER1, PEER2 = 104, 32
WINDOW = 16
TALL = 32


def iota(shape, dim):
    return lax.broadcasted_iota(jnp.int32, shape, dim)


def full_sum(x):
    return jnp.sum(jnp.sum(x, axis=0), axis=(0, 1), keepdims=True)


def split_index(column, cols):
    return column >> (cols.bit_length() - 1), column & (cols - 1)


def fold_take(values, block, lane):
    out = jnp.zeros(block.shape, F32)
    for b in range(values.shape[0]):
        source = jnp.broadcast_to(values[b : b + 1], block.shape)
        out = jnp.where(block == b, jnp.take_along_axis(source, lane, axis=1), out)
    return out


def shift_blocks(x, step):
    return jnp.concatenate([x[step:], x[:step]], axis=0)


def surface_apply(field, block, lane):
    n, rows, cols = field.shape
    col = iota(field.shape, 2)
    row = iota(field.shape, 1)
    left = pltpu.roll(field, 1, 2)
    right = pltpu.roll(field, cols - 1, 2)
    west = jnp.where(col == 0, shift_blocks(left, n - 1), left)
    east = jnp.where(col == cols - 1, shift_blocks(right, 1), right)
    across = fold_take(field[:, rows - 1, :], block, lane)
    north = jnp.where(row == rows - 1, across[:, None, :], pltpu.roll(field, rows - 1, 1))
    south = jnp.where(row == 0, 0.0, pltpu.roll(field, 1, 1))
    return (1.0 + 4.0 * SURFACE_COEF) * field - SURFACE_COEF * (east + west + north + south)


def surface_solve(forcing, block, lane):
    residual = forcing
    direction = forcing
    iterate = None
    norm_now = full_sum(residual * residual)
    for sweep in range(SOLVER_ITERS):
        applied = surface_apply(direction, block, lane)
        step_size = norm_now / full_sum(direction * applied)
        part = step_size * direction
        iterate = part if iterate is None else iterate + part
        if sweep + 1 < SOLVER_ITERS:
            residual = residual - step_size * applied
            norm_next = full_sum(residual * residual)
            direction = residual + norm_next / norm_now * direction
            norm_now = norm_next
    return iterate


def level_rows(ref, base, count, rows):
    return ref[pl.ds(base, count, stride=rows), :]


def pack_kernel(cp, adj, surf, u, v, lev, par, out, peer):
    rows, cols = surf.shape
    count = adj.shape[0] // rows
    top = lax.axis_index("ja") == lax.axis_size("ja") - 1
    lane = iota((rows, cols), 1)
    depth = lev[...].astype(F32)
    forcing = surf[...]
    last, first = cols - 1, 0
    edge = jnp.where(lane == 4 * count, depth[:, last:], 0.0)
    edge = jnp.where(lane == 4 * count + 1, depth[:, :1], edge)
    for k in range(count):
        here = adj[k * rows : (k + 1) * rows, :]
        u0 = u[0, k * rows : (k + 1) * rows, :]
        u1 = u[1, k * rows : (k + 1) * rows, :]
        forcing = forcing + cp[k] * jnp.where(depth > k, here, 0.0)
        edge = jnp.where(lane == k, here[:, last:], edge)
        edge = jnp.where(lane == count + k, u1[:, last:], edge)
        edge = jnp.where(lane == 2 * count + k, u0[:, last:], edge)
        edge = jnp.where(lane == 3 * count + k, here[:, :1], edge)
    out[0:rows, :] = forcing
    out[EDGE1 : EDGE1 + rows, :] = edge
    out[PART1:ROWS1, :] = jnp.zeros((ROWS1 - PART1, cols), F32)
    out[PART1 : PART1 + 1, :] = par[...].astype(F32)
    out[LEV1 : LEV1 + 1, :] = depth[rows - 1 :]
    peer[...] = jnp.zeros(peer.shape, F32)
    is_top = jnp.full((count, cols), top.astype(jnp.int32)) == 1
    last_row = level_rows(adj, rows - 1, count, rows)
    peer[0:count, :] = jnp.where(is_top, level_rows(adj, 0, count, rows), last_row)
    peer[count : 2 * count, :] = v[1, pl.ds(rows - 1, count, stride=rows), :]
    peer[2 * count : 3 * count, :] = v[0, pl.ds(rows - 1, count, stride=rows), :]
    peer[3 * count : 4 * count, :] = last_row
    peer[4 * count : 4 * count + 1, :] = jnp.where(is_top[:1], depth[:1], depth[rows - 1 :])


def parity(x):
    for shift in (16, 8, 4, 2, 1):
        x = x ^ (x >> shift)
    return x & 1


class Messages:
    def __init__(self, both):
        self.both = both
        self.count = both.shape[1]
        self.cols = both.shape[3]
        self.me = lax.axis_index("ia")
        self.core = lax.axis_index("ja")

    def place(self, block, core):
        return core ^ self.core ^ parity(block ^ self.me)

    def part(self, block, core, start, stop):
        return self.both[self.place(block, core), block, start:stop, :]

    def field(self, rows):
        blocks = [
            jnp.concatenate([self.part(b, 0, 0, rows), self.part(b, 1, 0, rows)], axis=0)
            for b in range(self.count)
        ]
        return jnp.stack(blocks, axis=0)

    def line(self, index):
        return self.both[0, :, index, :]

    def top_line(self, index):
        block = iota((self.count, self.cols), 0)
        here = (1 ^ self.core ^ parity(block ^ self.me)) == 0
        return jnp.where(here, self.both[0, :, index, :], self.both[1, :, index, :])


def level_column(values, count, cols):
    level = iota((TALL, cols), 0)
    out = jnp.zeros((TALL, cols), F32)
    for k in range(count):
        out = jnp.where(level == k, values[k], out)
    return out


def position(n):
    me = lax.axis_index("ia")
    return me, lax.rem(me + n - 1, n), lax.rem(me + 1, n)


def sweep_levels(count, rows, th, fetch, west_of, east_of, u, v, pieces, top, depth, masks, emit):
    own, left, right, beside, beside_temp, beside_v = pieces
    east_depth, west_depth, north_depth, south_depth = masks
    cols = own.shape[1]
    lane = iota((rows, cols), 1)
    row = iota((rows, cols), 0)
    is_top = jnp.full((1, cols), top.astype(jnp.int32)) == 1
    for k in range(count):
        here = fetch(k)
        add = th[k] * own
        mid = here + jnp.where(depth > k, add, 0.0)
        bare = here + add
        u_west, t_west = west_of(k)
        west_value = t_west + th[k] * left
        east_value = jnp.where(
            lane == cols - 1, east_of(k) + th[k] * right, pltpu.roll(bare, cols - 1, 1)
        )
        u_here = u[k * rows : (k + 1) * rows, :]
        v_here = v[k * rows : (k + 1) * rows, :]
        flux_east = jnp.where(east_depth > k, 0.25 * u_here * (east_value - bare), 0.0)
        flux_first = jnp.where(west_depth > k, 0.25 * u_west * (bare - west_value), 0.0)
        flux_west = jnp.where(lane == 0, flux_first, pltpu.roll(flux_east, 1, 1))
        beside_value = beside_temp(k) + th[k] * beside
        above = jnp.where(is_top, 0.0, beside_value)
        north_value = jnp.where(row == rows - 1, above, pltpu.roll(bare, rows - 1, 0))
        flux_north = jnp.where(north_depth > k, 0.25 * v_here * (north_value - bare), 0.0)
        flux_below = jnp.where(south_depth > k, 0.25 * beside_v(k) * (bare[:1] - beside_value), 0.0)
        flux_south = jnp.where(row == 0, flux_below, pltpu.roll(flux_north, 1, 0))
        emit(k, mid + flux_east + flux_west + flux_north + flux_south)


def face_depths(depth, edge_left, edge_right, beside_depth, count, top):
    rows, cols = depth.shape
    lane = iota(depth.shape, 1)
    row = iota(depth.shape, 0)
    is_top = jnp.full(depth.shape, top.astype(jnp.int32)) == 1
    right = edge_right[:, 4 * count + 1 : 4 * count + 2]
    east = jnp.minimum(depth, jnp.where(lane == cols - 1, right, pltpu.roll(depth, cols - 1, 1)))
    west = jnp.minimum(depth, edge_left[:, 4 * count : 4 * count + 1])
    above = jnp.where(is_top, depth, beside_depth)
    north = jnp.minimum(depth, jnp.where(row == rows - 1, above, pltpu.roll(depth, rows - 1, 0)))
    south = jnp.where(is_top[:1], jnp.minimum(depth[:1], beside_depth), 0.0)
    return east, west, north, south


def load_pieces(solved, me, west, east, rows, top):
    cols = solved.shape[-1]
    here = pl.ds(pl.multiple_of(jnp.where(top, rows, 0), 8), rows)
    own = solved[me, here, :]
    left = pltpu.roll(solved[west, here, :], 1, 1)
    right = pltpu.roll(solved[east, here, :], cols - 1, 1)
    is_top = jnp.full((1, cols), top.astype(jnp.int32)) == 1
    block = solved[me]
    beside = jnp.where(is_top, block[rows - 1 : rows], block[rows : rows + 1])
    return own, left, right, beside


def first_kernel(cp, th, both, beyond, adj, u, v, lev, t_out, out, peer, kept, solved, rowbuf, tall):
    rows, cols = lev.shape
    count = adj.shape[0] // rows
    top = lax.axis_index("ja") == lax.axis_size("ja") - 1
    sent = Messages(both)
    own_core = lax.axis_index("ja")
    me, west, east = position(sent.count)
    partner = sent.line(PART1).astype(jnp.int32)
    block, lane = split_index(partner, cols)
    solved[...] = surface_solve(sent.field(rows), block, lane)
    fold_depth = sent.top_line(LEV1)
    rowbuf[...] = fold_take(fold_depth, block, lane)
    across_depth = rowbuf[pl.ds(me, 1), :]
    rowbuf[...] = fold_depth
    fold_depth = rowbuf[pl.ds(me, 1), :]

    is_top = jnp.full((count, cols), top.astype(jnp.int32)) == 1
    level = iota((TALL, cols), 0).astype(F32)
    tall[0, 0:count, :] = jnp.where(
        is_top, level_rows(v.at[1], rows - 1, count, rows), beyond[count : 2 * count, :]
    )
    tall[1, 0:count, :] = jnp.where(
        is_top, level_rows(adj, rows - 1, count, rows), beyond[3 * count : 4 * count, :]
    )
    fold_solved = solved[me, 2 * rows - 8 :, :][7:]
    flux = jnp.where(
        fold_depth > level,
        0.25 * tall[0] * (tall[1] + level_column(th, count, cols) * fold_solved),
        0.0,
    )
    into = jnp.where(across_depth > level, level_column(cp, count, cols) * flux, 0.0)
    kept[0:TALL, :] = flux
    kept[TALL:, :] = jnp.broadcast_to(across_depth, (8, cols))
    out[HROW2 : HROW2 + 1, :] = jnp.sum(into, axis=0, keepdims=True)

    depth = lev[...].astype(F32)
    edge_left = sent.part(west, own_core, EDGE1, EDGE1 + rows)
    edge_right = sent.part(east, own_core, EDGE1, EDGE1 + rows)
    beside_depth = beyond[4 * count : 4 * count + 1, :]
    masks = face_depths(depth, edge_left, edge_right, beside_depth, count, top)
    own, left, right, beside = load_pieces(solved, me, west, east, rows, top)
    pieces = (
        own,
        left,
        right,
        beside,
        lambda k: beyond[k : k + 1, :],
        lambda k: beyond[count + k : count + k + 1, :],
    )
    spot = iota((rows, cols), 1)
    carry = {"forcing": own, "edge": jnp.zeros((rows, cols), F32)}

    def emit(k, value):
        t_out[k * rows : (k + 1) * rows, :] = value
        carry["forcing"] = carry["forcing"] + cp[k] * jnp.where(depth > k, value, 0.0)
        edge = jnp.where(spot == k, value[:, cols - 1 :], carry["edge"])
        carry["edge"] = jnp.where(spot == count + k, value[:, :1], edge)

    sweep_levels(
        count,
        rows,
        th,
        lambda k: adj[k * rows : (k + 1) * rows, :],
        lambda k: (edge_left[:, count + k : count + k + 1], edge_left[:, k : k + 1]),
        lambda k: edge_right[:, 3 * count + k : 3 * count + k + 1],
        u.at[1],
        v.at[1],
        pieces,
        top,
        depth,
        masks,
        emit,
    )
    out[0:rows, :] = carry["forcing"]
    half = rows // 2
    edge = carry["edge"]
    out[EDGE2 : EDGE2 + half, :] = jnp.where(
        spot[:half] < cols // 2, edge[:half], pltpu.roll(edge[half:], cols // 2, 1)
    )
    last_row = level_rows(t_out, rows - 1, count, rows)
    out[LINE2 : LINE2 + count, :] = jnp.where(is_top, last_row, beyond[2 * count : 3 * count, :])
    later, share = count // 2, count - count // 2
    out[FLUX2 : FLUX2 + share, :] = jnp.where(
        is_top[:share], kept[later:count, :], kept[0:share, :]
    )
    out[FLUX2 + share :, :] = jnp.zeros((ROWS2 - FLUX2 - share, cols), F32)
    peer[0:count, :] = jnp.where(is_top, level_rows(t_out, 0, count, rows), last_row)
    peer[count:, :] = jnp.zeros((peer.shape[0] - count, cols), F32)


def second_kernel(
    th, both, beyond, both1, beyond1, kept, temp, u, v, lev, t_out, s_out, solved, rowbuf, tall
):
    rows, cols = lev.shape
    count = temp.shape[0] // rows
    top = lax.axis_index("ja") == lax.axis_size("ja") - 1
    sent, sent1 = Messages(both), Messages(both1)
    own_core = lax.axis_index("ja")
    n = sent.count
    me, west, east = position(n)
    partner = sent1.line(PART1).astype(jnp.int32)
    block, lane = split_index(partner, cols)
    forcing = sent.field(rows)
    fold = fold_take(sent.line(HROW2), block, lane)
    row3 = iota(forcing.shape, 1)
    forcing = forcing - jnp.where(row3 == 2 * rows - 1, fold[:, None, :], 0.0)
    iterate = surface_solve(forcing, block, lane)
    solved[...] = iterate
    rowbuf[...] = fold_take(iterate[:, 2 * rows - 1, :], block, lane)
    across_solved = rowbuf[pl.ds(me, 1), :]

    spot = iota((1, cols), 1)
    rowbuf[...] = sent1.line(PART1)
    beside_left = pltpu.roll(rowbuf[pl.ds(west, 1), :], 1, 1)
    beside_right = pltpu.roll(rowbuf[pl.ds(east, 1), :], cols - 1, 1)
    end_partner = jnp.where(spot == 0, beside_left, beside_right)
    end_partner = jnp.where((spot == 0) | (spot == cols - 1), end_partner, 0.0)
    own_partner = jnp.broadcast_to(rowbuf[pl.ds(me, 1), :], (TALL, cols)).astype(jnp.int32)
    end_partner = jnp.broadcast_to(end_partner, (WINDOW, cols)).astype(jnp.int32)
    own_block, own_lane = split_index(own_partner, cols)
    end_block, end_lane = split_index(end_partner, cols)
    zero, low = jnp.zeros((TALL, cols), F32), jnp.zeros((WINDOW, cols), F32)
    temp_across, v_across = zero, zero
    own_flux, end_flux = [low, low], [low, low]
    for b in range(n):
        here, there = own_block == b, end_block == b
        line = sent.part(b, 1, LINE2, LINE2 + TALL)
        temp_across = jnp.where(here, jnp.take_along_axis(line, own_lane, axis=1), temp_across)
        line = sent.part(b, 0, LINE2, LINE2 + TALL)
        v_across = jnp.where(here, jnp.take_along_axis(line, own_lane, axis=1), v_across)
        for c in range(2):
            line = sent.part(b, c, ROWS2 - WINDOW, ROWS2)
            moved = jnp.take_along_axis(line, own_lane[:WINDOW], axis=1)
            own_flux[c] = jnp.where(here[:WINDOW], moved, own_flux[c])
            moved = jnp.take_along_axis(line, end_lane, axis=1)
            end_flux[c] = jnp.where(there, moved, end_flux[c])
    skip = FLUX2 - (ROWS2 - WINDOW)
    later, share = count // 2, count - count // 2
    for i, parts in enumerate((own_flux, end_flux)):
        for c, start in ((0, 0), (1, later)):
            tall[2, 0:WINDOW, :] = parts[c]
            tall[i, start : start + share, :] = tall[2, skip : skip + share, :]
    level = iota((TALL, cols), 0).astype(F32)
    fold_last = jnp.where(
        kept[TALL : TALL + 1, :] > level,
        0.25
        * v_across
        * (temp_across - kept[0:TALL, :] + level_column(th, count, cols) * across_solved),
        0.0,
    )
    tall[2] = fold_last

    depth = lev[...].astype(F32)
    edge1_left = sent1.part(west, own_core, EDGE1, EDGE1 + rows)
    edge1_right = sent1.part(east, own_core, EDGE1, EDGE1 + rows)
    half = rows // 2

    def both_rows(line):
        return jnp.concatenate([line, pltpu.roll(line, cols // 2, 1)], axis=0)

    edge_left = both_rows(sent.part(west, own_core, EDGE2, EDGE2 + half))
    edge_right = both_rows(sent.part(east, own_core, EDGE2, EDGE2 + half))
    beside_depth = beyond1[4 * count : 4 * count + 1, :]
    masks = face_depths(depth, edge1_left, edge1_right, beside_depth, count, top)
    own, left, right, beside = load_pieces(solved, me, west, east, rows, top)
    s_out[...] = own
    pieces = (
        own,
        left,
        right,
        beside,
        lambda k: beyond[k : k + 1, :],
        lambda k: beyond1[2 * count + k : 2 * count + k + 1, :],
    )
    row = iota((rows, cols), 0)
    on_fold = (row == rows - 1) & (jnp.full((rows, cols), top.astype(jnp.int32)) == 1)

    def less(value, index, k):
        return value - jnp.where(on_fold, tall[index, k : k + 1, :], 0.0)

    def emit(k, value):
        t_out[k * rows : (k + 1) * rows, :] = less(value, 2, k)

    def spread(column):
        return jnp.broadcast_to(column, (rows, cols))

    sweep_levels(
        count,
        rows,
        th,
        lambda k: less(temp[k * rows : (k + 1) * rows, :], 0, k),
        lambda k: (
            edge1_left[:, 2 * count + k : 2 * count + k + 1],
            less(spread(edge_left[:, k : k + 1]), 1, k),
        ),
        lambda k: less(spread(edge_right[:, count + k : count + k + 1]), 1, k),
        u.at[0],
        v.at[0],
        pieces,
        top,
        depth,
        masks,
        emit,
    )


def exchange(block, peer):
    n = lax.axis_size("ia")
    me = lax.axis_index("ia")
    rows, cols = block.shape
    y = block
    dim = 0
    step = n // 2
    while step:
        pairs = [(2 * i + c, 2 * (i ^ step) + (1 - c)) for i in range(n) for c in range(2)]
        z = lax.ppermute(y, ("ia", "ja"), pairs)
        odd = (me // step) % 2 == 1
        y = jnp.where(odd, jnp.stack([z, y], axis=dim), jnp.stack([y, z], axis=dim))
        dim += 1
        step //= 2
    y = y.reshape(n * rows, cols)
    z = lax.ppermute(jnp.concatenate([y, peer]), "ja", [(0, 1), (1, 0)])
    both = jnp.stack([y, z[: n * rows]]).reshape(2, n, rows, cols)
    return both, z[n * rows :]


def on_device(
    adjoint_temp, adjoint_surface, trajectory_u, trajectory_v, levels, partner, thickness, coupling
):
    steps, count, rows, cols = trajectory_u.shape
    n = lax.axis_size("ia")
    flat = count * rows
    adj = adjoint_temp.reshape(flat, cols)
    u = trajectory_u.reshape(steps, flat, cols)
    v = trajectory_v.reshape(steps, flat, cols)
    par = partner.reshape(1, cols)
    smem = pl.BlockSpec(memory_space=pltpu.SMEM)
    vmem = pl.BlockSpec(memory_space=pltpu.VMEM)

    def shape(*dims):
        return jax.ShapeDtypeStruct(dims, F32)

    small = pltpu.CompilerParams(vmem_limit_bytes=(8 + n // 2) * 2**20)
    out, peer = pl.pallas_call(
        pack_kernel,
        out_shape=(shape(ROWS1, cols), shape(PEER1, cols)),
        in_specs=[smem] + [vmem] * 6,
        out_specs=(vmem, vmem),
    )(coupling, adj, adjoint_surface, u, v, levels, par)
    both1, beyond1 = exchange(out, peer)
    temp, out, peer, kept = pl.pallas_call(
        first_kernel,
        out_shape=(
            shape(flat, cols),
            shape(ROWS2, cols),
            shape(PEER2, cols),
            shape(TALL + 8, cols),
        ),
        in_specs=[smem, smem] + [vmem] * 6,
        out_specs=(vmem,) * 4,
        scratch_shapes=[
            pltpu.VMEM((n, 2 * rows, cols), F32),
            pltpu.VMEM((n, cols), F32),
            pltpu.VMEM((2, TALL, cols), F32),
        ],
        compiler_params=small,
    )(coupling, thickness, both1, beyond1, adj, u, v, levels)
    both, beyond = exchange(out, peer)
    temp_gradient, surface_gradient = pl.pallas_call(
        second_kernel,
        out_shape=(shape(flat, cols), shape(rows, cols)),
        in_specs=[smem] + [vmem] * 9,
        out_specs=(vmem, vmem),
        scratch_shapes=[
            pltpu.VMEM((n, 2 * rows, cols), F32),
            pltpu.VMEM((n, cols), F32),
            pltpu.VMEM((3, TALL, cols), F32),
        ],
        compiler_params=small,
    )(thickness, both, beyond, both1, beyond1, kept, temp, u, v, levels)
    return temp_gradient.reshape(count, rows, cols), surface_gradient


def solution(mesh):
    return jax.shard_map(
        on_device,
        mesh=mesh,
        in_specs=(
            P("grp", "ja", "ia"),
            P(("grp", "ja"), "ia"),
            P(None, None, "ja", "ia"),
            P(None, None, "ja", "ia"),
            P("ja", "ia"),
            P("ia"),
            P(),
            P(),
        ),
        out_specs=(P("grp", "ja", "ia"), P(("grp", "ja"), "ia")),
        check_vma=False,
    )
```

time: 48.7 us -> 41.1 us (0.84)
  waiting for transfers between devices: 21 us -> 16.7 us
  Pallas kernels: 9.02 us -> 6.89 us
  local copies, waits for them, and re-layouts: 2.9 us -> 1.94 us
  other arithmetic: 1.07 us -> 0.21 us
  starting transfers between devices: 13.5 us -> 14.3 us
    ppermute x8, waiting for transfers between devices: 21 us -> 16.7 us  [the longest x6 14.1 us: exchange(): z = lax.ppermute(y, ('ia', 'ja'), pairs)]
    pallas_call x1, Pallas kernels: 3.34 us -> 1.98 us  [on_device(): pl.pallas_call(first_kernel, out_shape=(shape(flat, cols), shape(ROWS2, c...]
    unnamed x16, local copies, waits for them, and re-layouts: 2.84 us -> 1.87 us
    select_n x10, other arithmetic: 1.05 us -> 0.12 us  [exchange(): y = jnp.where(odd, jnp.stack([z, y], axis=dim), jnp.stack([y, z], axis=dim))]
    ppermute x8, starting transfers between devices: 13.5 us -> 14.3 us  [the longest x6 13.8 us: exchange(): z = lax.ppermute(y, ('ia', 'ja'), pairs)]
    pallas_call x1, Pallas kernels: 3.45 us -> 2.68 us  [on_device(): pl.pallas_call(second_kernel, out_shape=(shape(flat, cols), shape(rows, c...]
where the time goes in v2:
time: 41.1 us; the launch traced here: 40.8 us
  waiting for transfers between devices  16.7 us (41%)
  starting transfers between devices  14.3 us (35%)
  Pallas kernels  6.89 us (17%)
  local copies, waits for them, and re-layouts  1.94 us (5%)
  between operations  0.79 us (2%)
    ppermute x6, waiting for transfers between devices, exchange(): z = lax.ppermute(y, ('ia', 'ja'), pairs)  14.1 us
    ppermute x6, starting transfers between devices, exchange(): z = lax.ppermute(y, ('ia', 'ja'), pairs)  13.8 us
    pallas_call x1, Pallas kernels, on_device(): pl.pallas_call(second_kernel, out_shape=(shape(flat, cols), shape(rows, c...  2.68 us
    ppermute x2, waiting for transfers between devices, exchange(): z = lax.ppermute(jnp.concatenate([y, peer]), 'ja', [(0, 1), (1, 0)])  2.6 us
    pallas_call x1, Pallas kernels, on_device(): pl.pallas_call(pack_kernel, out_shape=(shape(ROWS1, cols), shape(PEER1, c...  2.23 us
    pallas_call x1, Pallas kernels, on_device(): pl.pallas_call(first_kernel, out_shape=(shape(flat, cols), shape(ROWS2, c...  1.98 us
    unnamed x16, local copies, waits for them, and re-layouts  1.87 us
  transfers between devices with their start and end apart: 8, of which 8 were waited for; matrix products, arithmetic and copies ran while one was open for 0% of the time, Pallas kernels for 0%

profile of v2, /device:TPU:0, one launch (start us, length us, event | category | flops | bytes accessed | tf_op | source)
XLA Modules:
  0.0 40.8 jit_solution(11120905080410802359)
XLA Ops:
  0.6 2.2 %shard_map.95 = (f32[40,128]{1,0:T(8,128)}, f32[104,128]{1,0:T(8,128)}) custom-call(f32[25]{0:T(128)} %cp.3, f32[400,128]{1,0:T(8,128)} %bitcast.39, f32[16,128]{1,0:T(8,128)} %surf.1, f32[2,400,128]{2,1,0:T(8,128)} %bitcast.33, f32[2,400,128]{2,1,0:T(8,128)} %bitcast.36, s32[16,128]{1,0:T(8,128)} %lev.5, s32[1,128]{1,0:T(1,128)} %bitcast.61), custom_call_target="tpu_custom_call" | custom-call | tf_op jit(solution)/shard_map/pallas_call | solution.py:462
  2.9 3.5 %collective-permute-start = (f32[40,128]{1,0:T(8,128)}, f32[40,128]{1,0:T(8,128)S(1)}, u32[]{:S(2)}, u32[]{:S(2)}) collective-permute-start(f32[40,128]{1,0:T(8,128)} %get-tuple-element.10), channel_id=1, source_target_pairs={{0,9},{1,8},{2,11},{3,10},{4,13},{5,12},{6,15},{7,14},{8,1},{9,0},... | collective-permute-start | bytes 61448 | tf_op jit(solution)/shard_map/ppermute | solution.py:434
  6.3 1.7 %collective-permute-done = f32[40,128]{1,0:T(8,128)S(1)} collective-permute-done((f32[40,128]{1,0:T(8,128)}, f32[40,128]{1,0:T(8,128)S(1)}, u32[]{:S(2)}, u32[]{:S(2)}) %collective-permute-start) | collective-permute-done | bytes 20512 | tf_op jit(solution)/shard_map/ppermute | solution.py:434
  8.1 1.9 %collective-permute-start.1 = (f32[2,40,128]{2,1,0:T(8,128)S(1)}, f32[2,40,128]{2,1,0:T(8,128)S(1)}, u32[]{:S(2)}, u32[]{:S(2)}) collective-permute-start(f32[2,40,128]{2,1,0:T(8,128)S(1)} %maximum_select_fusion.8), channel_id=1, source_target_pairs={{0,5},{1,4},{2,7},{3,6},{4,1},{5,0},{6,3},{7,2},{8,13},{9,12},{10,... | collective-permute-start | bytes 122888 | tf_op jit(solution)/shard_map/ppermute | solution.py:434
  10.0 1.7 %collective-permute-done.1 = f32[2,40,128]{2,1,0:T(8,128)S(1)} collective-permute-done((f32[2,40,128]{2,1,0:T(8,128)S(1)}, f32[2,40,128]{2,1,0:T(8,128)S(1)}, u32[]{:S(2)}, u32[]{:S(2)}) %collective-permute-start.1) | collective-permute-done | bytes 40992 | tf_op jit(solution)/shard_map/ppermute | solution.py:434
  11.7 1.9 %collective-permute-start.2 = (f32[2,2,40,128]{3,2,0,1:T(8,128)S(1)}, f32[2,2,40,128]{3,2,0,1:T(8,128)S(1)}, u32[]{:S(2)}, u32[]{:S(2)}) collective-permute-start(f32[2,2,40,128]{3,2,0,1:T(8,128)S(1)} %maximum_select_fusion.4), channel_id=1, source_target_pairs={{0,3},{1,2},{2,1},{3,0},{4,7},{5,6},{6,5},{7,4},{8,11},{9,10},{10,... | collective-permute-start | bytes 245768 | tf_op jit(solution)/shard_map/ppermute | solution.py:434
  13.6 2.5 %collective-permute-done.2 = f32[2,2,40,128]{3,2,0,1:T(8,128)S(1)} collective-permute-done((f32[2,2,40,128]{3,2,0,1:T(8,128)S(1)}, f32[2,2,40,128]{3,2,0,1:T(8,128)S(1)}, u32[]{:S(2)}, u32[]{:S(2)}) %collective-permute-start.2) | collective-permute-done | bytes 81952 | tf_op jit(solution)/shard_map/ppermute | solution.py:434
  16.2 0.8 %copy-done.7 = f32[104,128]{1,0:T(8,128)S(1)} copy-done((f32[104,128]{1,0:T(8,128)S(1)}, f32[104,128]{1,0:T(8,128)}, u32[]{:S(2)}) %copy-start.7) | copy-done | bytes 53272
  16.9 0.3 collective-permute-start.3
  17.3 1.2 %collective-permute-done.3 = f32[424,128]{1,0:T(8,128)S(1)} collective-permute-done((f32[424,128]{1,0:T(8,128)S(1)}, f32[424,128]{1,0:T(8,128)S(1)}, u32[]{:S(2)}, u32[]{:S(2)}) %collective-permute-start.3) | collective-permute-done | bytes 217120 | tf_op jit(solution)/shard_map/ppermute | solution.py:440
  18.5 0.0 copy-start.2
  18.6 0.9 %copy-done.1 = f32[2,25,16,128]{3,2,1,0:T(8,128)S(1)} copy-done((f32[2,25,16,128]{3,2,1,0:T(8,128)S(1)}, f32[2,25,16,128]{3,2,1,0:T(8,128)}, u32[]{:S(2)}) %copy-start.1) | copy-done | bytes 409624
  19.5 0.1 copy-done
  19.6 0.1 copy-done.2
  19.7 2.0 %shard_map.96 = (f32[400,128]{1,0:T(8,128)S(1)}, f32[64,128]{1,0:T(8,128)S(1)}, f32[32,128]{1,0:T(8,128)S(1)}, f32[40,128]{1,0:T(8,128)S(1)}) custom-call(f32[25]{0:T(128)S(1)} %copy-done.4, f32[25]{0:T(128)S(1)} %copy-done.5, f32[2,8,40,128]{3,2,1,0:T(8,128)S(1)} %pad_maximum_fusion.1.both.both1, f32[104,128]{1,0:T(8,128)S(1)} %slice.17.beyond.beyond1, ...), custom_call_target="tpu_custom_call" | custom-call | tf_op jit(solution)/shard_map/pallas_call | solution.py:469
  21.7 3.1 %collective-permute-start.4 = (f32[64,128]{1,0:T(8,128)S(1)}, f32[64,128]{1,0:T(8,128)S(1)}, u32[]{:S(2)}, u32[]{:S(2)}) collective-permute-start(f32[64,128]{1,0:T(8,128)S(1)} %get-tuple-element.12), channel_id=1, source_target_pairs={{0,9},{1,8},{2,11},{3,10},{4,13},{5,12},{6,15},{7,14},{8,1},{9,0},... | collective-permute-start | bytes 98312 | tf_op jit(solution)/shard_map/ppermute | solution.py:434
  24.8 1.6 %collective-permute-done.4 = f32[64,128]{1,0:T(8,128)S(1)} collective-permute-done((f32[64,128]{1,0:T(8,128)S(1)}, f32[64,128]{1,0:T(8,128)S(1)}, u32[]{:S(2)}, u32[]{:S(2)}) %collective-permute-start.4) | collective-permute-done | bytes 32800 | tf_op jit(solution)/shard_map/ppermute | solution.py:434
  26.4 2.1 %collective-permute-start.5 = (f32[2,64,128]{2,1,0:T(8,128)S(1)}, f32[2,64,128]{2,1,0:T(8,128)S(1)}, u32[]{:S(2)}, u32[]{:S(2)}) collective-permute-start(f32[2,64,128]{2,1,0:T(8,128)S(1)} %maximum_select_fusion.6), channel_id=1, source_target_pairs={{0,5},{1,4},{2,7},{3,6},{4,1},{5,0},{6,3},{7,2},{8,13},{9,12},{10,... | collective-permute-start | bytes 196616 | tf_op jit(solution)/shard_map/ppermute | solution.py:434
  28.5 2.3 %collective-permute-done.5 = f32[2,64,128]{2,1,0:T(8,128)S(1)} collective-permute-done((f32[2,64,128]{2,1,0:T(8,128)S(1)}, f32[2,64,128]{2,1,0:T(8,128)S(1)}, u32[]{:S(2)}, u32[]{:S(2)}) %collective-permute-start.5) | collective-permute-done | bytes 65568 | tf_op jit(solution)/shard_map/ppermute | solution.py:434
  30.8 1.3 %collective-permute-start.6 = (f32[2,2,64,128]{3,2,0,1:T(8,128)S(1)}, f32[2,2,64,128]{3,2,0,1:T(8,128)S(1)}, u32[]{:S(2)}, u32[]{:S(2)}) collective-permute-start(f32[2,2,64,128]{3,2,0,1:T(8,128)S(1)} %maximum_select_fusion.2), channel_id=1, source_target_pairs={{0,3},{1,2},{2,1},{3,0},{4,7},{5,6},{6,5},{7,4},{8,11},{9,10},{10,... | collective-permute-start | bytes 393224 | tf_op jit(solution)/shard_map/ppermute | solution.py:434
  32.1 4.2 %collective-permute-done.6 = f32[2,2,64,128]{3,2,0,1:T(8,128)S(1)} collective-permute-done((f32[2,2,64,128]{3,2,0,1:T(8,128)S(1)}, f32[2,2,64,128]{3,2,0,1:T(8,128)S(1)}, u32[]{:S(2)}, u32[]{:S(2)}) %collective-permute-start.6) | collective-permute-done | bytes 131104 | tf_op jit(solution)/shard_map/ppermute | solution.py:434
  36.5 0.2 collective-permute-start.7
  36.7 1.4 %collective-permute-done.7 = f32[544,128]{1,0:T(8,128)S(1)} collective-permute-done((f32[544,128]{1,0:T(8,128)S(1)}, f32[544,128]{1,0:T(8,128)S(1)}, u32[]{:S(2)}, u32[]{:S(2)}) %collective-permute-start.7) | collective-permute-done | bytes 278560 | tf_op jit(solution)/shard_map/ppermute | solution.py:440
  38.2 2.7 %shard_map.97 = (f32[400,128]{1,0:T(8,128)}, f32[16,128]{1,0:T(8,128)}) custom-call(f32[25]{0:T(128)S(1)} %copy-done.5, f32[2,8,64,128]{3,2,1,0:T(8,128)S(1)} %pad_maximum_fusion.both, f32[32,128]{1,0:T(8,128)S(1)} %slice.19.beyond, f32[2,8,40,128]{3,2,1,0:T(8,128)S(1)} %pad_maximum_fusion.1.both.both1, f32[104,128]{1,0:T(8,128)S(1)} %slice.17.beyond.beyond1, ...), custom_call_target="tpu_custom_call" | custom-call | tf_op jit(solution)/shard_map/pallas_call | solution.py:487
  (31 shorter events, 0.3 us)
Async XLA Ops:
  2.9 5.2 %collective-permute-start = (f32[40,128]{1,0:T(8,128)}, f32[40,128]{1,0:T(8,128)S(1)}, u32[]{:S(2)}, u32[]{:S(2)}) collective-permute-start(f32[40,128]{1,0:T(8,128)} %get-tuple-element.10), channel_id=1, source_target_pairs={{0,9},{1,8},{2,11},{3,10},{4,13},{5,12},{6,15},{7,14},{8,1},{9,0},... | collective-permute-start | bytes 61448 | tf_op jit(solution)/shard_map/ppermute | solution.py:434
  6.3 1.7 %copy-start.6 = (f32[40,128]{1,0:T(8,128)S(1)}, f32[40,128]{1,0:T(8,128)}, u32[]{:S(2)}) copy-start(f32[40,128]{1,0:T(8,128)} %get-tuple-element.10) | copy-start | bytes 61444
  8.1 3.6 %collective-permute-start.1 = (f32[2,40,128]{2,1,0:T(8,128)S(1)}, f32[2,40,128]{2,1,0:T(8,128)S(1)}, u32[]{:S(2)}, u32[]{:S(2)}) collective-permute-start(f32[2,40,128]{2,1,0:T(8,128)S(1)} %maximum_select_fusion.8), channel_id=1, source_target_pairs={{0,5},{1,4},{2,7},{3,6},{4,1},{5,0},{6,3},{7,2},{8,13},{9,12},{10,... | collective-permute-start | bytes 122888 | tf_op jit(solution)/shard_map/ppermute | solution.py:434
  11.7 4.4 %collective-permute-start.2 = (f32[2,2,40,128]{3,2,0,1:T(8,128)S(1)}, f32[2,2,40,128]{3,2,0,1:T(8,128)S(1)}, u32[]{:S(2)}, u32[]{:S(2)}) collective-permute-start(f32[2,2,40,128]{3,2,0,1:T(8,128)S(1)} %maximum_select_fusion.4), channel_id=1, source_target_pairs={{0,3},{1,2},{2,1},{3,0},{4,7},{5,6},{6,5},{7,4},{8,11},{9,10},{10,... | collective-permute-start | bytes 245768 | tf_op jit(solution)/shard_map/ppermute | solution.py:434
  16.1 0.8 %copy-start.7 = (f32[104,128]{1,0:T(8,128)S(1)}, f32[104,128]{1,0:T(8,128)}, u32[]{:S(2)}) copy-start(f32[104,128]{1,0:T(8,128)} %get-tuple-element.11) | copy-start | bytes 159748
  16.9 1.5 %collective-permute-start.3 = (f32[424,128]{1,0:T(8,128)S(1)}, f32[424,128]{1,0:T(8,128)S(1)}, u32[]{:S(2)}, u32[]{:S(2)}) collective-permute-start(f32[424,128]{1,0:T(8,128)S(1)} %pad_maximum_fusion.3), channel_id=1, source_target_pairs={{0,1},{1,0},{2,3},{3,2},{4,5},{5,4},{6,7},{7,6},{8,9},{9,8},{10,11... | collective-permute-start | bytes 651272 | tf_op jit(solution)/shard_map/ppermute | solution.py:440
  18.5 1.0 %copy-start.1 = (f32[2,25,16,128]{3,2,1,0:T(8,128)S(1)}, f32[2,25,16,128]{3,2,1,0:T(8,128)}, u32[]{:S(2)}) copy-start(f32[2,25,16,128]{3,2,1,0:T(8,128)} %param.11) | copy-start | bytes 1228804
  18.5 1.1 %copy-start = (f32[2,25,16,128]{3,2,1,0:T(8,128)S(1)}, f32[2,25,16,128]{3,2,1,0:T(8,128)}, u32[]{:S(2)}) copy-start(f32[2,25,16,128]{3,2,1,0:T(8,128)} %param.10) | copy-start | bytes 1228804
  18.5 1.2 %copy-start.2 = (f32[25,16,128]{2,1,0:T(8,128)S(1)}, f32[25,16,128]{2,1,0:T(8,128)}, u32[]{:S(2)}) copy-start(f32[25,16,128]{2,1,0:T(8,128)} %param.8) | copy-start | bytes 614404
  18.6 1.1 %copy-start.3 = (s32[16,128]{1,0:T(8,128)S(1)}, s32[16,128]{1,0:T(8,128)}, u32[]{:S(2)}) copy-start(s32[16,128]{1,0:T(8,128)} %lev.5) | copy-start | bytes 24580
  18.6 1.1 %copy-start.4 = (f32[25]{0:T(128)S(1)}, f32[25]{0:T(128)}, u32[]{:S(2)}) copy-start(f32[25]{0:T(128)} %cp.3) | copy-start | bytes 304
  18.6 1.1 %copy-start.5 = (f32[25]{0:T(128)S(1)}, f32[25]{0:T(128)}, u32[]{:S(2)}) copy-start(f32[25]{0:T(128)} %th.3) | copy-start | bytes 304
  21.7 4.7 %collective-permute-start.4 = (f32[64,128]{1,0:T(8,128)S(1)}, f32[64,128]{1,0:T(8,128)S(1)}, u32[]{:S(2)}, u32[]{:S(2)}) collective-permute-start(f32[64,128]{1,0:T(8,128)S(1)} %get-tuple-element.12), channel_id=1, source_target_pairs={{0,9},{1,8},{2,11},{3,10},{4,13},{5,12},{6,15},{7,14},{8,1},{9,0},... | collective-permute-start | bytes 98312 | tf_op jit(solution)/shard_map/ppermute | solution.py:434
  26.4 4.4 %collective-permute-start.5 = (f32[2,64,128]{2,1,0:T(8,128)S(1)}, f32[2,64,128]{2,1,0:T(8,128)S(1)}, u32[]{:S(2)}, u32[]{:S(2)}) collective-permute-start(f32[2,64,128]{2,1,0:T(8,128)S(1)} %maximum_select_fusion.6), channel_id=1, source_target_pairs={{0,5},{1,4},{2,7},{3,6},{4,1},{5,0},{6,3},{7,2},{8,13},{9,12},{10,... | collective-permute-start | bytes 196616 | tf_op jit(solution)/shard_map/ppermute | solution.py:434
  30.8 5.5 %collective-permute-start.6 = (f32[2,2,64,128]{3,2,0,1:T(8,128)S(1)}, f32[2,2,64,128]{3,2,0,1:T(8,128)S(1)}, u32[]{:S(2)}, u32[]{:S(2)}) collective-permute-start(f32[2,2,64,128]{3,2,0,1:T(8,128)S(1)} %maximum_select_fusion.2), channel_id=1, source_target_pairs={{0,3},{1,2},{2,1},{3,0},{4,7},{5,6},{6,5},{7,4},{8,11},{9,10},{10,... | collective-permute-start | bytes 393224 | tf_op jit(solution)/shard_map/ppermute | solution.py:434
  36.5 1.6 %collective-permute-start.7 = (f32[544,128]{1,0:T(8,128)S(1)}, f32[544,128]{1,0:T(8,128)S(1)}, u32[]{:S(2)}, u32[]{:S(2)}) collective-permute-start(f32[544,128]{1,0:T(8,128)S(1)} %pad_maximum_fusion.2), channel_id=1, source_target_pairs={{0,1},{1,0},{2,3},{3,2},{4,5},{5,4},{6,7},{7,6},{8,9},{9,8},{10,11... | collective-permute-start | bytes 835592 | tf_op jit(solution)/shard_map/ppermute | solution.py:440

commit v3 on v2

--- a/solution.py
+++ b/solution.py
@@ -76,25 +76,46 @@
     return ref[pl.ds(base, count, stride=rows), :]
 
 
-def pack_kernel(cp, adj, surf, u, v, lev, par, out, peer):
+def start_all(pairs, sems):
+    copies = [pltpu.make_async_copy(src, dst, sems.at[i]) for i, (src, dst) in enumerate(pairs)]
+    for copy in copies:
+        copy.start()
+    return copies
+
+
+def pack_kernel(
+    cp_in, th_in, adj_in, surf_in, u_in, v_in, lev_in, par_in, out, peer, depth_out, cp_out, th_out,
+    cp, adj, surf, u, v, lev, par, sems
+):
+    copies = start_all(
+        ((cp_in, cp), (lev_in, lev), (surf_in, surf), (par_in, par), (adj_in, adj), (u_in, u), (v_in, v), (cp_in, cp_out), (th_in, th_out)),
+        sems,
+    )
+    for copy in copies[:5]:
+        copy.wait()
     rows, cols = surf.shape
     count = adj.shape[0] // rows
     top = lax.axis_index("ja") == lax.axis_size("ja") - 1
     lane = iota((rows, cols), 1)
     depth = lev[...].astype(F32)
+    depth_out[...] = depth
     forcing = surf[...]
-    last, first = cols - 1, 0
+    last = cols - 1
     edge = jnp.where(lane == 4 * count, depth[:, last:], 0.0)
     edge = jnp.where(lane == 4 * count + 1, depth[:, :1], edge)
     for k in range(count):
         here = adj[k * rows : (k + 1) * rows, :]
+        forcing = forcing + cp[k] * jnp.where(depth > k, here, 0.0)
+        edge = jnp.where(lane == k, here[:, last:], edge)
+        edge = jnp.where(lane == 3 * count + k, here[:, :1], edge)
+    copies[5].wait()
+    for k in range(count):
         u0 = u[0, k * rows : (k + 1) * rows, :]
         u1 = u[1, k * rows : (k + 1) * rows, :]
-        forcing = forcing + cp[k] * jnp.where(depth > k, here, 0.0)
-        edge = jnp.where(lane == k, here[:, last:], edge)
         edge = jnp.where(lane == count + k, u1[:, last:], edge)
         edge = jnp.where(lane == 2 * count + k, u0[:, last:], edge)
-        edge = jnp.where(lane == 3 * count + k, here[:, :1], edge)
+    for copy in copies[6:]:
+        copy.wait()
     out[0:rows, :] = forcing
     out[EDGE1 : EDGE1 + rows, :] = edge
     out[PART1:ROWS1, :] = jnp.zeros((ROWS1 - PART1, cols), F32)
@@ -111,24 +132,46 @@
 
 
 def parity(x):
-    for shift in (16, 8, 4, 2, 1):
+    for shift in (8, 4, 2, 1):
         x = x ^ (x >> shift)
     return x & 1
+
+
+def exchange_steps(n, kind):
+    steps = []
+    while n > 1:
+        n //= 2
+        steps.append(n)
+    return steps if kind == 0 else steps[:1] + steps[:0:-1]
+
+
+def slot_of(distance, n, kind):
+    out = 0
+    for r, step in enumerate(exchange_steps(n, kind)):
+        out = out | (((distance >> (step.bit_length() - 1)) & 1) << r)
+    return out
 
 
 class Messages:
     def __init__(self, both):
         self.both = both
         self.count = both.shape[1]
-        self.cols = both.shape[3]
         self.me = lax.axis_index("ia")
-        self.core = lax.axis_index("ja")
-
-    def place(self, block, core):
-        return core ^ self.core ^ parity(block ^ self.me)
+        self.kind = parity(self.me) ^ lax.axis_index("ja")
+        self.own = [slot_of(self.me, self.count, kind) for kind in range(2)]
 
     def part(self, block, core, start, stop):
-        return self.both[self.place(block, core), block, start:stop, :]
+        kind = parity(block) ^ core
+        slot = self.own[kind] ^ slot_of(block, self.count, kind)
+        return self.both[self.kind ^ kind, slot, start:stop, :]
+
+    def beside(self, block, start, stop):
+        kind = parity(block) ^ lax.axis_index("ja")
+        away = block ^ self.me
+        slot = jnp.where(
+            kind == 0, slot_of(away, self.count, 0), slot_of(away, self.count, 1)
+        )
+        return self.both[self.kind ^ kind, slot, start:stop, :]
 
     def field(self, rows):
         blocks = [
@@ -137,13 +180,10 @@
         ]
         return jnp.stack(blocks, axis=0)
 
-    def line(self, index):
-        return self.both[0, :, index, :]
-
-    def top_line(self, index):
-        block = iota((self.count, self.cols), 0)
-        here = (1 ^ self.core ^ parity(block ^ self.me)) == 0
-        return jnp.where(here, self.both[0, :, index, :], self.both[1, :, index, :])
+    def line(self, core, index, out):
+        for b in range(self.count):
+            out[b : b + 1, :] = self.part(b, core, index, index + 1)
+        return out[...]
 
 
 def level_column(values, count, cols):
@@ -216,26 +256,27 @@
     return own, left, right, beside
 
 
-def first_kernel(cp, th, both, beyond, adj, u, v, lev, t_out, out, peer, kept, solved, rowbuf, tall):
-    rows, cols = lev.shape
+def first_kernel(
+    cp, th, both, beyond, adj, u_in, v_in, depth_in, t_out, out, peer, kept, solved, rowbuf, tall
+):
+    u, v = u_in.at[1], v_in.at[1]
+    rows, cols = depth_in.shape
     count = adj.shape[0] // rows
     top = lax.axis_index("ja") == lax.axis_size("ja") - 1
     sent = Messages(both)
-    own_core = lax.axis_index("ja")
     me, west, east = position(sent.count)
-    partner = sent.line(PART1).astype(jnp.int32)
+    partner = sent.line(0, PART1, rowbuf).astype(jnp.int32)
     block, lane = split_index(partner, cols)
     solved[...] = surface_solve(sent.field(rows), block, lane)
-    fold_depth = sent.top_line(LEV1)
-    rowbuf[...] = fold_take(fold_depth, block, lane)
+    depths = sent.line(1, LEV1, rowbuf)
+    fold_depth = rowbuf[pl.ds(me, 1), :]
+    rowbuf[...] = fold_take(depths, block, lane)
     across_depth = rowbuf[pl.ds(me, 1), :]
-    rowbuf[...] = fold_depth
-    fold_depth = rowbuf[pl.ds(me, 1), :]
 
     is_top = jnp.full((count, cols), top.astype(jnp.int32)) == 1
     level = iota((TALL, cols), 0).astype(F32)
     tall[0, 0:count, :] = jnp.where(
-        is_top, level_rows(v.at[1], rows - 1, count, rows), beyond[count : 2 * count, :]
+        is_top, level_rows(v, rows - 1, count, rows), beyond[count : 2 * count, :]
     )
     tall[1, 0:count, :] = jnp.where(
         is_top, level_rows(adj, rows - 1, count, rows), beyond[3 * count : 4 * count, :]
@@ -251,9 +292,9 @@
     kept[TALL:, :] = jnp.broadcast_to(across_depth, (8, cols))
     out[HROW2 : HROW2 + 1, :] = jnp.sum(into, axis=0, keepdims=True)
 
-    depth = lev[...].astype(F32)
-    edge_left = sent.part(west, own_core, EDGE1, EDGE1 + rows)
-    edge_right = sent.part(east, own_core, EDGE1, EDGE1 + rows)
+    depth = depth_in[...]
+    edge_left = sent.beside(west, EDGE1, EDGE1 + rows)
+    edge_right = sent.beside(east, EDGE1, EDGE1 + rows)
     beside_depth = beyond[4 * count : 4 * count + 1, :]
     masks = face_depths(depth, edge_left, edge_right, beside_depth, count, top)
     own, left, right, beside = load_pieces(solved, me, west, east, rows, top)
@@ -281,8 +322,8 @@
         lambda k: adj[k * rows : (k + 1) * rows, :],
         lambda k: (edge_left[:, count + k : count + k + 1], edge_left[:, k : k + 1]),
         lambda k: edge_right[:, 3 * count + k : 3 * count + k + 1],
-        u.at[1],
-        v.at[1],
+        u,
+        v,
         pieces,
         top,
         depth,
@@ -307,19 +348,20 @@
 
 
 def second_kernel(
-    th, both, beyond, both1, beyond1, kept, temp, u, v, lev, t_out, s_out, solved, rowbuf, tall
+    th, both, beyond, both1, beyond1, kept, temp, u_in, v_in, depth_in, t_out, s_out, solved, rowbuf, tall
 ):
-    rows, cols = lev.shape
+    u, v = u_in.at[0], v_in.at[0]
+    rows, cols = depth_in.shape
     count = temp.shape[0] // rows
     top = lax.axis_index("ja") == lax.axis_size("ja") - 1
     sent, sent1 = Messages(both), Messages(both1)
-    own_core = lax.axis_index("ja")
     n = sent.count
     me, west, east = position(n)
-    partner = sent1.line(PART1).astype(jnp.int32)
+    partners = sent1.line(0, PART1, rowbuf)
+    partner = partners.astype(jnp.int32)
     block, lane = split_index(partner, cols)
     forcing = sent.field(rows)
-    fold = fold_take(sent.line(HROW2), block, lane)
+    fold = fold_take(sent.line(0, HROW2, rowbuf), block, lane)
     row3 = iota(forcing.shape, 1)
     forcing = forcing - jnp.where(row3 == 2 * rows - 1, fold[:, None, :], 0.0)
     iterate = surface_solve(forcing, block, lane)
@@ -328,7 +370,7 @@
     across_solved = rowbuf[pl.ds(me, 1), :]
 
     spot = iota((1, cols), 1)
-    rowbuf[...] = sent1.line(PART1)
+    rowbuf[...] = partners
     beside_left = pltpu.roll(rowbuf[pl.ds(west, 1), :], 1, 1)
     beside_right = pltpu.roll(rowbuf[pl.ds(east, 1), :], cols - 1, 1)
     end_partner = jnp.where(spot == 0, beside_left, beside_right)
@@ -368,16 +410,16 @@
     )
     tall[2] = fold_last
 
-    depth = lev[...].astype(F32)
-    edge1_left = sent1.part(west, own_core, EDGE1, EDGE1 + rows)
-    edge1_right = sent1.part(east, own_core, EDGE1, EDGE1 + rows)
+    depth = depth_in[...]
+    edge1_left = sent1.beside(west, EDGE1, EDGE1 + rows)
+    edge1_right = sent1.beside(east, EDGE1, EDGE1 + rows)
     half = rows // 2
 
     def both_rows(line):
         return jnp.concatenate([line, pltpu.roll(line, cols // 2, 1)], axis=0)
 
-    edge_left = both_rows(sent.part(west, own_core, EDGE2, EDGE2 + half))
-    edge_right = both_rows(sent.part(east, own_core, EDGE2, EDGE2 + half))
+    edge_left = both_rows(sent.beside(west, EDGE2, EDGE2 + half))
+    edge_right = both_rows(sent.beside(east, EDGE2, EDGE2 + half))
     beside_depth = beyond1[4 * count : 4 * count + 1, :]
     masks = face_depths(depth, edge1_left, edge1_right, beside_depth, count, top)
     own, left, right, beside = load_pieces(solved, me, west, east, rows, top)
@@ -412,8 +454,8 @@
             less(spread(edge_left[:, k : k + 1]), 1, k),
         ),
         lambda k: less(spread(edge_right[:, count + k : count + k + 1]), 1, k),
-        u.at[0],
-        v.at[0],
+        u,
+        v,
         pieces,
         top,
         depth,
@@ -424,21 +466,18 @@
 
 def exchange(block, peer):
     n = lax.axis_size("ia")
-    me = lax.axis_index("ia")
     rows, cols = block.shape
+    kinds = [exchange_steps(n, kind) for kind in range(2)]
     y = block
-    dim = 0
-    step = n // 2
-    while step:
-        pairs = [(2 * i + c, 2 * (i ^ step) + (1 - c)) for i in range(n) for c in range(2)]
-        z = lax.ppermute(y, ("ia", "ja"), pairs)
-        odd = (me // step) % 2 == 1
-        y = jnp.where(odd, jnp.stack([z, y], axis=dim), jnp.stack([y, z], axis=dim))
-        dim += 1
-        step //= 2
-    y = y.reshape(n * rows, cols)
+    for near, far in zip(*kinds):
+        pairs = []
+        for i in range(n):
+            for c in range(2):
+                step = far if parity(i) ^ c else near
+                pairs.append((2 * i + c, 2 * (i ^ step) + 1 - c))
+        y = jnp.concatenate([y, lax.ppermute(y, ("ia", "ja"), pairs)])
     z = lax.ppermute(jnp.concatenate([y, peer]), "ja", [(0, 1), (1, 0)])
-    both = jnp.stack([y, z[: n * rows]]).reshape(2, n, rows, cols)
+    both = jnp.concatenate([y, z[: n * rows]]).reshape(2, n, rows, cols)
     return both, z[n * rows :]
 
 
@@ -452,19 +491,41 @@
     u = trajectory_u.reshape(steps, flat, cols)
     v = trajectory_v.reshape(steps, flat, cols)
     par = partner.reshape(1, cols)
+
+    def stay(x):
+        return pltpu.with_memory_space_constraint(x, pltpu.HBM)
+
     smem = pl.BlockSpec(memory_space=pltpu.SMEM)
     vmem = pl.BlockSpec(memory_space=pltpu.VMEM)
+    hbm = pl.BlockSpec(memory_space=pltpu.HBM)
 
     def shape(*dims):
         return jax.ShapeDtypeStruct(dims, F32)
 
     small = pltpu.CompilerParams(vmem_limit_bytes=(8 + n // 2) * 2**20)
-    out, peer = pl.pallas_call(
+    out, peer, depth, cp, th = pl.pallas_call(
         pack_kernel,
-        out_shape=(shape(ROWS1, cols), shape(PEER1, cols)),
-        in_specs=[smem] + [vmem] * 6,
-        out_specs=(vmem, vmem),
-    )(coupling, adj, adjoint_surface, u, v, levels, par)
+        out_shape=(
+            shape(ROWS1, cols),
+            shape(PEER1, cols),
+            shape(rows, cols),
+            shape(count),
+            shape(count),
+        ),
+        in_specs=[hbm] * 8,
+        out_specs=(vmem,) * 5,
+        scratch_shapes=[
+            pltpu.SMEM((count,), F32),
+            pltpu.VMEM((flat, cols), F32),
+            pltpu.VMEM((rows, cols), F32),
+            pltpu.VMEM((steps, flat, cols), F32),
+            pltpu.VMEM((steps, flat, cols), F32),
+            pltpu.VMEM((rows, cols), jnp.int32),
+            pltpu.VMEM((1, cols), jnp.int32),
+            pltpu.SemaphoreType.DMA((9,)),
+        ],
+        compiler_params=small,
+    )(*(stay(x) for x in (coupling, thickness, adj, adjoint_surface, u, v, levels, par)))
     both1, beyond1 = exchange(out, peer)
     temp, out, peer, kept = pl.pallas_call(
         first_kernel,
@@ -474,7 +535,7 @@
             shape(PEER2, cols),
             shape(TALL + 8, cols),
         ),
-        in_specs=[smem, smem] + [vmem] * 6,
+        in_specs=[smem, smem, vmem, vmem, vmem, vmem, vmem, vmem],
         out_specs=(vmem,) * 4,
         scratch_shapes=[
             pltpu.VMEM((n, 2 * rows, cols), F32),
@@ -482,12 +543,12 @@
             pltpu.VMEM((2, TALL, cols), F32),
         ],
         compiler_params=small,
-    )(coupling, thickness, both1, beyond1, adj, u, v, levels)
+    )(cp, th, both1, beyond1, adj, u, v, depth)
     both, beyond = exchange(out, peer)
     temp_gradient, surface_gradient = pl.pallas_call(
         second_kernel,
         out_shape=(shape(flat, cols), shape(rows, cols)),
-        in_specs=[smem] + [vmem] * 9,
+        in_specs=[smem] + [vmem] * 6 + [vmem]*3,
         out_specs=(vmem, vmem),
         scratch_shapes=[
             pltpu.VMEM((n, 2 * rows, cols), F32),
@@ -495,7 +556,7 @@
             pltpu.VMEM((3, TALL, cols), F32),
         ],
         compiler_params=small,
-    )(thickness, both, beyond, both1, beyond1, kept, temp, u, v, levels)
+    )(th, both, beyond, both1, beyond1, kept, temp, u, v, depth)
     return temp_gradient.reshape(count, rows, cols), surface_gradient
 
 

time: 41.1 us -> 35.8 us (0.87)
  waiting for transfers between devices: 16.7 us -> 14.1 us
  local copies, waits for them, and re-layouts: 1.94 us -> 0.13 us
  Pallas kernels: 6.89 us -> 6.21 us
    ppermute x6, waiting for transfers between devices: 14.1 us -> 11.8 us  [exchange(): y = jnp.concatenate([y, lax.ppermute(y, ('ia', 'ja'), pairs)])]
    unnamed x16 -> x14, local copies, waits for them, and re-layouts: 1.87 us -> 0.08 us
    pallas_call x1, Pallas kernels: 2.23 us -> 1.49 us  [on_device(): pl.pallas_call(pack_kernel, out_shape=(shape(ROWS1, cols), shape(PEER1, c...]
    ppermute x2, starting transfers between devices: 0.56 us -> 1.03 us  [exchange(): z = lax.ppermute(jnp.concatenate([y, peer]), 'ja', [(0, 1), (1, 0)])]
where the time goes in v3:
time: 35.8 us; the launch traced here: 35.6 us
  starting transfers between devices  14.5 us (41%)
  waiting for transfers between devices  14.1 us (39%)
  Pallas kernels  6.21 us (17%)
  between operations  0.73 us (2%)
    ppermute x6, starting transfers between devices, exchange(): y = jnp.concatenate([y, lax.ppermute(y, ('ia', 'ja'), pairs)])  13.4 us
    ppermute x6, waiting for transfers between devices, exchange(): y = jnp.concatenate([y, lax.ppermute(y, ('ia', 'ja'), pairs)])  11.8 us
    pallas_call x1, Pallas kernels, on_device(): pl.pallas_call(second_kernel, out_shape=(shape(flat, cols), shape(rows, c...  2.74 us
    ppermute x2, waiting for transfers between devices, exchange(): z = lax.ppermute(jnp.concatenate([y, peer]), 'ja', [(0, 1), (1, 0)])  2.28 us
    pallas_call x1, Pallas kernels, on_device(): pl.pallas_call(first_kernel, out_shape=(shape(flat, cols), shape(ROWS2, c...  1.97 us
    pallas_call x1, Pallas kernels, on_device(): pl.pallas_call(pack_kernel, out_shape=(shape(ROWS1, cols), shape(PEER1, c...  1.49 us
    ppermute x2, starting transfers between devices, exchange(): z = lax.ppermute(jnp.concatenate([y, peer]), 'ja', [(0, 1), (1, 0)])  1.03 us
  transfers between devices with their start and end apart: 8, of which 8 were waited for; matrix products, arithmetic and copies ran while one was open for 0% of the time, Pallas kernels for 0%

profile of v3, /device:TPU:0, one launch (start us, length us, event | category | flops | bytes accessed | tf_op | source)
XLA Modules:
  0.0 35.6 jit_solution(18218545576411340531)
XLA Ops:
  0.6 1.5 %shard_map.95 = (f32[40,128]{1,0:T(8,128)S(1)}, f32[104,128]{1,0:T(8,128)S(1)}, f32[16,128]{1,0:T(8,128)S(1)}, f32[25]{0:T(128)S(1)}, f32[25]{0:T(128)S(1)}) custom-call(f32[25]{0:T(128)} %cp_in.1, f32[25]{0:T(128)} %th_in.1, f32[400,128]{1,0:T(8,128)} %bitcast.15, f32[16,128]{1,0:T(8,128)} %surf_in.1, f32[2,400,128]{2,1,0:T(8,128)} %bitcast.7, ...), custom_call_target="tpu_custom_call" | custom-call | tf_op jit(solution)/shard_map/pallas_call | solution.py:506
  2.1 3.5 %collective-permute-start = (f32[40,128]{1,0:T(8,128)S(1)}, f32[40,128]{1,0:T(8,128)S(1)}, u32[]{:S(2)}, u32[]{:S(2)}) collective-permute-start(f32[40,128]{1,0:T(8,128)S(1)} %get-tuple-element.15), channel_id=1, source_target_pairs={{0,9},{1,8},{2,11},{3,10},{4,13},{5,12},{6,15},{7,14},{8,1},{9,0},... | collective-permute-start | bytes 61448 | tf_op jit(solution)/shard_map/ppermute | solution.py:478
  5.7 1.5 %collective-permute-done = f32[40,128]{1,0:T(8,128)S(1)} collective-permute-done((f32[40,128]{1,0:T(8,128)S(1)}, f32[40,128]{1,0:T(8,128)S(1)}, u32[]{:S(2)}, u32[]{:S(2)}) %collective-permute-start) | collective-permute-done | bytes 20512 | tf_op jit(solution)/shard_map/ppermute | solution.py:478
  7.2 1.9 %collective-permute-start.1 = (f32[80,128]{1,0:T(8,128)S(1)}, f32[80,128]{1,0:T(8,128)S(1)}, u32[]{:S(2)}, u32[]{:S(2)}) collective-permute-start(f32[80,128]{1,0:T(8,128)S(1)} %pad_maximum_fusion.3), channel_id=1, source_target_pairs={{0,5},{1,2},{2,1},{3,6},{4,7},{5,0},{6,3},{7,4},{8,11},{9,12},{10,... | collective-permute-start | bytes 122888 | tf_op jit(solution)/shard_map/ppermute | solution.py:478
  9.1 1.7 %collective-permute-done.1 = f32[80,128]{1,0:T(8,128)S(1)} collective-permute-done((f32[80,128]{1,0:T(8,128)S(1)}, f32[80,128]{1,0:T(8,128)S(1)}, u32[]{:S(2)}, u32[]{:S(2)}) %collective-permute-start.1) | collective-permute-done | bytes 40992 | tf_op jit(solution)/shard_map/ppermute | solution.py:478
  10.7 0.0 copy-start.2
  10.8 1.7 %collective-permute-start.2 = (f32[160,128]{1,0:T(8,128)S(1)}, f32[160,128]{1,0:T(8,128)S(1)}, u32[]{:S(2)}, u32[]{:S(2)}) collective-permute-start(f32[160,128]{1,0:T(8,128)S(1)} %pad_maximum_fusion.1), channel_id=1, source_target_pairs={{0,3},{1,4},{2,7},{3,0},{4,1},{5,6},{6,5},{7,2},{8,13},{9,10},{10,... | collective-permute-start | bytes 245768 | tf_op jit(solution)/shard_map/ppermute | solution.py:478
  12.5 0.0 copy-start
  12.5 2.2 %collective-permute-done.2 = f32[160,128]{1,0:T(8,128)S(1)} collective-permute-done((f32[160,128]{1,0:T(8,128)S(1)}, f32[160,128]{1,0:T(8,128)S(1)}, u32[]{:S(2)}, u32[]{:S(2)}) %collective-permute-start.2) | collective-permute-done | bytes 81952 | tf_op jit(solution)/shard_map/ppermute | solution.py:478
  14.7 0.6 %collective-permute-start.3 = (f32[424,128]{1,0:T(8,128)S(1)}, f32[424,128]{1,0:T(8,128)S(1)}, u32[]{:S(2)}, u32[]{:S(2)}) collective-permute-start(f32[424,128]{1,0:T(8,128)S(1)} %constant_dynamic-update-slice_fusion), channel_id=1, source_target_pairs={{0,1},{1,0},{2,3},{3,2},{4,5},{5,4},{6,7},{7,6},{8,9},{9,8},{10,11... | collective-permute-start | bytes 651272 | tf_op jit(solution)/shard_map/ppermute | solution.py:479
  15.3 1.1 %collective-permute-done.3 = f32[424,128]{1,0:T(8,128)S(1)} collective-permute-done((f32[424,128]{1,0:T(8,128)S(1)}, f32[424,128]{1,0:T(8,128)S(1)}, u32[]{:S(2)}, u32[]{:S(2)}) %collective-permute-start.3) | collective-permute-done | bytes 217120 | tf_op jit(solution)/shard_map/ppermute | solution.py:479
  16.4 0.0 copy-done.2
  16.4 0.0 copy-done.1
  16.4 0.0 copy-done
  16.4 2.0 %shard_map.96 = (f32[400,128]{1,0:T(8,128)S(1)}, f32[64,128]{1,0:T(8,128)S(1)}, f32[32,128]{1,0:T(8,128)S(1)}, f32[40,128]{1,0:T(8,128)S(1)}) custom-call(f32[25]{0:T(128)S(1)} %get-tuple-element.14.cp, f32[25]{0:T(128)S(1)} %get-tuple-element.13.th, f32[2,8,40,128]{3,2,1,0:T(8,128)S(1)} %bitcast.13, f32[104,128]{1,0:T(8,128)S(1)} %slice.17.beyond.beyond1, ...), custom_call_target="tpu_custom_call" | custom-call | tf_op jit(solution)/shard_map/pallas_call | solution.py:530
  18.4 3.0 %collective-permute-start.4 = (f32[64,128]{1,0:T(8,128)S(1)}, f32[64,128]{1,0:T(8,128)S(1)}, u32[]{:S(2)}, u32[]{:S(2)}) collective-permute-start(f32[64,128]{1,0:T(8,128)S(1)} %get-tuple-element.18), channel_id=1, source_target_pairs={{0,9},{1,8},{2,11},{3,10},{4,13},{5,12},{6,15},{7,14},{8,1},{9,0},... | collective-permute-start | bytes 98312 | tf_op jit(solution)/shard_map/ppermute | solution.py:478
  21.4 1.6 %collective-permute-done.4 = f32[64,128]{1,0:T(8,128)S(1)} collective-permute-done((f32[64,128]{1,0:T(8,128)S(1)}, f32[64,128]{1,0:T(8,128)S(1)}, u32[]{:S(2)}, u32[]{:S(2)}) %collective-permute-start.4) | collective-permute-done | bytes 32800 | tf_op jit(solution)/shard_map/ppermute | solution.py:478
  23.0 1.7 %collective-permute-start.5 = (f32[128,128]{1,0:T(8,128)S(1)}, f32[128,128]{1,0:T(8,128)S(1)}, u32[]{:S(2)}, u32[]{:S(2)}) collective-permute-start(f32[128,128]{1,0:T(8,128)S(1)} %pad_maximum_fusion.2), channel_id=1, source_target_pairs={{0,5},{1,2},{2,1},{3,6},{4,7},{5,0},{6,3},{7,4},{8,11},{9,12},{10,... | collective-permute-start | bytes 196616 | tf_op jit(solution)/shard_map/ppermute | solution.py:478
  24.8 1.9 %collective-permute-done.5 = f32[128,128]{1,0:T(8,128)S(1)} collective-permute-done((f32[128,128]{1,0:T(8,128)S(1)}, f32[128,128]{1,0:T(8,128)S(1)}, u32[]{:S(2)}, u32[]{:S(2)}) %collective-permute-start.5) | collective-permute-done | bytes 65568 | tf_op jit(solution)/shard_map/ppermute | solution.py:478
  26.7 1.6 %collective-permute-start.6 = (f32[256,128]{1,0:T(8,128)S(1)}, f32[256,128]{1,0:T(8,128)S(1)}, u32[]{:S(2)}, u32[]{:S(2)}) collective-permute-start(f32[256,128]{1,0:T(8,128)S(1)} %pad_maximum_fusion), channel_id=1, source_target_pairs={{0,3},{1,4},{2,7},{3,0},{4,1},{5,6},{6,5},{7,2},{8,13},{9,10},{10,... | collective-permute-start | bytes 393224 | tf_op jit(solution)/shard_map/ppermute | solution.py:478
  28.3 2.9 %collective-permute-done.6 = f32[256,128]{1,0:T(8,128)S(1)} collective-permute-done((f32[256,128]{1,0:T(8,128)S(1)}, f32[256,128]{1,0:T(8,128)S(1)}, u32[]{:S(2)}, u32[]{:S(2)}) %collective-permute-start.6) | collective-permute-done | bytes 131104 | tf_op jit(solution)/shard_map/ppermute | solution.py:478
  31.2 0.5 %collective-permute-start.7 = (f32[544,128]{1,0:T(8,128)S(1)}, f32[544,128]{1,0:T(8,128)S(1)}, u32[]{:S(2)}, u32[]{:S(2)}) collective-permute-start(f32[544,128]{1,0:T(8,128)S(1)} %constant_dynamic-update-slice_fusion.9), channel_id=1, source_target_pairs={{0,1},{1,0},{2,3},{3,2},{4,5},{5,4},{6,7},{7,6},{8,9},{9,8},{10,11... | collective-permute-start | bytes 835592 | tf_op jit(solution)/shard_map/ppermute | solution.py:479
  31.7 1.2 %collective-permute-done.7 = f32[544,128]{1,0:T(8,128)S(1)} collective-permute-done((f32[544,128]{1,0:T(8,128)S(1)}, f32[544,128]{1,0:T(8,128)S(1)}, u32[]{:S(2)}, u32[]{:S(2)}) %collective-permute-start.7) | collective-permute-done | bytes 278560 | tf_op jit(solution)/shard_map/ppermute | solution.py:479
  32.9 2.7 %shard_map.97 = (f32[400,128]{1,0:T(8,128)}, f32[16,128]{1,0:T(8,128)}) custom-call(f32[25]{0:T(128)S(1)} %get-tuple-element.13.th, f32[2,8,64,128]{3,2,1,0:T(8,128)S(1)} %bitcast.17, f32[32,128]{1,0:T(8,128)S(1)} %slice.19.beyond, f32[2,8,40,128]{3,2,1,0:T(8,128)S(1)} %bitcast.14, f32[104,128]{1,0:T(8,128)S(1)} %slice.17.beyond.beyond1, ...), custom_call_target="tpu_custom_call" | custom-call | tf_op jit(solution)/shard_map/pallas_call | solution.py:548
  (19 shorter events, 0.1 us)
Async XLA Ops:
  2.1 5.1 %collective-permute-start = (f32[40,128]{1,0:T(8,128)S(1)}, f32[40,128]{1,0:T(8,128)S(1)}, u32[]{:S(2)}, u32[]{:S(2)}) collective-permute-start(f32[40,128]{1,0:T(8,128)S(1)} %get-tuple-element.15), channel_id=1, source_target_pairs={{0,9},{1,8},{2,11},{3,10},{4,13},{5,12},{6,15},{7,14},{8,1},{9,0},... | collective-permute-start | bytes 61448 | tf_op jit(solution)/shard_map/ppermute | solution.py:478
  7.2 3.5 %collective-permute-start.1 = (f32[80,128]{1,0:T(8,128)S(1)}, f32[80,128]{1,0:T(8,128)S(1)}, u32[]{:S(2)}, u32[]{:S(2)}) collective-permute-start(f32[80,128]{1,0:T(8,128)S(1)} %pad_maximum_fusion.3), channel_id=1, source_target_pairs={{0,5},{1,2},{2,1},{3,6},{4,7},{5,0},{6,3},{7,4},{8,11},{9,12},{10,... | collective-permute-start | bytes 122888 | tf_op jit(solution)/shard_map/ppermute | solution.py:478
  10.7 5.7 %copy-start.2 = (f32[25,16,128]{2,1,0:T(8,128)S(1)}, f32[25,16,128]{2,1,0:T(8,128)}, u32[]{:S(2)}) copy-start(f32[25,16,128]{2,1,0:T(8,128)} %param.8) | copy-start | bytes 614404
  10.8 3.9 %collective-permute-start.2 = (f32[160,128]{1,0:T(8,128)S(1)}, f32[160,128]{1,0:T(8,128)S(1)}, u32[]{:S(2)}, u32[]{:S(2)}) collective-permute-start(f32[160,128]{1,0:T(8,128)S(1)} %pad_maximum_fusion.1), channel_id=1, source_target_pairs={{0,3},{1,4},{2,7},{3,0},{4,1},{5,6},{6,5},{7,2},{8,13},{9,10},{10,... | collective-permute-start | bytes 245768 | tf_op jit(solution)/shard_map/ppermute | solution.py:478
  12.5 3.9 %copy-start.1 = (f32[2,25,16,128]{3,2,1,0:T(8,128)S(1)}, f32[2,25,16,128]{3,2,1,0:T(8,128)}, u32[]{:S(2)}) copy-start(f32[2,25,16,128]{3,2,1,0:T(8,128)} %param.11) | copy-start | bytes 1228804
  12.5 3.9 %copy-start = (f32[2,25,16,128]{3,2,1,0:T(8,128)S(1)}, f32[2,25,16,128]{3,2,1,0:T(8,128)}, u32[]{:S(2)}) copy-start(f32[2,25,16,128]{3,2,1,0:T(8,128)} %param.10) | copy-start | bytes 1228804
  14.7 1.7 %collective-permute-start.3 = (f32[424,128]{1,0:T(8,128)S(1)}, f32[424,128]{1,0:T(8,128)S(1)}, u32[]{:S(2)}, u32[]{:S(2)}) collective-permute-start(f32[424,128]{1,0:T(8,128)S(1)} %constant_dynamic-update-slice_fusion), channel_id=1, source_target_pairs={{0,1},{1,0},{2,3},{3,2},{4,5},{5,4},{6,7},{7,6},{8,9},{9,8},{10,11... | collective-permute-start | bytes 651272 | tf_op jit(solution)/shard_map/ppermute | solution.py:479
  18.4 4.6 %collective-permute-start.4 = (f32[64,128]{1,0:T(8,128)S(1)}, f32[64,128]{1,0:T(8,128)S(1)}, u32[]{:S(2)}, u32[]{:S(2)}) collective-permute-start(f32[64,128]{1,0:T(8,128)S(1)} %get-tuple-element.18), channel_id=1, source_target_pairs={{0,9},{1,8},{2,11},{3,10},{4,13},{5,12},{6,15},{7,14},{8,1},{9,0},... | collective-permute-start | bytes 98312 | tf_op jit(solution)/shard_map/ppermute | solution.py:478
  23.0 3.7 %collective-permute-start.5 = (f32[128,128]{1,0:T(8,128)S(1)}, f32[128,128]{1,0:T(8,128)S(1)}, u32[]{:S(2)}, u32[]{:S(2)}) collective-permute-start(f32[128,128]{1,0:T(8,128)S(1)} %pad_maximum_fusion.2), channel_id=1, source_target_pairs={{0,5},{1,2},{2,1},{3,6},{4,7},{5,0},{6,3},{7,4},{8,11},{9,12},{10,... | collective-permute-start | bytes 196616 | tf_op jit(solution)/shard_map/ppermute | solution.py:478
  26.7 4.5 %collective-permute-start.6 = (f32[256,128]{1,0:T(8,128)S(1)}, f32[256,128]{1,0:T(8,128)S(1)}, u32[]{:S(2)}, u32[]{:S(2)}) collective-permute-start(f32[256,128]{1,0:T(8,128)S(1)} %pad_maximum_fusion), channel_id=1, source_target_pairs={{0,3},{1,4},{2,7},{3,0},{4,1},{5,6},{6,5},{7,2},{8,13},{9,10},{10,... | collective-permute-start | bytes 393224 | tf_op jit(solution)/shard_map/ppermute | solution.py:478
  31.2 1.6 %collective-permute-start.7 = (f32[544,128]{1,0:T(8,128)S(1)}, f32[544,128]{1,0:T(8,128)S(1)}, u32[]{:S(2)}, u32[]{:S(2)}) collective-permute-start(f32[544,128]{1,0:T(8,128)S(1)} %constant_dynamic-update-slice_fusion.9), channel_id=1, source_target_pairs={{0,1},{1,0},{2,3},{3,2},{4,5},{5,4},{6,7},{7,6},{8,9},{9,8},{10,11... | collective-permute-start | bytes 835592 | tf_op jit(solution)/shard_map/ppermute | solution.py:479

commit v4 on v3

--- a/solution.py
+++ b/solution.py
@@ -85,10 +85,10 @@
 
 def pack_kernel(
     cp_in, th_in, adj_in, surf_in, u_in, v_in, lev_in, par_in, out, peer, depth_out, cp_out, th_out,
-    cp, adj, surf, u, v, lev, par, sems
+    cp, th, adj, surf, u, v, lev, par, sems
 ):
     copies = start_all(
-        ((cp_in, cp), (lev_in, lev), (surf_in, surf), (par_in, par), (adj_in, adj), (u_in, u), (v_in, v), (cp_in, cp_out), (th_in, th_out)),
+        ((cp_in, cp), (lev_in, lev), (surf_in, surf), (par_in, par), (adj_in, adj), (u_in, u), (v_in, v), (th_in, th)),
         sems,
     )
     for copy in copies[:5]:
@@ -116,6 +116,8 @@
         edge = jnp.where(lane == 2 * count + k, u0[:, last:], edge)
     for copy in copies[6:]:
         copy.wait()
+    cp_out[...] = level_column(cp, count, cols)
+    th_out[...] = level_column(th, count, cols)
     out[0:rows, :] = forcing
     out[EDGE1 : EDGE1 + rows, :] = edge
     out[PART1:ROWS1, :] = jnp.zeros((ROWS1 - PART1, cols), F32)
@@ -208,20 +210,21 @@
     is_top = jnp.full((1, cols), top.astype(jnp.int32)) == 1
     for k in range(count):
         here = fetch(k)
-        add = th[k] * own
+        weight = th[k : k + 1, :]
+        add = weight * own
         mid = here + jnp.where(depth > k, add, 0.0)
         bare = here + add
         u_west, t_west = west_of(k)
-        west_value = t_west + th[k] * left
+        west_value = t_west + weight * left
         east_value = jnp.where(
-            lane == cols - 1, east_of(k) + th[k] * right, pltpu.roll(bare, cols - 1, 1)
+            lane == cols - 1, east_of(k) + weight * right, pltpu.roll(bare, cols - 1, 1)
         )
         u_here = u[k * rows : (k + 1) * rows, :]
         v_here = v[k * rows : (k + 1) * rows, :]
         flux_east = jnp.where(east_depth > k, 0.25 * u_here * (east_value - bare), 0.0)
         flux_first = jnp.where(west_depth > k, 0.25 * u_west * (bare - west_value), 0.0)
         flux_west = jnp.where(lane == 0, flux_first, pltpu.roll(flux_east, 1, 1))
-        beside_value = beside_temp(k) + th[k] * beside
+        beside_value = beside_temp(k) + weight * beside
         above = jnp.where(is_top, 0.0, beside_value)
         north_value = jnp.where(row == rows - 1, above, pltpu.roll(bare, rows - 1, 0))
         flux_north = jnp.where(north_depth > k, 0.25 * v_here * (north_value - bare), 0.0)
@@ -284,10 +287,10 @@
     fold_solved = solved[me, 2 * rows - 8 :, :][7:]
     flux = jnp.where(
         fold_depth > level,
-        0.25 * tall[0] * (tall[1] + level_column(th, count, cols) * fold_solved),
+        0.25 * tall[0] * (tall[1] + th[...] * fold_solved),
         0.0,
     )
-    into = jnp.where(across_depth > level, level_column(cp, count, cols) * flux, 0.0)
+    into = jnp.where(across_depth > level, cp[...] * flux, 0.0)
     kept[0:TALL, :] = flux
     kept[TALL:, :] = jnp.broadcast_to(across_depth, (8, cols))
     out[HROW2 : HROW2 + 1, :] = jnp.sum(into, axis=0, keepdims=True)
@@ -311,7 +314,7 @@
 
     def emit(k, value):
         t_out[k * rows : (k + 1) * rows, :] = value
-        carry["forcing"] = carry["forcing"] + cp[k] * jnp.where(depth > k, value, 0.0)
+        carry["forcing"] = carry["forcing"] + cp[k : k + 1, :] * jnp.where(depth > k, value, 0.0)
         edge = jnp.where(spot == k, value[:, cols - 1 :], carry["edge"])
         carry["edge"] = jnp.where(spot == count + k, value[:, :1], edge)
 
@@ -405,7 +408,7 @@
         kept[TALL : TALL + 1, :] > level,
         0.25
         * v_across
-        * (temp_across - kept[0:TALL, :] + level_column(th, count, cols) * across_solved),
+        * (temp_across - kept[0:TALL, :] + th[...] * across_solved),
         0.0,
     )
     tall[2] = fold_last
@@ -495,7 +498,6 @@
     def stay(x):
         return pltpu.with_memory_space_constraint(x, pltpu.HBM)
 
-    smem = pl.BlockSpec(memory_space=pltpu.SMEM)
     vmem = pl.BlockSpec(memory_space=pltpu.VMEM)
     hbm = pl.BlockSpec(memory_space=pltpu.HBM)
 
@@ -509,12 +511,13 @@
             shape(ROWS1, cols),
             shape(PEER1, cols),
             shape(rows, cols),
-            shape(count),
-            shape(count),
+            shape(TALL, cols),
+            shape(TALL, cols),
         ),
         in_specs=[hbm] * 8,
         out_specs=(vmem,) * 5,
         scratch_shapes=[
+            pltpu.SMEM((count,), F32),
             pltpu.SMEM((count,), F32),
             pltpu.VMEM((flat, cols), F32),
             pltpu.VMEM((rows, cols), F32),
@@ -522,7 +525,7 @@
             pltpu.VMEM((steps, flat, cols), F32),
             pltpu.VMEM((rows, cols), jnp.int32),
             pltpu.VMEM((1, cols), jnp.int32),
-            pltpu.SemaphoreType.DMA((9,)),
+            pltpu.SemaphoreType.DMA((8,)),
         ],
         compiler_params=small,
     )(*(stay(x) for x in (coupling, thickness, adj, adjoint_surface, u, v, levels, par)))
@@ -535,7 +538,7 @@
             shape(PEER2, cols),
             shape(TALL + 8, cols),
         ),
-        in_specs=[smem, smem, vmem, vmem, vmem, vmem, vmem, vmem],
+        in_specs=[vmem] * 8,
         out_specs=(vmem,) * 4,
         scratch_shapes=[
             pltpu.VMEM((n, 2 * rows, cols), F32),
@@ -548,7 +551,7 @@
     temp_gradient, surface_gradient = pl.pallas_call(
         second_kernel,
         out_shape=(shape(flat, cols), shape(rows, cols)),
-        in_specs=[smem] + [vmem] * 6 + [vmem]*3,
+        in_specs=[vmem] * 10,
         out_specs=(vmem, vmem),
         scratch_shapes=[
             pltpu.VMEM((n, 2 * rows, cols), F32),

time: 35.8 us -> 34.7 us (0.969)
  Pallas kernels: 6.21 us -> 5.12 us
    pallas_call x1, Pallas kernels: 1.97 us -> 1.42 us  [on_device(): pl.pallas_call(first_kernel, out_shape=(shape(flat, cols), shape(ROWS2, c...]
    pallas_call x1, Pallas kernels: 2.74 us -> 2.2 us  [on_device(): pl.pallas_call(second_kernel, out_shape=(shape(flat, cols), shape(rows, c...]
where the time goes in v4:
time: 34.7 us; the launch traced here: 34.6 us
  starting transfers between devices  14.5 us (42%)
  waiting for transfers between devices  14.1 us (41%)
  Pallas kernels  5.12 us (15%)
  between operations  0.73 us (2%)
    ppermute x6, starting transfers between devices, exchange(): y = jnp.concatenate([y, lax.ppermute(y, ('ia', 'ja'), pairs)])  13.4 us
    ppermute x6, waiting for transfers between devices, exchange(): y = jnp.concatenate([y, lax.ppermute(y, ('ia', 'ja'), pairs)])  11.8 us
    ppermute x2, waiting for transfers between devices, exchange(): z = lax.ppermute(jnp.concatenate([y, peer]), 'ja', [(0, 1), (1, 0)])  2.28 us
    pallas_call x1, Pallas kernels, on_device(): pl.pallas_call(second_kernel, out_shape=(shape(flat, cols), shape(rows, c...  2.2 us
    pallas_call x1, Pallas kernels, on_device(): pl.pallas_call(pack_kernel, out_shape=(shape(ROWS1, cols), shape(PEER1, c...  1.5 us
    pallas_call x1, Pallas kernels, on_device(): pl.pallas_call(first_kernel, out_shape=(shape(flat, cols), shape(ROWS2, c...  1.42 us
    ppermute x2, starting transfers between devices, exchange(): z = lax.ppermute(jnp.concatenate([y, peer]), 'ja', [(0, 1), (1, 0)])  1.03 us
  transfers between devices with their start and end apart: 8, of which 8 were waited for; matrix products, arithmetic and copies ran while one was open for 0% of the time, Pallas kernels for 0%

profile of v4, /device:TPU:0, one launch (start us, length us, event | category | flops | bytes accessed | tf_op | source)
XLA Modules:
  0.0 34.6 jit_solution(6217551742955714598)
XLA Ops:
  0.6 1.5 %shard_map.95 = (f32[40,128]{1,0:T(8,128)S(1)}, f32[104,128]{1,0:T(8,128)S(1)}, f32[16,128]{1,0:T(8,128)S(1)}, f32[32,128]{1,0:T(8,128)S(1)}, f32[32,128]{1,0:T(8,128)S(1)}) custom-call(f32[25]{0:T(128)} %cp_in.1, f32[25]{0:T(128)} %th_in.1, f32[400,128]{1,0:T(8,128)} %bitcast.15, f32[16,128]{1,0:T(8,128)} %surf_in.1, f32[2,400,128]{2,1,0:T(8,128)} %bitcast.7, ...), custom_call_target="tpu_custom_call" | custom-call | tf_op jit(solution)/shard_map/pallas_call | solution.py:508
  2.1 3.5 %collective-permute-start = (f32[40,128]{1,0:T(8,128)S(1)}, f32[40,128]{1,0:T(8,128)S(1)}, u32[]{:S(2)}, u32[]{:S(2)}) collective-permute-start(f32[40,128]{1,0:T(8,128)S(1)} %get-tuple-element.15), channel_id=1, source_target_pairs={{0,9},{1,8},{2,11},{3,10},{4,13},{5,12},{6,15},{7,14},{8,1},{9,0},... | collective-permute-start | bytes 61448 | tf_op jit(solution)/shard_map/ppermute | solution.py:481
  5.7 1.5 %collective-permute-done = f32[40,128]{1,0:T(8,128)S(1)} collective-permute-done((f32[40,128]{1,0:T(8,128)S(1)}, f32[40,128]{1,0:T(8,128)S(1)}, u32[]{:S(2)}, u32[]{:S(2)}) %collective-permute-start) | collective-permute-done | bytes 20512 | tf_op jit(solution)/shard_map/ppermute | solution.py:481
  7.2 1.9 %collective-permute-start.1 = (f32[80,128]{1,0:T(8,128)S(1)}, f32[80,128]{1,0:T(8,128)S(1)}, u32[]{:S(2)}, u32[]{:S(2)}) collective-permute-start(f32[80,128]{1,0:T(8,128)S(1)} %pad_maximum_fusion.3), channel_id=1, source_target_pairs={{0,5},{1,2},{2,1},{3,6},{4,7},{5,0},{6,3},{7,4},{8,11},{9,12},{10,... | collective-permute-start | bytes 122888 | tf_op jit(solution)/shard_map/ppermute | solution.py:481
  9.1 1.7 %collective-permute-done.1 = f32[80,128]{1,0:T(8,128)S(1)} collective-permute-done((f32[80,128]{1,0:T(8,128)S(1)}, f32[80,128]{1,0:T(8,128)S(1)}, u32[]{:S(2)}, u32[]{:S(2)}) %collective-permute-start.1) | collective-permute-done | bytes 40992 | tf_op jit(solution)/shard_map/ppermute | solution.py:481
  10.7 0.0 copy-start.2
  10.8 1.7 %collective-permute-start.2 = (f32[160,128]{1,0:T(8,128)S(1)}, f32[160,128]{1,0:T(8,128)S(1)}, u32[]{:S(2)}, u32[]{:S(2)}) collective-permute-start(f32[160,128]{1,0:T(8,128)S(1)} %pad_maximum_fusion.1), channel_id=1, source_target_pairs={{0,3},{1,4},{2,7},{3,0},{4,1},{5,6},{6,5},{7,2},{8,13},{9,10},{10,... | collective-permute-start | bytes 245768 | tf_op jit(solution)/shard_map/ppermute | solution.py:481
  12.5 0.0 copy-start
  12.5 2.2 %collective-permute-done.2 = f32[160,128]{1,0:T(8,128)S(1)} collective-permute-done((f32[160,128]{1,0:T(8,128)S(1)}, f32[160,128]{1,0:T(8,128)S(1)}, u32[]{:S(2)}, u32[]{:S(2)}) %collective-permute-start.2) | collective-permute-done | bytes 81952 | tf_op jit(solution)/shard_map/ppermute | solution.py:481
  14.7 0.6 %collective-permute-start.3 = (f32[424,128]{1,0:T(8,128)S(1)}, f32[424,128]{1,0:T(8,128)S(1)}, u32[]{:S(2)}, u32[]{:S(2)}) collective-permute-start(f32[424,128]{1,0:T(8,128)S(1)} %constant_dynamic-update-slice_fusion), channel_id=1, source_target_pairs={{0,1},{1,0},{2,3},{3,2},{4,5},{5,4},{6,7},{7,6},{8,9},{9,8},{10,11... | collective-permute-start | bytes 651272 | tf_op jit(solution)/shard_map/ppermute | solution.py:482
  15.3 1.1 %collective-permute-done.3 = f32[424,128]{1,0:T(8,128)S(1)} collective-permute-done((f32[424,128]{1,0:T(8,128)S(1)}, f32[424,128]{1,0:T(8,128)S(1)}, u32[]{:S(2)}, u32[]{:S(2)}) %collective-permute-start.3) | collective-permute-done | bytes 217120 | tf_op jit(solution)/shard_map/ppermute | solution.py:482
  16.4 0.0 copy-done.2
  16.4 0.0 copy-done.1
  16.4 0.0 copy-done
  16.4 1.4 %shard_map.96 = (f32[400,128]{1,0:T(8,128)S(1)}, f32[64,128]{1,0:T(8,128)S(1)}, f32[32,128]{1,0:T(8,128)S(1)}, f32[40,128]{1,0:T(8,128)S(1)}) custom-call(f32[32,128]{1,0:T(8,128)S(1)} %get-tuple-element.14.cp, f32[32,128]{1,0:T(8,128)S(1)} %get-tuple-element.13.th, f32[2,8,40,128]{3,2,1,0:T(8,128)S(1)} %bitcast.13, f32[104,128]{1,0:T(8,128)S(1)} %slice.17.beyond.beyond1, ...), custom_call_target="tpu_custom_call" | custom-call | tf_op jit(solution)/shard_map/pallas_call | solution.py:533
  17.9 3.0 %collective-permute-start.4 = (f32[64,128]{1,0:T(8,128)S(1)}, f32[64,128]{1,0:T(8,128)S(1)}, u32[]{:S(2)}, u32[]{:S(2)}) collective-permute-start(f32[64,128]{1,0:T(8,128)S(1)} %get-tuple-element.18), channel_id=1, source_target_pairs={{0,9},{1,8},{2,11},{3,10},{4,13},{5,12},{6,15},{7,14},{8,1},{9,0},... | collective-permute-start | bytes 98312 | tf_op jit(solution)/shard_map/ppermute | solution.py:481
  20.9 1.6 %collective-permute-done.4 = f32[64,128]{1,0:T(8,128)S(1)} collective-permute-done((f32[64,128]{1,0:T(8,128)S(1)}, f32[64,128]{1,0:T(8,128)S(1)}, u32[]{:S(2)}, u32[]{:S(2)}) %collective-permute-start.4) | collective-permute-done | bytes 32800 | tf_op jit(solution)/shard_map/ppermute | solution.py:481
  22.5 1.7 %collective-permute-start.5 = (f32[128,128]{1,0:T(8,128)S(1)}, f32[128,128]{1,0:T(8,128)S(1)}, u32[]{:S(2)}, u32[]{:S(2)}) collective-permute-start(f32[128,128]{1,0:T(8,128)S(1)} %pad_maximum_fusion.2), channel_id=1, source_target_pairs={{0,5},{1,2},{2,1},{3,6},{4,7},{5,0},{6,3},{7,4},{8,11},{9,12},{10,... | collective-permute-start | bytes 196616 | tf_op jit(solution)/shard_map/ppermute | solution.py:481
  24.2 1.9 %collective-permute-done.5 = f32[128,128]{1,0:T(8,128)S(1)} collective-permute-done((f32[128,128]{1,0:T(8,128)S(1)}, f32[128,128]{1,0:T(8,128)S(1)}, u32[]{:S(2)}, u32[]{:S(2)}) %collective-permute-start.5) | collective-permute-done | bytes 65568 | tf_op jit(solution)/shard_map/ppermute | solution.py:481
  26.2 1.5 %collective-permute-start.6 = (f32[256,128]{1,0:T(8,128)S(1)}, f32[256,128]{1,0:T(8,128)S(1)}, u32[]{:S(2)}, u32[]{:S(2)}) collective-permute-start(f32[256,128]{1,0:T(8,128)S(1)} %pad_maximum_fusion), channel_id=1, source_target_pairs={{0,3},{1,4},{2,7},{3,0},{4,1},{5,6},{6,5},{7,2},{8,13},{9,10},{10,... | collective-permute-start | bytes 393224 | tf_op jit(solution)/shard_map/ppermute | solution.py:481
  27.8 2.9 %collective-permute-done.6 = f32[256,128]{1,0:T(8,128)S(1)} collective-permute-done((f32[256,128]{1,0:T(8,128)S(1)}, f32[256,128]{1,0:T(8,128)S(1)}, u32[]{:S(2)}, u32[]{:S(2)}) %collective-permute-start.6) | collective-permute-done | bytes 131104 | tf_op jit(solution)/shard_map/ppermute | solution.py:481
  30.7 0.5 %collective-permute-start.7 = (f32[544,128]{1,0:T(8,128)S(1)}, f32[544,128]{1,0:T(8,128)S(1)}, u32[]{:S(2)}, u32[]{:S(2)}) collective-permute-start(f32[544,128]{1,0:T(8,128)S(1)} %constant_dynamic-update-slice_fusion.9), channel_id=1, source_target_pairs={{0,1},{1,0},{2,3},{3,2},{4,5},{5,4},{6,7},{7,6},{8,9},{9,8},{10,11... | collective-permute-start | bytes 835592 | tf_op jit(solution)/shard_map/ppermute | solution.py:482
  31.1 1.2 %collective-permute-done.7 = f32[544,128]{1,0:T(8,128)S(1)} collective-permute-done((f32[544,128]{1,0:T(8,128)S(1)}, f32[544,128]{1,0:T(8,128)S(1)}, u32[]{:S(2)}, u32[]{:S(2)}) %collective-permute-start.7) | collective-permute-done | bytes 278560 | tf_op jit(solution)/shard_map/ppermute | solution.py:482
  32.4 2.2 %shard_map.97 = (f32[400,128]{1,0:T(8,128)}, f32[16,128]{1,0:T(8,128)}) custom-call(f32[32,128]{1,0:T(8,128)S(1)} %get-tuple-element.13.th, f32[2,8,64,128]{3,2,1,0:T(8,128)S(1)} %bitcast.17, f32[32,128]{1,0:T(8,128)S(1)} %slice.19.beyond, f32[2,8,40,128]{3,2,1,0:T(8,128)S(1)} %bitcast.14, f32[104,128]{1,0:T(8,128)S(1)} %slice.17.beyond.beyond1, ...), custom_call_target="tpu_custom_call" | custom-call | tf_op jit(solution)/shard_map/pallas_call | solution.py:551
  (19 shorter events, 0.1 us)
Async XLA Ops:
  2.1 5.1 %collective-permute-start = (f32[40,128]{1,0:T(8,128)S(1)}, f32[40,128]{1,0:T(8,128)S(1)}, u32[]{:S(2)}, u32[]{:S(2)}) collective-permute-start(f32[40,128]{1,0:T(8,128)S(1)} %get-tuple-element.15), channel_id=1, source_target_pairs={{0,9},{1,8},{2,11},{3,10},{4,13},{5,12},{6,15},{7,14},{8,1},{9,0},... | collective-permute-start | bytes 61448 | tf_op jit(solution)/shard_map/ppermute | solution.py:481
  7.2 3.5 %collective-permute-start.1 = (f32[80,128]{1,0:T(8,128)S(1)}, f32[80,128]{1,0:T(8,128)S(1)}, u32[]{:S(2)}, u32[]{:S(2)}) collective-permute-start(f32[80,128]{1,0:T(8,128)S(1)} %pad_maximum_fusion.3), channel_id=1, source_target_pairs={{0,5},{1,2},{2,1},{3,6},{4,7},{5,0},{6,3},{7,4},{8,11},{9,12},{10,... | collective-permute-start | bytes 122888 | tf_op jit(solution)/shard_map/ppermute | solution.py:481
  10.7 5.7 %copy-start.2 = (f32[25,16,128]{2,1,0:T(8,128)S(1)}, f32[25,16,128]{2,1,0:T(8,128)}, u32[]{:S(2)}) copy-start(f32[25,16,128]{2,1,0:T(8,128)} %param.8) | copy-start | bytes 614404
  10.8 3.9 %collective-permute-start.2 = (f32[160,128]{1,0:T(8,128)S(1)}, f32[160,128]{1,0:T(8,128)S(1)}, u32[]{:S(2)}, u32[]{:S(2)}) collective-permute-start(f32[160,128]{1,0:T(8,128)S(1)} %pad_maximum_fusion.1), channel_id=1, source_target_pairs={{0,3},{1,4},{2,7},{3,0},{4,1},{5,6},{6,5},{7,2},{8,13},{9,10},{10,... | collective-permute-start | bytes 245768 | tf_op jit(solution)/shard_map/ppermute | solution.py:481
  12.5 3.9 %copy-start.1 = (f32[2,25,16,128]{3,2,1,0:T(8,128)S(1)}, f32[2,25,16,128]{3,2,1,0:T(8,128)}, u32[]{:S(2)}) copy-start(f32[2,25,16,128]{3,2,1,0:T(8,128)} %param.11) | copy-start | bytes 1228804
  12.5 3.9 %copy-start = (f32[2,25,16,128]{3,2,1,0:T(8,128)S(1)}, f32[2,25,16,128]{3,2,1,0:T(8,128)}, u32[]{:S(2)}) copy-start(f32[2,25,16,128]{3,2,1,0:T(8,128)} %param.10) | copy-start | bytes 1228804
  14.7 1.7 %collective-permute-start.3 = (f32[424,128]{1,0:T(8,128)S(1)}, f32[424,128]{1,0:T(8,128)S(1)}, u32[]{:S(2)}, u32[]{:S(2)}) collective-permute-start(f32[424,128]{1,0:T(8,128)S(1)} %constant_dynamic-update-slice_fusion), channel_id=1, source_target_pairs={{0,1},{1,0},{2,3},{3,2},{4,5},{5,4},{6,7},{7,6},{8,9},{9,8},{10,11... | collective-permute-start | bytes 651272 | tf_op jit(solution)/shard_map/ppermute | solution.py:482
  17.9 4.6 %collective-permute-start.4 = (f32[64,128]{1,0:T(8,128)S(1)}, f32[64,128]{1,0:T(8,128)S(1)}, u32[]{:S(2)}, u32[]{:S(2)}) collective-permute-start(f32[64,128]{1,0:T(8,128)S(1)} %get-tuple-element.18), channel_id=1, source_target_pairs={{0,9},{1,8},{2,11},{3,10},{4,13},{5,12},{6,15},{7,14},{8,1},{9,0},... | collective-permute-start | bytes 98312 | tf_op jit(solution)/shard_map/ppermute | solution.py:481
  22.5 3.7 %collective-permute-start.5 = (f32[128,128]{1,0:T(8,128)S(1)}, f32[128,128]{1,0:T(8,128)S(1)}, u32[]{:S(2)}, u32[]{:S(2)}) collective-permute-start(f32[128,128]{1,0:T(8,128)S(1)} %pad_maximum_fusion.2), channel_id=1, source_target_pairs={{0,5},{1,2},{2,1},{3,6},{4,7},{5,0},{6,3},{7,4},{8,11},{9,12},{10,... | collective-permute-start | bytes 196616 | tf_op jit(solution)/shard_map/ppermute | solution.py:481
  26.2 4.5 %collective-permute-start.6 = (f32[256,128]{1,0:T(8,128)S(1)}, f32[256,128]{1,0:T(8,128)S(1)}, u32[]{:S(2)}, u32[]{:S(2)}) collective-permute-start(f32[256,128]{1,0:T(8,128)S(1)} %pad_maximum_fusion), channel_id=1, source_target_pairs={{0,3},{1,4},{2,7},{3,0},{4,1},{5,6},{6,5},{7,2},{8,13},{9,10},{10,... | collective-permute-start | bytes 393224 | tf_op jit(solution)/shard_map/ppermute | solution.py:481
  30.7 1.6 %collective-permute-start.7 = (f32[544,128]{1,0:T(8,128)S(1)}, f32[544,128]{1,0:T(8,128)S(1)}, u32[]{:S(2)}, u32[]{:S(2)}) collective-permute-start(f32[544,128]{1,0:T(8,128)S(1)} %constant_dynamic-update-slice_fusion.9), channel_id=1, source_target_pairs={{0,1},{1,0},{2,3},{3,2},{4,5},{5,4},{6,7},{7,6},{8,9},{9,8},{10,11... | collective-permute-start | bytes 835592 | tf_op jit(solution)/shard_map/ppermute | solution.py:482

commit v5 on v4

--- a/solution.py
+++ b/solution.py
@@ -9,7 +9,8 @@
 SURFACE_COEF = 2.0
 F32 = jnp.float32
 
-EDGE1, PART1, LEV1, ROWS1 = 16, 32, 33, 40
+EDGE1, ROWS1 = 16, 32
+DEPTHS = 32
 EDGE2, HROW2, LINE2, FLUX2, ROWS2 = 16, 24, 25, 50, 64
 PEER1, PEER2 = 104, 32
 WINDOW = 16
@@ -21,7 +22,8 @@
 
 
 def full_sum(x):
-    return jnp.sum(jnp.sum(x, axis=0), axis=(0, 1), keepdims=True)
+    lines = jnp.sum(x.reshape(-1, 8, x.shape[-1]), axis=0)
+    return jnp.sum(jnp.sum(lines, axis=0, keepdims=True), axis=1, keepdims=True)
 
 
 def split_index(column, cols):
@@ -55,25 +57,24 @@
 
 
 def surface_solve(forcing, block, lane):
-    residual = forcing
-    direction = forcing
-    iterate = None
-    norm_now = full_sum(residual * residual)
-    for sweep in range(SOLVER_ITERS):
-        applied = surface_apply(direction, block, lane)
-        step_size = norm_now / full_sum(direction * applied)
-        part = step_size * direction
-        iterate = part if iterate is None else iterate + part
-        if sweep + 1 < SOLVER_ITERS:
-            residual = residual - step_size * applied
-            norm_next = full_sum(residual * residual)
-            direction = residual + norm_next / norm_now * direction
-            norm_now = norm_next
-    return iterate
+    applied = surface_apply(forcing, block, lane)
+    again = surface_apply(applied, block, lane)
+    norm = full_sum(forcing * forcing)
+    step_size = norm / full_sum(forcing * applied)
+    residual = forcing - step_size * applied
+    ratio = full_sum(residual * residual) / norm
+    direction = residual + ratio * forcing
+    turned = (1.0 + ratio) * applied - step_size * again
+    next_size = ratio * norm / full_sum(direction * turned)
+    return step_size * forcing + next_size * direction
 
 
 def level_rows(ref, base, count, rows):
     return ref[pl.ds(base, count, stride=rows), :]
+
+
+def code_place(rows, cols):
+    return rows - 2
 
 
 def start_all(pairs, sems):
@@ -114,15 +115,17 @@
         u1 = u[1, k * rows : (k + 1) * rows, :]
         edge = jnp.where(lane == count + k, u1[:, last:], edge)
         edge = jnp.where(lane == 2 * count + k, u0[:, last:], edge)
+    width = cols // rows
+    code = par[...].astype(F32) * DEPTHS + depth[rows - 1 :]
+    taken = (iota((rows, cols), 0) * width + (lane & (width - 1))) & (cols - 1)
+    spread = jnp.take_along_axis(jnp.broadcast_to(code, (rows, cols)), taken, axis=1)
+    edge = jnp.where(lane // width == code_place(rows, cols), spread, edge)
+    out[EDGE1 : EDGE1 + rows, :] = edge
     for copy in copies[6:]:
         copy.wait()
     cp_out[...] = level_column(cp, count, cols)
     th_out[...] = level_column(th, count, cols)
     out[0:rows, :] = forcing
-    out[EDGE1 : EDGE1 + rows, :] = edge
-    out[PART1:ROWS1, :] = jnp.zeros((ROWS1 - PART1, cols), F32)
-    out[PART1 : PART1 + 1, :] = par[...].astype(F32)
-    out[LEV1 : LEV1 + 1, :] = depth[rows - 1 :]
     peer[...] = jnp.zeros(peer.shape, F32)
     is_top = jnp.full((count, cols), top.astype(jnp.int32)) == 1
     last_row = level_rows(adj, rows - 1, count, rows)
@@ -181,6 +184,18 @@
             for b in range(self.count)
         ]
         return jnp.stack(blocks, axis=0)
+
+    def codes(self, rows, out):
+        cols = self.both.shape[3]
+        width = cols // rows
+        lane = iota((rows, cols), 1)
+        taken = code_place(rows, cols) * width + (lane & (width - 1))
+        here = lane // width == iota((rows, cols), 0)
+        for b in range(self.count):
+            edge = self.part(b, 1, EDGE1, EDGE1 + rows)
+            moved = jnp.where(here, jnp.take_along_axis(edge, taken, axis=1), 0.0)
+            out[b : b + 1, :] = jnp.sum(moved, axis=0, keepdims=True)
+        return out[...].astype(jnp.int32)
 
     def line(self, core, index, out):
         for b in range(self.count):
@@ -260,7 +275,7 @@
 
 
 def first_kernel(
-    cp, th, both, beyond, adj, u_in, v_in, depth_in, t_out, out, peer, kept, solved, rowbuf, tall
+    cp, th, both, beyond, adj, u_in, v_in, depth_in, t_out, out, peer, kept, table, solved, rowbuf, tall
 ):
     u, v = u_in.at[1], v_in.at[1]
     rows, cols = depth_in.shape
@@ -268,10 +283,13 @@
     top = lax.axis_index("ja") == lax.axis_size("ja") - 1
     sent = Messages(both)
     me, west, east = position(sent.count)
-    partner = sent.line(0, PART1, rowbuf).astype(jnp.int32)
+    code = sent.codes(rows, rowbuf)
+    partner = code >> (DEPTHS.bit_length() - 1)
+    table[...] = partner
     block, lane = split_index(partner, cols)
     solved[...] = surface_solve(sent.field(rows), block, lane)
-    depths = sent.line(1, LEV1, rowbuf)
+    depths = (code & (DEPTHS - 1)).astype(F32)
+    rowbuf[...] = depths
     fold_depth = rowbuf[pl.ds(me, 1), :]
     rowbuf[...] = fold_take(depths, block, lane)
     across_depth = rowbuf[pl.ds(me, 1), :]
@@ -351,7 +369,7 @@
 
 
 def second_kernel(
-    th, both, beyond, both1, beyond1, kept, temp, u_in, v_in, depth_in, t_out, s_out, solved, rowbuf, tall
+    th, both, beyond, both1, beyond1, kept, table, temp, u_in, v_in, depth_in, t_out, s_out, solved, rowbuf, tall
 ):
     u, v = u_in.at[0], v_in.at[0]
     rows, cols = depth_in.shape
@@ -360,8 +378,7 @@
     sent, sent1 = Messages(both), Messages(both1)
     n = sent.count
     me, west, east = position(n)
-    partners = sent1.line(0, PART1, rowbuf)
-    partner = partners.astype(jnp.int32)
+    partner = table[...]
     block, lane = split_index(partner, cols)
     forcing = sent.field(rows)
     fold = fold_take(sent.line(0, HROW2, rowbuf), block, lane)
@@ -373,7 +390,7 @@
     across_solved = rowbuf[pl.ds(me, 1), :]
 
     spot = iota((1, cols), 1)
-    rowbuf[...] = partners
+    rowbuf[...] = partner.astype(F32)
     beside_left = pltpu.roll(rowbuf[pl.ds(west, 1), :], 1, 1)
     beside_right = pltpu.roll(rowbuf[pl.ds(east, 1), :], cols - 1, 1)
     end_partner = jnp.where(spot == 0, beside_left, beside_right)
@@ -530,16 +547,17 @@
         compiler_params=small,
     )(*(stay(x) for x in (coupling, thickness, adj, adjoint_surface, u, v, levels, par)))
     both1, beyond1 = exchange(out, peer)
-    temp, out, peer, kept = pl.pallas_call(
+    temp, out, peer, kept, table = pl.pallas_call(
         first_kernel,
         out_shape=(
             shape(flat, cols),
             shape(ROWS2, cols),
             shape(PEER2, cols),
             shape(TALL + 8, cols),
+            jax.ShapeDtypeStruct((n, cols), jnp.int32),
         ),
         in_specs=[vmem] * 8,
-        out_specs=(vmem,) * 4,
+        out_specs=(vmem,) * 5,
         scratch_shapes=[
             pltpu.VMEM((n, 2 * rows, cols), F32),
             pltpu.VMEM((n, cols), F32),
@@ -551,7 +569,7 @@
     temp_gradient, surface_gradient = pl.pallas_call(
         second_kernel,
         out_shape=(shape(flat, cols), shape(rows, cols)),
-        in_specs=[vmem] * 10,
+        in_specs=[vmem] * 11,
         out_specs=(vmem, vmem),
         scratch_shapes=[
             pltpu.VMEM((n, 2 * rows, cols), F32),
@@ -559,7 +577,7 @@
             pltpu.VMEM((3, TALL, cols), F32),
         ],
         compiler_params=small,
-    )(th, both, beyond, both1, beyond1, kept, temp, u, v, depth)
+    )(th, both, beyond, both1, beyond1, kept, table, temp, u, v, depth)
     return temp_gradient.reshape(count, rows, cols), surface_gradient
 
 

time: 34.7 us -> 34.1 us (0.983)
  waiting for transfers between devices: 14.1 us -> 13.7 us
where the time goes in v5:
time: 34.1 us; the launch traced here: 34 us
  starting transfers between devices  14.4 us (42%)
  waiting for transfers between devices  13.7 us (40%)
  Pallas kernels  4.99 us (15%)
  between operations  0.72 us (2%)
    ppermute x6, starting transfers between devices, exchange(): y = jnp.concatenate([y, lax.ppermute(y, ('ia', 'ja'), pairs)])  13.3 us
    ppermute x6, waiting for transfers between devices, exchange(): y = jnp.concatenate([y, lax.ppermute(y, ('ia', 'ja'), pairs)])  11.5 us
    ppermute x2, waiting for transfers between devices, exchange(): z = lax.ppermute(jnp.concatenate([y, peer]), 'ja', [(0, 1), (1, 0)])  2.24 us
    pallas_call x1, Pallas kernels, on_device(): pl.pallas_call(second_kernel, out_shape=(shape(flat, cols), shape(rows, c...  2.11 us
    pallas_call x1, Pallas kernels, on_device(): pl.pallas_call(pack_kernel, out_shape=(shape(ROWS1, cols), shape(PEER1, c...  1.51 us
    pallas_call x1, Pallas kernels, on_device(): pl.pallas_call(first_kernel, out_shape=(shape(flat, cols), shape(ROWS2, c...  1.38 us
    ppermute x2, starting transfers between devices, exchange(): z = lax.ppermute(jnp.concatenate([y, peer]), 'ja', [(0, 1), (1, 0)])  1.04 us
  transfers between devices with their start and end apart: 8, of which 8 were waited for; matrix products, arithmetic and copies ran while one was open for 0% of the time, Pallas kernels for 0%

profile of v5, /device:TPU:0, one launch (start us, length us, event | category | flops | bytes accessed | tf_op | source)
XLA Modules:
  0.0 34.0 jit_solution(3320537692202200932)
XLA Ops:
  0.6 1.5 %shard_map.95 = (f32[32,128]{1,0:T(8,128)S(1)}, f32[104,128]{1,0:T(8,128)S(1)}, f32[16,128]{1,0:T(8,128)S(1)}, f32[32,128]{1,0:T(8,128)S(1)}, f32[32,128]{1,0:T(8,128)S(1)}) custom-call(f32[25]{0:T(128)} %cp_in.1, f32[25]{0:T(128)} %th_in.1, f32[400,128]{1,0:T(8,128)} %bitcast.15, f32[16,128]{1,0:T(8,128)} %surf_in.1, f32[2,400,128]{2,1,0:T(8,128)} %bitcast.7, ...), custom_call_target="tpu_custom_call" | custom-call | tf_op jit(solution)/shard_map/pallas_call | solution.py:525
  2.1 3.5 %collective-permute-start = (f32[32,128]{1,0:T(8,128)S(1)}, f32[32,128]{1,0:T(8,128)S(1)}, u32[]{:S(2)}, u32[]{:S(2)}) collective-permute-start(f32[32,128]{1,0:T(8,128)S(1)} %get-tuple-element.16), channel_id=1, source_target_pairs={{0,9},{1,8},{2,11},{3,10},{4,13},{5,12},{6,15},{7,14},{8,1},{9,0},... | collective-permute-start | bytes 49160 | tf_op jit(solution)/shard_map/ppermute | solution.py:498
  5.7 1.4 %collective-permute-done = f32[32,128]{1,0:T(8,128)S(1)} collective-permute-done((f32[32,128]{1,0:T(8,128)S(1)}, f32[32,128]{1,0:T(8,128)S(1)}, u32[]{:S(2)}, u32[]{:S(2)}) %collective-permute-start) | collective-permute-done | bytes 16416 | tf_op jit(solution)/shard_map/ppermute | solution.py:498
  7.1 0.0 copy-start.2
  7.1 1.9 %collective-permute-start.1 = (f32[64,128]{1,0:T(8,128)S(1)}, f32[64,128]{1,0:T(8,128)S(1)}, u32[]{:S(2)}, u32[]{:S(2)}) collective-permute-start(f32[64,128]{1,0:T(8,128)S(1)} %pad_maximum_fusion.3), channel_id=1, source_target_pairs={{0,5},{1,2},{2,1},{3,6},{4,7},{5,0},{6,3},{7,4},{8,11},{9,12},{10,... | collective-permute-start | bytes 98312 | tf_op jit(solution)/shard_map/ppermute | solution.py:498
  9.0 1.6 %collective-permute-done.1 = f32[64,128]{1,0:T(8,128)S(1)} collective-permute-done((f32[64,128]{1,0:T(8,128)S(1)}, f32[64,128]{1,0:T(8,128)S(1)}, u32[]{:S(2)}, u32[]{:S(2)}) %collective-permute-start.1) | collective-permute-done | bytes 32800 | tf_op jit(solution)/shard_map/ppermute | solution.py:498
  10.6 0.0 copy-start
  10.6 1.7 %collective-permute-start.2 = (f32[128,128]{1,0:T(8,128)S(1)}, f32[128,128]{1,0:T(8,128)S(1)}, u32[]{:S(2)}, u32[]{:S(2)}) collective-permute-start(f32[128,128]{1,0:T(8,128)S(1)} %pad_maximum_fusion.1), channel_id=1, source_target_pairs={{0,3},{1,4},{2,7},{3,0},{4,1},{5,6},{6,5},{7,2},{8,13},{9,10},{10,... | collective-permute-start | bytes 196616 | tf_op jit(solution)/shard_map/ppermute | solution.py:498
  12.4 2.0 %collective-permute-done.2 = f32[128,128]{1,0:T(8,128)S(1)} collective-permute-done((f32[128,128]{1,0:T(8,128)S(1)}, f32[128,128]{1,0:T(8,128)S(1)}, u32[]{:S(2)}, u32[]{:S(2)}) %collective-permute-start.2) | collective-permute-done | bytes 65568 | tf_op jit(solution)/shard_map/ppermute | solution.py:498
  14.4 0.6 %collective-permute-start.3 = (f32[360,128]{1,0:T(8,128)S(1)}, f32[360,128]{1,0:T(8,128)S(1)}, u32[]{:S(2)}, u32[]{:S(2)}) collective-permute-start(f32[360,128]{1,0:T(8,128)S(1)} %constant_dynamic-update-slice_fusion), channel_id=1, source_target_pairs={{0,1},{1,0},{2,3},{3,2},{4,5},{5,4},{6,7},{7,6},{8,9},{9,8},{10,11... | collective-permute-start | bytes 552968 | tf_op jit(solution)/shard_map/ppermute | solution.py:499
  15.0 1.1 %collective-permute-done.3 = f32[360,128]{1,0:T(8,128)S(1)} collective-permute-done((f32[360,128]{1,0:T(8,128)S(1)}, f32[360,128]{1,0:T(8,128)S(1)}, u32[]{:S(2)}, u32[]{:S(2)}) %collective-permute-start.3) | collective-permute-done | bytes 184352 | tf_op jit(solution)/shard_map/ppermute | solution.py:499
  16.1 0.0 copy-done.2
  16.1 0.0 copy-done.1
  16.1 0.0 copy-done
  16.1 1.4 %shard_map.96 = (f32[400,128]{1,0:T(8,128)S(1)}, f32[64,128]{1,0:T(8,128)S(1)}, f32[32,128]{1,0:T(8,128)S(1)}, f32[40,128]{1,0:T(8,128)S(1)}, s32[8,128]{1,0:T(8,128)S(1)}) custom-call(f32[32,128]{1,0:T(8,128)S(1)} %get-tuple-element.15.cp, f32[32,128]{1,0:T(8,128)S(1)} %get-tuple-element.14.th, f32[2,8,32,128]{3,2,1,0:T(8,128)S(1)} %bitcast.13, ...), custom_call_target="tpu_custom_call" | custom-call | tf_op jit(solution)/shard_map/pallas_call | solution.py:550
  17.5 2.9 %collective-permute-start.4 = (f32[64,128]{1,0:T(8,128)S(1)}, f32[64,128]{1,0:T(8,128)S(1)}, u32[]{:S(2)}, u32[]{:S(2)}) collective-permute-start(f32[64,128]{1,0:T(8,128)S(1)} %get-tuple-element.19), channel_id=1, source_target_pairs={{0,9},{1,8},{2,11},{3,10},{4,13},{5,12},{6,15},{7,14},{8,1},{9,0},... | collective-permute-start | bytes 98312 | tf_op jit(solution)/shard_map/ppermute | solution.py:498
  20.4 1.6 %collective-permute-done.4 = f32[64,128]{1,0:T(8,128)S(1)} collective-permute-done((f32[64,128]{1,0:T(8,128)S(1)}, f32[64,128]{1,0:T(8,128)S(1)}, u32[]{:S(2)}, u32[]{:S(2)}) %collective-permute-start.4) | collective-permute-done | bytes 32800 | tf_op jit(solution)/shard_map/ppermute | solution.py:498
  22.0 1.7 %collective-permute-start.5 = (f32[128,128]{1,0:T(8,128)S(1)}, f32[128,128]{1,0:T(8,128)S(1)}, u32[]{:S(2)}, u32[]{:S(2)}) collective-permute-start(f32[128,128]{1,0:T(8,128)S(1)} %pad_maximum_fusion.2), channel_id=1, source_target_pairs={{0,5},{1,2},{2,1},{3,6},{4,7},{5,0},{6,3},{7,4},{8,11},{9,12},{10,... | collective-permute-start | bytes 196616 | tf_op jit(solution)/shard_map/ppermute | solution.py:498
  23.7 1.9 %collective-permute-done.5 = f32[128,128]{1,0:T(8,128)S(1)} collective-permute-done((f32[128,128]{1,0:T(8,128)S(1)}, f32[128,128]{1,0:T(8,128)S(1)}, u32[]{:S(2)}, u32[]{:S(2)}) %collective-permute-start.5) | collective-permute-done | bytes 65568 | tf_op jit(solution)/shard_map/ppermute | solution.py:498
  25.7 1.6 %collective-permute-start.6 = (f32[256,128]{1,0:T(8,128)S(1)}, f32[256,128]{1,0:T(8,128)S(1)}, u32[]{:S(2)}, u32[]{:S(2)}) collective-permute-start(f32[256,128]{1,0:T(8,128)S(1)} %pad_maximum_fusion), channel_id=1, source_target_pairs={{0,3},{1,4},{2,7},{3,0},{4,1},{5,6},{6,5},{7,2},{8,13},{9,10},{10,... | collective-permute-start | bytes 393224 | tf_op jit(solution)/shard_map/ppermute | solution.py:498
  27.3 2.9 %collective-permute-done.6 = f32[256,128]{1,0:T(8,128)S(1)} collective-permute-done((f32[256,128]{1,0:T(8,128)S(1)}, f32[256,128]{1,0:T(8,128)S(1)}, u32[]{:S(2)}, u32[]{:S(2)}) %collective-permute-start.6) | collective-permute-done | bytes 131104 | tf_op jit(solution)/shard_map/ppermute | solution.py:498
  30.2 0.5 %collective-permute-start.7 = (f32[544,128]{1,0:T(8,128)S(1)}, f32[544,128]{1,0:T(8,128)S(1)}, u32[]{:S(2)}, u32[]{:S(2)}) collective-permute-start(f32[544,128]{1,0:T(8,128)S(1)} %constant_dynamic-update-slice_fusion.9), channel_id=1, source_target_pairs={{0,1},{1,0},{2,3},{3,2},{4,5},{5,4},{6,7},{7,6},{8,9},{9,8},{10,11... | collective-permute-start | bytes 835592 | tf_op jit(solution)/shard_map/ppermute | solution.py:499
  30.6 1.2 %collective-permute-done.7 = f32[544,128]{1,0:T(8,128)S(1)} collective-permute-done((f32[544,128]{1,0:T(8,128)S(1)}, f32[544,128]{1,0:T(8,128)S(1)}, u32[]{:S(2)}, u32[]{:S(2)}) %collective-permute-start.7) | collective-permute-done | bytes 278560 | tf_op jit(solution)/shard_map/ppermute | solution.py:499
  31.8 2.1 %shard_map.97 = (f32[400,128]{1,0:T(8,128)}, f32[16,128]{1,0:T(8,128)}) custom-call(f32[32,128]{1,0:T(8,128)S(1)} %get-tuple-element.14.th, f32[2,8,64,128]{3,2,1,0:T(8,128)S(1)} %bitcast.17, f32[32,128]{1,0:T(8,128)S(1)} %slice.19.beyond, f32[2,8,32,128]{3,2,1,0:T(8,128)S(1)} %bitcast.14, f32[104,128]{1,0:T(8,128)S(1)} %slice.17.beyond.beyond1, ...), custom_call_target="tpu_custom_call" | custom-call | tf_op jit(solution)/shard_map/pallas_call | solution.py:569
  (19 shorter events, 0.1 us)
Async XLA Ops:
  2.1 5.0 %collective-permute-start = (f32[32,128]{1,0:T(8,128)S(1)}, f32[32,128]{1,0:T(8,128)S(1)}, u32[]{:S(2)}, u32[]{:S(2)}) collective-permute-start(f32[32,128]{1,0:T(8,128)S(1)} %get-tuple-element.16), channel_id=1, source_target_pairs={{0,9},{1,8},{2,11},{3,10},{4,13},{5,12},{6,15},{7,14},{8,1},{9,0},... | collective-permute-start | bytes 49160 | tf_op jit(solution)/shard_map/ppermute | solution.py:498
  7.1 9.0 %copy-start.2 = (f32[25,16,128]{2,1,0:T(8,128)S(1)}, f32[25,16,128]{2,1,0:T(8,128)}, u32[]{:S(2)}) copy-start(f32[25,16,128]{2,1,0:T(8,128)} %param.8) | copy-start | bytes 614404
  7.1 3.5 %collective-permute-start.1 = (f32[64,128]{1,0:T(8,128)S(1)}, f32[64,128]{1,0:T(8,128)S(1)}, u32[]{:S(2)}, u32[]{:S(2)}) collective-permute-start(f32[64,128]{1,0:T(8,128)S(1)} %pad_maximum_fusion.3), channel_id=1, source_target_pairs={{0,5},{1,2},{2,1},{3,6},{4,7},{5,0},{6,3},{7,4},{8,11},{9,12},{10,... | collective-permute-start | bytes 98312 | tf_op jit(solution)/shard_map/ppermute | solution.py:498
  10.6 5.5 %copy-start.1 = (f32[2,25,16,128]{3,2,1,0:T(8,128)S(1)}, f32[2,25,16,128]{3,2,1,0:T(8,128)}, u32[]{:S(2)}) copy-start(f32[2,25,16,128]{3,2,1,0:T(8,128)} %param.11) | copy-start | bytes 1228804
  10.6 5.5 %copy-start = (f32[2,25,16,128]{3,2,1,0:T(8,128)S(1)}, f32[2,25,16,128]{3,2,1,0:T(8,128)}, u32[]{:S(2)}) copy-start(f32[2,25,16,128]{3,2,1,0:T(8,128)} %param.10) | copy-start | bytes 1228804
  10.6 3.8 %collective-permute-start.2 = (f32[128,128]{1,0:T(8,128)S(1)}, f32[128,128]{1,0:T(8,128)S(1)}, u32[]{:S(2)}, u32[]{:S(2)}) collective-permute-start(f32[128,128]{1,0:T(8,128)S(1)} %pad_maximum_fusion.1), channel_id=1, source_target_pairs={{0,3},{1,4},{2,7},{3,0},{4,1},{5,6},{6,5},{7,2},{8,13},{9,10},{10,... | collective-permute-start | bytes 196616 | tf_op jit(solution)/shard_map/ppermute | solution.py:498
  14.4 1.6 %collective-permute-start.3 = (f32[360,128]{1,0:T(8,128)S(1)}, f32[360,128]{1,0:T(8,128)S(1)}, u32[]{:S(2)}, u32[]{:S(2)}) collective-permute-start(f32[360,128]{1,0:T(8,128)S(1)} %constant_dynamic-update-slice_fusion), channel_id=1, source_target_pairs={{0,1},{1,0},{2,3},{3,2},{4,5},{5,4},{6,7},{7,6},{8,9},{9,8},{10,11... | collective-permute-start | bytes 552968 | tf_op jit(solution)/shard_map/ppermute | solution.py:499
  17.5 4.5 %collective-permute-start.4 = (f32[64,128]{1,0:T(8,128)S(1)}, f32[64,128]{1,0:T(8,128)S(1)}, u32[]{:S(2)}, u32[]{:S(2)}) collective-permute-start(f32[64,128]{1,0:T(8,128)S(1)} %get-tuple-element.19), channel_id=1, source_target_pairs={{0,9},{1,8},{2,11},{3,10},{4,13},{5,12},{6,15},{7,14},{8,1},{9,0},... | collective-permute-start | bytes 98312 | tf_op jit(solution)/shard_map/ppermute | solution.py:498
  22.0 3.7 %collective-permute-start.5 = (f32[128,128]{1,0:T(8,128)S(1)}, f32[128,128]{1,0:T(8,128)S(1)}, u32[]{:S(2)}, u32[]{:S(2)}) collective-permute-start(f32[128,128]{1,0:T(8,128)S(1)} %pad_maximum_fusion.2), channel_id=1, source_target_pairs={{0,5},{1,2},{2,1},{3,6},{4,7},{5,0},{6,3},{7,4},{8,11},{9,12},{10,... | collective-permute-start | bytes 196616 | tf_op jit(solution)/shard_map/ppermute | solution.py:498
  25.7 4.5 %collective-permute-start.6 = (f32[256,128]{1,0:T(8,128)S(1)}, f32[256,128]{1,0:T(8,128)S(1)}, u32[]{:S(2)}, u32[]{:S(2)}) collective-permute-start(f32[256,128]{1,0:T(8,128)S(1)} %pad_maximum_fusion), channel_id=1, source_target_pairs={{0,3},{1,4},{2,7},{3,0},{4,1},{5,6},{6,5},{7,2},{8,13},{9,10},{10,... | collective-permute-start | bytes 393224 | tf_op jit(solution)/shard_map/ppermute | solution.py:498
  30.2 1.6 %collective-permute-start.7 = (f32[544,128]{1,0:T(8,128)S(1)}, f32[544,128]{1,0:T(8,128)S(1)}, u32[]{:S(2)}, u32[]{:S(2)}) collective-permute-start(f32[544,128]{1,0:T(8,128)S(1)} %constant_dynamic-update-slice_fusion.9), channel_id=1, source_target_pairs={{0,1},{1,0},{2,3},{3,2},{4,5},{5,4},{6,7},{7,6},{8,9},{9,8},{10,11... | collective-permute-start | bytes 835592 | tf_op jit(solution)/shard_map/ppermute | solution.py:499

commit v6 on v5

--- a/solution.py
+++ b/solution.py
@@ -23,7 +23,7 @@
 
 def full_sum(x):
     lines = jnp.sum(x.reshape(-1, 8, x.shape[-1]), axis=0)
-    return jnp.sum(jnp.sum(lines, axis=0, keepdims=True), axis=1, keepdims=True)
+    return jnp.sum(jnp.sum(lines, axis=1, keepdims=True), axis=0, keepdims=True)
 
 
 def split_index(column, cols):
@@ -384,11 +384,6 @@
     fold = fold_take(sent.line(0, HROW2, rowbuf), block, lane)
     row3 = iota(forcing.shape, 1)
     forcing = forcing - jnp.where(row3 == 2 * rows - 1, fold[:, None, :], 0.0)
-    iterate = surface_solve(forcing, block, lane)
-    solved[...] = iterate
-    rowbuf[...] = fold_take(iterate[:, 2 * rows - 1, :], block, lane)
-    across_solved = rowbuf[pl.ds(me, 1), :]
-
     spot = iota((1, cols), 1)
     rowbuf[...] = partner.astype(F32)
     beside_left = pltpu.roll(rowbuf[pl.ds(west, 1), :], 1, 1)
@@ -420,6 +415,10 @@
         for c, start in ((0, 0), (1, later)):
             tall[2, 0:WINDOW, :] = parts[c]
             tall[i, start : start + share, :] = tall[2, skip : skip + share, :]
+    iterate = surface_solve(forcing, block, lane)
+    solved[...] = iterate
+    rowbuf[...] = fold_take(iterate[:, 2 * rows - 1, :], block, lane)
+    across_solved = rowbuf[pl.ds(me, 1), :]
     level = iota((TALL, cols), 0).astype(F32)
     fold_last = jnp.where(
         kept[TALL : TALL + 1, :] > level,

time: 34.1 us -> 34 us (level)
  no operation moved by 1% of the time
where the time goes in v6:
time: 34 us; the launch traced here: 33.8 us
  starting transfers between devices  14.4 us (42%)
  waiting for transfers between devices  13.7 us (40%)
  Pallas kernels  4.84 us (14%)
  between operations  0.72 us (2%)
    ppermute x6, starting transfers between devices, exchange(): y = jnp.concatenate([y, lax.ppermute(y, ('ia', 'ja'), pairs)])  13.3 us
    ppermute x6, waiting for transfers between devices, exchange(): y = jnp.concatenate([y, lax.ppermute(y, ('ia', 'ja'), pairs)])  11.5 us
    ppermute x2, waiting for transfers between devices, exchange(): z = lax.ppermute(jnp.concatenate([y, peer]), 'ja', [(0, 1), (1, 0)])  2.24 us
    pallas_call x1, Pallas kernels, on_device(): pl.pallas_call(second_kernel, out_shape=(shape(flat, cols), shape(rows, c...  1.97 us
    pallas_call x1, Pallas kernels, on_device(): pl.pallas_call(pack_kernel, out_shape=(shape(ROWS1, cols), shape(PEER1, c...  1.51 us
    pallas_call x1, Pallas kernels, on_device(): pl.pallas_call(first_kernel, out_shape=(shape(flat, cols), shape(ROWS2, c...  1.37 us
    ppermute x2, starting transfers between devices, exchange(): z = lax.ppermute(jnp.concatenate([y, peer]), 'ja', [(0, 1), (1, 0)])  1.04 us
  transfers between devices with their start and end apart: 8, of which 8 were waited for; matrix products, arithmetic and copies ran while one was open for 0% of the time, Pallas kernels for 0%

profile of v6, /device:TPU:0, one launch (start us, length us, event | category | flops | bytes accessed | tf_op | source)
XLA Modules:
  0.0 33.8 jit_solution(4833509174022064078)
XLA Ops:
  0.6 1.5 %shard_map.95 = (f32[32,128]{1,0:T(8,128)S(1)}, f32[104,128]{1,0:T(8,128)S(1)}, f32[16,128]{1,0:T(8,128)S(1)}, f32[32,128]{1,0:T(8,128)S(1)}, f32[32,128]{1,0:T(8,128)S(1)}) custom-call(f32[25]{0:T(128)} %cp_in.1, f32[25]{0:T(128)} %th_in.1, f32[400,128]{1,0:T(8,128)} %bitcast.15, f32[16,128]{1,0:T(8,128)} %surf_in.1, f32[2,400,128]{2,1,0:T(8,128)} %bitcast.7, ...), custom_call_target="tpu_custom_call" | custom-call | tf_op jit(solution)/shard_map/pallas_call | solution.py:524
  2.1 3.5 %collective-permute-start = (f32[32,128]{1,0:T(8,128)S(1)}, f32[32,128]{1,0:T(8,128)S(1)}, u32[]{:S(2)}, u32[]{:S(2)}) collective-permute-start(f32[32,128]{1,0:T(8,128)S(1)} %get-tuple-element.16), channel_id=1, source_target_pairs={{0,9},{1,8},{2,11},{3,10},{4,13},{5,12},{6,15},{7,14},{8,1},{9,0},... | collective-permute-start | bytes 49160 | tf_op jit(solution)/shard_map/ppermute | solution.py:497
  5.7 1.4 %collective-permute-done = f32[32,128]{1,0:T(8,128)S(1)} collective-permute-done((f32[32,128]{1,0:T(8,128)S(1)}, f32[32,128]{1,0:T(8,128)S(1)}, u32[]{:S(2)}, u32[]{:S(2)}) %collective-permute-start) | collective-permute-done | bytes 16416 | tf_op jit(solution)/shard_map/ppermute | solution.py:497
  7.1 1.9 %collective-permute-start.1 = (f32[64,128]{1,0:T(8,128)S(1)}, f32[64,128]{1,0:T(8,128)S(1)}, u32[]{:S(2)}, u32[]{:S(2)}) collective-permute-start(f32[64,128]{1,0:T(8,128)S(1)} %pad_maximum_fusion.3), channel_id=1, source_target_pairs={{0,5},{1,2},{2,1},{3,6},{4,7},{5,0},{6,3},{7,4},{8,11},{9,12},{10,... | collective-permute-start | bytes 98312 | tf_op jit(solution)/shard_map/ppermute | solution.py:497
  9.0 1.6 %collective-permute-done.1 = f32[64,128]{1,0:T(8,128)S(1)} collective-permute-done((f32[64,128]{1,0:T(8,128)S(1)}, f32[64,128]{1,0:T(8,128)S(1)}, u32[]{:S(2)}, u32[]{:S(2)}) %collective-permute-start.1) | collective-permute-done | bytes 32800 | tf_op jit(solution)/shard_map/ppermute | solution.py:497
  10.6 0.0 copy-start.1
  10.6 0.0 copy-start
  10.6 1.7 %collective-permute-start.2 = (f32[128,128]{1,0:T(8,128)S(1)}, f32[128,128]{1,0:T(8,128)S(1)}, u32[]{:S(2)}, u32[]{:S(2)}) collective-permute-start(f32[128,128]{1,0:T(8,128)S(1)} %pad_maximum_fusion.1), channel_id=1, source_target_pairs={{0,3},{1,4},{2,7},{3,0},{4,1},{5,6},{6,5},{7,2},{8,13},{9,10},{10,... | collective-permute-start | bytes 196616 | tf_op jit(solution)/shard_map/ppermute | solution.py:497
  12.4 2.0 %collective-permute-done.2 = f32[128,128]{1,0:T(8,128)S(1)} collective-permute-done((f32[128,128]{1,0:T(8,128)S(1)}, f32[128,128]{1,0:T(8,128)S(1)}, u32[]{:S(2)}, u32[]{:S(2)}) %collective-permute-start.2) | collective-permute-done | bytes 65568 | tf_op jit(solution)/shard_map/ppermute | solution.py:497
  14.4 0.6 %collective-permute-start.3 = (f32[360,128]{1,0:T(8,128)S(1)}, f32[360,128]{1,0:T(8,128)S(1)}, u32[]{:S(2)}, u32[]{:S(2)}) collective-permute-start(f32[360,128]{1,0:T(8,128)S(1)} %constant_dynamic-update-slice_fusion), channel_id=1, source_target_pairs={{0,1},{1,0},{2,3},{3,2},{4,5},{5,4},{6,7},{7,6},{8,9},{9,8},{10,11... | collective-permute-start | bytes 552968 | tf_op jit(solution)/shard_map/ppermute | solution.py:498
  15.0 1.1 %collective-permute-done.3 = f32[360,128]{1,0:T(8,128)S(1)} collective-permute-done((f32[360,128]{1,0:T(8,128)S(1)}, f32[360,128]{1,0:T(8,128)S(1)}, u32[]{:S(2)}, u32[]{:S(2)}) %collective-permute-start.3) | collective-permute-done | bytes 184352 | tf_op jit(solution)/shard_map/ppermute | solution.py:498
  16.1 0.0 copy-done.2
  16.1 0.0 copy-done.1
  16.1 0.0 copy-done
  16.1 1.4 %shard_map.96 = (f32[400,128]{1,0:T(8,128)S(1)}, f32[64,128]{1,0:T(8,128)S(1)}, f32[32,128]{1,0:T(8,128)S(1)}, f32[40,128]{1,0:T(8,128)S(1)}, s32[8,128]{1,0:T(8,128)S(1)}) custom-call(f32[32,128]{1,0:T(8,128)S(1)} %get-tuple-element.15.cp, f32[32,128]{1,0:T(8,128)S(1)} %get-tuple-element.14.th, f32[2,8,32,128]{3,2,1,0:T(8,128)S(1)} %bitcast.13, ...), custom_call_target="tpu_custom_call" | custom-call | tf_op jit(solution)/shard_map/pallas_call | solution.py:549
  17.5 2.9 %collective-permute-start.4 = (f32[64,128]{1,0:T(8,128)S(1)}, f32[64,128]{1,0:T(8,128)S(1)}, u32[]{:S(2)}, u32[]{:S(2)}) collective-permute-start(f32[64,128]{1,0:T(8,128)S(1)} %get-tuple-element.19), channel_id=1, source_target_pairs={{0,9},{1,8},{2,11},{3,10},{4,13},{5,12},{6,15},{7,14},{8,1},{9,0},... | collective-permute-start | bytes 98312 | tf_op jit(solution)/shard_map/ppermute | solution.py:497
  20.4 1.6 %collective-permute-done.4 = f32[64,128]{1,0:T(8,128)S(1)} collective-permute-done((f32[64,128]{1,0:T(8,128)S(1)}, f32[64,128]{1,0:T(8,128)S(1)}, u32[]{:S(2)}, u32[]{:S(2)}) %collective-permute-start.4) | collective-permute-done | bytes 32800 | tf_op jit(solution)/shard_map/ppermute | solution.py:497
  22.0 1.7 %collective-permute-start.5 = (f32[128,128]{1,0:T(8,128)S(1)}, f32[128,128]{1,0:T(8,128)S(1)}, u32[]{:S(2)}, u32[]{:S(2)}) collective-permute-start(f32[128,128]{1,0:T(8,128)S(1)} %pad_maximum_fusion.2), channel_id=1, source_target_pairs={{0,5},{1,2},{2,1},{3,6},{4,7},{5,0},{6,3},{7,4},{8,11},{9,12},{10,... | collective-permute-start | bytes 196616 | tf_op jit(solution)/shard_map/ppermute | solution.py:497
  23.7 1.9 %collective-permute-done.5 = f32[128,128]{1,0:T(8,128)S(1)} collective-permute-done((f32[128,128]{1,0:T(8,128)S(1)}, f32[128,128]{1,0:T(8,128)S(1)}, u32[]{:S(2)}, u32[]{:S(2)}) %collective-permute-start.5) | collective-permute-done | bytes 65568 | tf_op jit(solution)/shard_map/ppermute | solution.py:497
  25.7 1.6 %collective-permute-start.6 = (f32[256,128]{1,0:T(8,128)S(1)}, f32[256,128]{1,0:T(8,128)S(1)}, u32[]{:S(2)}, u32[]{:S(2)}) collective-permute-start(f32[256,128]{1,0:T(8,128)S(1)} %pad_maximum_fusion), channel_id=1, source_target_pairs={{0,3},{1,4},{2,7},{3,0},{4,1},{5,6},{6,5},{7,2},{8,13},{9,10},{10,... | collective-permute-start | bytes 393224 | tf_op jit(solution)/shard_map/ppermute | solution.py:497
  27.2 2.9 %collective-permute-done.6 = f32[256,128]{1,0:T(8,128)S(1)} collective-permute-done((f32[256,128]{1,0:T(8,128)S(1)}, f32[256,128]{1,0:T(8,128)S(1)}, u32[]{:S(2)}, u32[]{:S(2)}) %collective-permute-start.6) | collective-permute-done | bytes 131104 | tf_op jit(solution)/shard_map/ppermute | solution.py:497
  30.2 0.5 %collective-permute-start.7 = (f32[544,128]{1,0:T(8,128)S(1)}, f32[544,128]{1,0:T(8,128)S(1)}, u32[]{:S(2)}, u32[]{:S(2)}) collective-permute-start(f32[544,128]{1,0:T(8,128)S(1)} %constant_dynamic-update-slice_fusion.9), channel_id=1, source_target_pairs={{0,1},{1,0},{2,3},{3,2},{4,5},{5,4},{6,7},{7,6},{8,9},{9,8},{10,11... | collective-permute-start | bytes 835592 | tf_op jit(solution)/shard_map/ppermute | solution.py:498
  30.6 1.2 %collective-permute-done.7 = f32[544,128]{1,0:T(8,128)S(1)} collective-permute-done((f32[544,128]{1,0:T(8,128)S(1)}, f32[544,128]{1,0:T(8,128)S(1)}, u32[]{:S(2)}, u32[]{:S(2)}) %collective-permute-start.7) | collective-permute-done | bytes 278560 | tf_op jit(solution)/shard_map/ppermute | solution.py:498
  31.8 2.0 %shard_map.97 = (f32[400,128]{1,0:T(8,128)}, f32[16,128]{1,0:T(8,128)}) custom-call(f32[32,128]{1,0:T(8,128)S(1)} %get-tuple-element.14.th, f32[2,8,64,128]{3,2,1,0:T(8,128)S(1)} %bitcast.17, f32[32,128]{1,0:T(8,128)S(1)} %slice.19.beyond, f32[2,8,32,128]{3,2,1,0:T(8,128)S(1)} %bitcast.14, f32[104,128]{1,0:T(8,128)S(1)} %slice.17.beyond.beyond1, ...), custom_call_target="tpu_custom_call" | custom-call | tf_op jit(solution)/shard_map/pallas_call | solution.py:568
  (19 shorter events, 0.1 us)
Async XLA Ops:
  2.1 5.0 %collective-permute-start = (f32[32,128]{1,0:T(8,128)S(1)}, f32[32,128]{1,0:T(8,128)S(1)}, u32[]{:S(2)}, u32[]{:S(2)}) collective-permute-start(f32[32,128]{1,0:T(8,128)S(1)} %get-tuple-element.16), channel_id=1, source_target_pairs={{0,9},{1,8},{2,11},{3,10},{4,13},{5,12},{6,15},{7,14},{8,1},{9,0},... | collective-permute-start | bytes 49160 | tf_op jit(solution)/shard_map/ppermute | solution.py:497
  7.1 9.0 %copy-start.2 = (f32[25,16,128]{2,1,0:T(8,128)S(1)}, f32[25,16,128]{2,1,0:T(8,128)}, u32[]{:S(2)}) copy-start(f32[25,16,128]{2,1,0:T(8,128)} %param.8) | copy-start | bytes 614404
  7.1 3.5 %collective-permute-start.1 = (f32[64,128]{1,0:T(8,128)S(1)}, f32[64,128]{1,0:T(8,128)S(1)}, u32[]{:S(2)}, u32[]{:S(2)}) collective-permute-start(f32[64,128]{1,0:T(8,128)S(1)} %pad_maximum_fusion.3), channel_id=1, source_target_pairs={{0,5},{1,2},{2,1},{3,6},{4,7},{5,0},{6,3},{7,4},{8,11},{9,12},{10,... | collective-permute-start | bytes 98312 | tf_op jit(solution)/shard_map/ppermute | solution.py:497
  10.6 5.5 %copy-start.1 = (f32[2,25,16,128]{3,2,1,0:T(8,128)S(1)}, f32[2,25,16,128]{3,2,1,0:T(8,128)}, u32[]{:S(2)}) copy-start(f32[2,25,16,128]{3,2,1,0:T(8,128)} %param.11) | copy-start | bytes 1228804
  10.6 5.5 %copy-start = (f32[2,25,16,128]{3,2,1,0:T(8,128)S(1)}, f32[2,25,16,128]{3,2,1,0:T(8,128)}, u32[]{:S(2)}) copy-start(f32[2,25,16,128]{3,2,1,0:T(8,128)} %param.10) | copy-start | bytes 1228804
  10.6 3.8 %collective-permute-start.2 = (f32[128,128]{1,0:T(8,128)S(1)}, f32[128,128]{1,0:T(8,128)S(1)}, u32[]{:S(2)}, u32[]{:S(2)}) collective-permute-start(f32[128,128]{1,0:T(8,128)S(1)} %pad_maximum_fusion.1), channel_id=1, source_target_pairs={{0,3},{1,4},{2,7},{3,0},{4,1},{5,6},{6,5},{7,2},{8,13},{9,10},{10,... | collective-permute-start | bytes 196616 | tf_op jit(solution)/shard_map/ppermute | solution.py:497
  14.4 1.6 %collective-permute-start.3 = (f32[360,128]{1,0:T(8,128)S(1)}, f32[360,128]{1,0:T(8,128)S(1)}, u32[]{:S(2)}, u32[]{:S(2)}) collective-permute-start(f32[360,128]{1,0:T(8,128)S(1)} %constant_dynamic-update-slice_fusion), channel_id=1, source_target_pairs={{0,1},{1,0},{2,3},{3,2},{4,5},{5,4},{6,7},{7,6},{8,9},{9,8},{10,11... | collective-permute-start | bytes 552968 | tf_op jit(solution)/shard_map/ppermute | solution.py:498
  17.5 4.5 %collective-permute-start.4 = (f32[64,128]{1,0:T(8,128)S(1)}, f32[64,128]{1,0:T(8,128)S(1)}, u32[]{:S(2)}, u32[]{:S(2)}) collective-permute-start(f32[64,128]{1,0:T(8,128)S(1)} %get-tuple-element.19), channel_id=1, source_target_pairs={{0,9},{1,8},{2,11},{3,10},{4,13},{5,12},{6,15},{7,14},{8,1},{9,0},... | collective-permute-start | bytes 98312 | tf_op jit(solution)/shard_map/ppermute | solution.py:497
  22.0 3.7 %collective-permute-start.5 = (f32[128,128]{1,0:T(8,128)S(1)}, f32[128,128]{1,0:T(8,128)S(1)}, u32[]{:S(2)}, u32[]{:S(2)}) collective-permute-start(f32[128,128]{1,0:T(8,128)S(1)} %pad_maximum_fusion.2), channel_id=1, source_target_pairs={{0,5},{1,2},{2,1},{3,6},{4,7},{5,0},{6,3},{7,4},{8,11},{9,12},{10,... | collective-permute-start | bytes 196616 | tf_op jit(solution)/shard_map/ppermute | solution.py:497
  25.7 4.5 %collective-permute-start.6 = (f32[256,128]{1,0:T(8,128)S(1)}, f32[256,128]{1,0:T(8,128)S(1)}, u32[]{:S(2)}, u32[]{:S(2)}) collective-permute-start(f32[256,128]{1,0:T(8,128)S(1)} %pad_maximum_fusion), channel_id=1, source_target_pairs={{0,3},{1,4},{2,7},{3,0},{4,1},{5,6},{6,5},{7,2},{8,13},{9,10},{10,... | collective-permute-start | bytes 393224 | tf_op jit(solution)/shard_map/ppermute | solution.py:497
  30.2 1.6 %collective-permute-start.7 = (f32[544,128]{1,0:T(8,128)S(1)}, f32[544,128]{1,0:T(8,128)S(1)}, u32[]{:S(2)}, u32[]{:S(2)}) collective-permute-start(f32[544,128]{1,0:T(8,128)S(1)} %constant_dynamic-update-slice_fusion.9), channel_id=1, source_target_pairs={{0,1},{1,0},{2,3},{3,2},{4,5},{5,4},{6,7},{7,6},{8,9},{9,8},{10,11... | collective-permute-start | bytes 835592 | tf_op jit(solution)/shard_map/ppermute | solution.py:498

commit v7 on v6

--- a/solution.py
+++ b/solution.py
@@ -287,7 +287,6 @@
     partner = code >> (DEPTHS.bit_length() - 1)
     table[...] = partner
     block, lane = split_index(partner, cols)
-    solved[...] = surface_solve(sent.field(rows), block, lane)
     depths = (code & (DEPTHS - 1)).astype(F32)
     rowbuf[...] = depths
     fold_depth = rowbuf[pl.ds(me, 1), :]
@@ -302,6 +301,7 @@
     tall[1, 0:count, :] = jnp.where(
         is_top, level_rows(adj, rows - 1, count, rows), beyond[3 * count : 4 * count, :]
     )
+    solved[...] = surface_solve(sent.field(rows), block, lane)
     fold_solved = solved[me, 2 * rows - 8 :, :][7:]
     flux = jnp.where(
         fold_depth > level,
@@ -415,6 +415,18 @@
         for c, start in ((0, 0), (1, later)):
             tall[2, 0:WINDOW, :] = parts[c]
             tall[i, start : start + share, :] = tall[2, skip : skip + share, :]
+    depth = depth_in[...]
+    edge1_left = sent1.beside(west, EDGE1, EDGE1 + rows)
+    edge1_right = sent1.beside(east, EDGE1, EDGE1 + rows)
+    half = rows // 2
+
+    def both_rows(line):
+        return jnp.concatenate([line, pltpu.roll(line, cols // 2, 1)], axis=0)
+
+    edge_left = both_rows(sent.beside(west, EDGE2, EDGE2 + half))
+    edge_right = both_rows(sent.beside(east, EDGE2, EDGE2 + half))
+    beside_depth = beyond1[4 * count : 4 * count + 1, :]
+    masks = face_depths(depth, edge1_left, edge1_right, beside_depth, count, top)
     iterate = surface_solve(forcing, block, lane)
     solved[...] = iterate
     rowbuf[...] = fold_take(iterate[:, 2 * rows - 1, :], block, lane)
@@ -429,18 +441,6 @@
     )
     tall[2] = fold_last
 
-    depth = depth_in[...]
-    edge1_left = sent1.beside(west, EDGE1, EDGE1 + rows)
-    edge1_right = sent1.beside(east, EDGE1, EDGE1 + rows)
-    half = rows // 2
-
-    def both_rows(line):
-        return jnp.concatenate([line, pltpu.roll(line, cols // 2, 1)], axis=0)
-
-    edge_left = both_rows(sent.beside(west, EDGE2, EDGE2 + half))
-    edge_right = both_rows(sent.beside(east, EDGE2, EDGE2 + half))
-    beside_depth = beyond1[4 * count : 4 * count + 1, :]
-    masks = face_depths(depth, edge1_left, edge1_right, beside_depth, count, top)
     own, left, right, beside = load_pieces(solved, me, west, east, rows, top)
     s_out[...] = own
     pieces = (

time: 34 us -> 33.9 us (level)
  no operation moved by 1% of the time
where the time goes in v7:
time: 33.9 us; the launch traced here: 33.8 us
  starting transfers between devices  14.4 us (42%)
  waiting for transfers between devices  13.7 us (40%)
  Pallas kernels  4.79 us (14%)
  between operations  0.72 us (2%)
    ppermute x6, starting transfers between devices, exchange(): y = jnp.concatenate([y, lax.ppermute(y, ('ia', 'ja'), pairs)])  13.3 us
    ppermute x6, waiting for transfers between devices, exchange(): y = jnp.concatenate([y, lax.ppermute(y, ('ia', 'ja'), pairs)])  11.5 us
    ppermute x2, waiting for transfers between devices, exchange(): z = lax.ppermute(jnp.concatenate([y, peer]), 'ja', [(0, 1), (1, 0)])  2.24 us
    pallas_call x1, Pallas kernels, on_device(): pl.pallas_call(second_kernel, out_shape=(shape(flat, cols), shape(rows, c...  1.98 us
    pallas_call x1, Pallas kernels, on_device(): pl.pallas_call(pack_kernel, out_shape=(shape(ROWS1, cols), shape(PEER1, c...  1.51 us
    pallas_call x1, Pallas kernels, on_device(): pl.pallas_call(first_kernel, out_shape=(shape(flat, cols), shape(ROWS2, c...  1.31 us
    ppermute x2, starting transfers between devices, exchange(): z = lax.ppermute(jnp.concatenate([y, peer]), 'ja', [(0, 1), (1, 0)])  1.04 us
  transfers between devices with their start and end apart: 8, of which 8 were waited for; matrix products, arithmetic and copies ran while one was open for 0% of the time, Pallas kernels for 0%

profile of v7, /device:TPU:0, one launch (start us, length us, event | category | flops | bytes accessed | tf_op | source)
XLA Modules:
  0.0 33.8 jit_solution(1677473383852524607)
XLA Ops:
  0.6 1.5 %shard_map.95 = (f32[32,128]{1,0:T(8,128)S(1)}, f32[104,128]{1,0:T(8,128)S(1)}, f32[16,128]{1,0:T(8,128)S(1)}, f32[32,128]{1,0:T(8,128)S(1)}, f32[32,128]{1,0:T(8,128)S(1)}) custom-call(f32[25]{0:T(128)} %cp_in.1, f32[25]{0:T(128)} %th_in.1, f32[400,128]{1,0:T(8,128)} %bitcast.15, f32[16,128]{1,0:T(8,128)} %surf_in.1, f32[2,400,128]{2,1,0:T(8,128)} %bitcast.7, ...), custom_call_target="tpu_custom_call" | custom-call | tf_op jit(solution)/shard_map/pallas_call | solution.py:524
  2.1 3.5 %collective-permute-start = (f32[32,128]{1,0:T(8,128)S(1)}, f32[32,128]{1,0:T(8,128)S(1)}, u32[]{:S(2)}, u32[]{:S(2)}) collective-permute-start(f32[32,128]{1,0:T(8,128)S(1)} %get-tuple-element.16), channel_id=1, source_target_pairs={{0,9},{1,8},{2,11},{3,10},{4,13},{5,12},{6,15},{7,14},{8,1},{9,0},... | collective-permute-start | bytes 49160 | tf_op jit(solution)/shard_map/ppermute | solution.py:497
  5.7 1.4 %collective-permute-done = f32[32,128]{1,0:T(8,128)S(1)} collective-permute-done((f32[32,128]{1,0:T(8,128)S(1)}, f32[32,128]{1,0:T(8,128)S(1)}, u32[]{:S(2)}, u32[]{:S(2)}) %collective-permute-start) | collective-permute-done | bytes 16416 | tf_op jit(solution)/shard_map/ppermute | solution.py:497
  7.1 1.9 %collective-permute-start.1 = (f32[64,128]{1,0:T(8,128)S(1)}, f32[64,128]{1,0:T(8,128)S(1)}, u32[]{:S(2)}, u32[]{:S(2)}) collective-permute-start(f32[64,128]{1,0:T(8,128)S(1)} %pad_maximum_fusion.3), channel_id=1, source_target_pairs={{0,5},{1,2},{2,1},{3,6},{4,7},{5,0},{6,3},{7,4},{8,11},{9,12},{10,... | collective-permute-start | bytes 98312 | tf_op jit(solution)/shard_map/ppermute | solution.py:497
  9.0 1.6 %collective-permute-done.1 = f32[64,128]{1,0:T(8,128)S(1)} collective-permute-done((f32[64,128]{1,0:T(8,128)S(1)}, f32[64,128]{1,0:T(8,128)S(1)}, u32[]{:S(2)}, u32[]{:S(2)}) %collective-permute-start.1) | collective-permute-done | bytes 32800 | tf_op jit(solution)/shard_map/ppermute | solution.py:497
  10.6 0.0 copy-start.1
  10.6 0.0 copy-start
  10.6 1.7 %collective-permute-start.2 = (f32[128,128]{1,0:T(8,128)S(1)}, f32[128,128]{1,0:T(8,128)S(1)}, u32[]{:S(2)}, u32[]{:S(2)}) collective-permute-start(f32[128,128]{1,0:T(8,128)S(1)} %pad_maximum_fusion.1), channel_id=1, source_target_pairs={{0,3},{1,4},{2,7},{3,0},{4,1},{5,6},{6,5},{7,2},{8,13},{9,10},{10,... | collective-permute-start | bytes 196616 | tf_op jit(solution)/shard_map/ppermute | solution.py:497
  12.4 2.0 %collective-permute-done.2 = f32[128,128]{1,0:T(8,128)S(1)} collective-permute-done((f32[128,128]{1,0:T(8,128)S(1)}, f32[128,128]{1,0:T(8,128)S(1)}, u32[]{:S(2)}, u32[]{:S(2)}) %collective-permute-start.2) | collective-permute-done | bytes 65568 | tf_op jit(solution)/shard_map/ppermute | solution.py:497
  14.4 0.6 %collective-permute-start.3 = (f32[360,128]{1,0:T(8,128)S(1)}, f32[360,128]{1,0:T(8,128)S(1)}, u32[]{:S(2)}, u32[]{:S(2)}) collective-permute-start(f32[360,128]{1,0:T(8,128)S(1)} %constant_dynamic-update-slice_fusion), channel_id=1, source_target_pairs={{0,1},{1,0},{2,3},{3,2},{4,5},{5,4},{6,7},{7,6},{8,9},{9,8},{10,11... | collective-permute-start | bytes 552968 | tf_op jit(solution)/shard_map/ppermute | solution.py:498
  15.0 1.1 %collective-permute-done.3 = f32[360,128]{1,0:T(8,128)S(1)} collective-permute-done((f32[360,128]{1,0:T(8,128)S(1)}, f32[360,128]{1,0:T(8,128)S(1)}, u32[]{:S(2)}, u32[]{:S(2)}) %collective-permute-start.3) | collective-permute-done | bytes 184352 | tf_op jit(solution)/shard_map/ppermute | solution.py:498
  16.1 0.0 copy-done.2
  16.1 0.0 copy-done.1
  16.1 0.0 copy-done
  16.1 1.3 %shard_map.96 = (f32[400,128]{1,0:T(8,128)S(1)}, f32[64,128]{1,0:T(8,128)S(1)}, f32[32,128]{1,0:T(8,128)S(1)}, f32[40,128]{1,0:T(8,128)S(1)}, s32[8,128]{1,0:T(8,128)S(1)}) custom-call(f32[32,128]{1,0:T(8,128)S(1)} %get-tuple-element.15.cp, f32[32,128]{1,0:T(8,128)S(1)} %get-tuple-element.14.th, f32[2,8,32,128]{3,2,1,0:T(8,128)S(1)} %bitcast.13, ...), custom_call_target="tpu_custom_call" | custom-call | tf_op jit(solution)/shard_map/pallas_call | solution.py:549
  17.4 2.9 %collective-permute-start.4 = (f32[64,128]{1,0:T(8,128)S(1)}, f32[64,128]{1,0:T(8,128)S(1)}, u32[]{:S(2)}, u32[]{:S(2)}) collective-permute-start(f32[64,128]{1,0:T(8,128)S(1)} %get-tuple-element.19), channel_id=1, source_target_pairs={{0,9},{1,8},{2,11},{3,10},{4,13},{5,12},{6,15},{7,14},{8,1},{9,0},... | collective-permute-start | bytes 98312 | tf_op jit(solution)/shard_map/ppermute | solution.py:497
  20.3 1.6 %collective-permute-done.4 = f32[64,128]{1,0:T(8,128)S(1)} collective-permute-done((f32[64,128]{1,0:T(8,128)S(1)}, f32[64,128]{1,0:T(8,128)S(1)}, u32[]{:S(2)}, u32[]{:S(2)}) %collective-permute-start.4) | collective-permute-done | bytes 32800 | tf_op jit(solution)/shard_map/ppermute | solution.py:497
  21.9 1.7 %collective-permute-start.5 = (f32[128,128]{1,0:T(8,128)S(1)}, f32[128,128]{1,0:T(8,128)S(1)}, u32[]{:S(2)}, u32[]{:S(2)}) collective-permute-start(f32[128,128]{1,0:T(8,128)S(1)} %pad_maximum_fusion.2), channel_id=1, source_target_pairs={{0,5},{1,2},{2,1},{3,6},{4,7},{5,0},{6,3},{7,4},{8,11},{9,12},{10,... | collective-permute-start | bytes 196616 | tf_op jit(solution)/shard_map/ppermute | solution.py:497
  23.7 1.9 %collective-permute-done.5 = f32[128,128]{1,0:T(8,128)S(1)} collective-permute-done((f32[128,128]{1,0:T(8,128)S(1)}, f32[128,128]{1,0:T(8,128)S(1)}, u32[]{:S(2)}, u32[]{:S(2)}) %collective-permute-start.5) | collective-permute-done | bytes 65568 | tf_op jit(solution)/shard_map/ppermute | solution.py:497
  25.6 1.6 %collective-permute-start.6 = (f32[256,128]{1,0:T(8,128)S(1)}, f32[256,128]{1,0:T(8,128)S(1)}, u32[]{:S(2)}, u32[]{:S(2)}) collective-permute-start(f32[256,128]{1,0:T(8,128)S(1)} %pad_maximum_fusion), channel_id=1, source_target_pairs={{0,3},{1,4},{2,7},{3,0},{4,1},{5,6},{6,5},{7,2},{8,13},{9,10},{10,... | collective-permute-start | bytes 393224 | tf_op jit(solution)/shard_map/ppermute | solution.py:497
  27.2 2.9 %collective-permute-done.6 = f32[256,128]{1,0:T(8,128)S(1)} collective-permute-done((f32[256,128]{1,0:T(8,128)S(1)}, f32[256,128]{1,0:T(8,128)S(1)}, u32[]{:S(2)}, u32[]{:S(2)}) %collective-permute-start.6) | collective-permute-done | bytes 131104 | tf_op jit(solution)/shard_map/ppermute | solution.py:497
  30.1 0.5 %collective-permute-start.7 = (f32[544,128]{1,0:T(8,128)S(1)}, f32[544,128]{1,0:T(8,128)S(1)}, u32[]{:S(2)}, u32[]{:S(2)}) collective-permute-start(f32[544,128]{1,0:T(8,128)S(1)} %constant_dynamic-update-slice_fusion.9), channel_id=1, source_target_pairs={{0,1},{1,0},{2,3},{3,2},{4,5},{5,4},{6,7},{7,6},{8,9},{9,8},{10,11... | collective-permute-start | bytes 835592 | tf_op jit(solution)/shard_map/ppermute | solution.py:498
  30.6 1.2 %collective-permute-done.7 = f32[544,128]{1,0:T(8,128)S(1)} collective-permute-done((f32[544,128]{1,0:T(8,128)S(1)}, f32[544,128]{1,0:T(8,128)S(1)}, u32[]{:S(2)}, u32[]{:S(2)}) %collective-permute-start.7) | collective-permute-done | bytes 278560 | tf_op jit(solution)/shard_map/ppermute | solution.py:498
  31.8 2.0 %shard_map.97 = (f32[400,128]{1,0:T(8,128)}, f32[16,128]{1,0:T(8,128)}) custom-call(f32[32,128]{1,0:T(8,128)S(1)} %get-tuple-element.14.th, f32[2,8,64,128]{3,2,1,0:T(8,128)S(1)} %bitcast.17, f32[32,128]{1,0:T(8,128)S(1)} %slice.19.beyond, f32[2,8,32,128]{3,2,1,0:T(8,128)S(1)} %bitcast.14, f32[104,128]{1,0:T(8,128)S(1)} %slice.17.beyond.beyond1, ...), custom_call_target="tpu_custom_call" | custom-call | tf_op jit(solution)/shard_map/pallas_call | solution.py:568
  (19 shorter events, 0.1 us)
Async XLA Ops:
  2.1 5.0 %collective-permute-start = (f32[32,128]{1,0:T(8,128)S(1)}, f32[32,128]{1,0:T(8,128)S(1)}, u32[]{:S(2)}, u32[]{:S(2)}) collective-permute-start(f32[32,128]{1,0:T(8,128)S(1)} %get-tuple-element.16), channel_id=1, source_target_pairs={{0,9},{1,8},{2,11},{3,10},{4,13},{5,12},{6,15},{7,14},{8,1},{9,0},... | collective-permute-start | bytes 49160 | tf_op jit(solution)/shard_map/ppermute | solution.py:497
  7.1 9.0 %copy-start.2 = (f32[25,16,128]{2,1,0:T(8,128)S(1)}, f32[25,16,128]{2,1,0:T(8,128)}, u32[]{:S(2)}) copy-start(f32[25,16,128]{2,1,0:T(8,128)} %param.8) | copy-start | bytes 614404
  7.1 3.5 %collective-permute-start.1 = (f32[64,128]{1,0:T(8,128)S(1)}, f32[64,128]{1,0:T(8,128)S(1)}, u32[]{:S(2)}, u32[]{:S(2)}) collective-permute-start(f32[64,128]{1,0:T(8,128)S(1)} %pad_maximum_fusion.3), channel_id=1, source_target_pairs={{0,5},{1,2},{2,1},{3,6},{4,7},{5,0},{6,3},{7,4},{8,11},{9,12},{10,... | collective-permute-start | bytes 98312 | tf_op jit(solution)/shard_map/ppermute | solution.py:497
  10.6 5.5 %copy-start.1 = (f32[2,25,16,128]{3,2,1,0:T(8,128)S(1)}, f32[2,25,16,128]{3,2,1,0:T(8,128)}, u32[]{:S(2)}) copy-start(f32[2,25,16,128]{3,2,1,0:T(8,128)} %param.11) | copy-start | bytes 1228804
  10.6 5.5 %copy-start = (f32[2,25,16,128]{3,2,1,0:T(8,128)S(1)}, f32[2,25,16,128]{3,2,1,0:T(8,128)}, u32[]{:S(2)}) copy-start(f32[2,25,16,128]{3,2,1,0:T(8,128)} %param.10) | copy-start | bytes 1228804
  10.6 3.8 %collective-permute-start.2 = (f32[128,128]{1,0:T(8,128)S(1)}, f32[128,128]{1,0:T(8,128)S(1)}, u32[]{:S(2)}, u32[]{:S(2)}) collective-permute-start(f32[128,128]{1,0:T(8,128)S(1)} %pad_maximum_fusion.1), channel_id=1, source_target_pairs={{0,3},{1,4},{2,7},{3,0},{4,1},{5,6},{6,5},{7,2},{8,13},{9,10},{10,... | collective-permute-start | bytes 196616 | tf_op jit(solution)/shard_map/ppermute | solution.py:497
  14.4 1.6 %collective-permute-start.3 = (f32[360,128]{1,0:T(8,128)S(1)}, f32[360,128]{1,0:T(8,128)S(1)}, u32[]{:S(2)}, u32[]{:S(2)}) collective-permute-start(f32[360,128]{1,0:T(8,128)S(1)} %constant_dynamic-update-slice_fusion), channel_id=1, source_target_pairs={{0,1},{1,0},{2,3},{3,2},{4,5},{5,4},{6,7},{7,6},{8,9},{9,8},{10,11... | collective-permute-start | bytes 552968 | tf_op jit(solution)/shard_map/ppermute | solution.py:498
  17.4 4.5 %collective-permute-start.4 = (f32[64,128]{1,0:T(8,128)S(1)}, f32[64,128]{1,0:T(8,128)S(1)}, u32[]{:S(2)}, u32[]{:S(2)}) collective-permute-start(f32[64,128]{1,0:T(8,128)S(1)} %get-tuple-element.19), channel_id=1, source_target_pairs={{0,9},{1,8},{2,11},{3,10},{4,13},{5,12},{6,15},{7,14},{8,1},{9,0},... | collective-permute-start | bytes 98312 | tf_op jit(solution)/shard_map/ppermute | solution.py:497
  21.9 3.7 %collective-permute-start.5 = (f32[128,128]{1,0:T(8,128)S(1)}, f32[128,128]{1,0:T(8,128)S(1)}, u32[]{:S(2)}, u32[]{:S(2)}) collective-permute-start(f32[128,128]{1,0:T(8,128)S(1)} %pad_maximum_fusion.2), channel_id=1, source_target_pairs={{0,5},{1,2},{2,1},{3,6},{4,7},{5,0},{6,3},{7,4},{8,11},{9,12},{10,... | collective-permute-start | bytes 196616 | tf_op jit(solution)/shard_map/ppermute | solution.py:497
  25.6 4.5 %collective-permute-start.6 = (f32[256,128]{1,0:T(8,128)S(1)}, f32[256,128]{1,0:T(8,128)S(1)}, u32[]{:S(2)}, u32[]{:S(2)}) collective-permute-start(f32[256,128]{1,0:T(8,128)S(1)} %pad_maximum_fusion), channel_id=1, source_target_pairs={{0,3},{1,4},{2,7},{3,0},{4,1},{5,6},{6,5},{7,2},{8,13},{9,10},{10,... | collective-permute-start | bytes 393224 | tf_op jit(solution)/shard_map/ppermute | solution.py:497
  30.1 1.6 %collective-permute-start.7 = (f32[544,128]{1,0:T(8,128)S(1)}, f32[544,128]{1,0:T(8,128)S(1)}, u32[]{:S(2)}, u32[]{:S(2)}) collective-permute-start(f32[544,128]{1,0:T(8,128)S(1)} %constant_dynamic-update-slice_fusion.9), channel_id=1, source_target_pairs={{0,1},{1,0},{2,3},{3,2},{4,5},{5,4},{6,7},{7,6},{8,9},{9,8},{10,11... | collective-permute-start | bytes 835592 | tf_op jit(solution)/shard_map/ppermute | solution.py:498
